TPU v7x, 32 devices: a whole 2x2x4 slice. The times are simulated.
32 devices in a mesh: label: 16 (over z, y, x), fsdp: 2 (over core).
Axes of the slice: x: 2, y: 2, z: 4, core: 2. Of those that a mesh axis runs over, the one named last changes fastest.
Arguments:
- final_hidden: bfloat16 [16, 32, 3584], P('label', 'fsdp'), may hold values from -6 to 6
- norm_gain: float32 [3584], replicated, may hold values from 0.5 to 1.5
- label_weights: bfloat16 [16, 128, 3584], P('label'), may hold values from -0.09375 to 0.09375
- active_blocks: int32 [16, 16, 8], P('label', 'fsdp'), may hold values from 0 to 15, all different within a row; in each aligned block of 8 rows (0 to 7, 8 to 15, ..., all dimensions but the last counted through in order) at most 6 rows name the same one
- positives: int32 [16, 32, 8], P('label', 'fsdp'), may hold values from 0 to 1023
- gate_pre: bfloat16 [16, 32, 18944], P(None, 'fsdp', 'label'), may hold values from -6 to 6
- up_pre: bfloat16 [16, 32, 18944], P(None, 'fsdp', 'label'), may hold values from -6 to 6
- down_weight: bfloat16 [3584, 18944], P('fsdp', 'label'), may hold values from -0.046875 to 0.046875
Outputs:
- resid_grad: bfloat16 [16, 32, 3584], P('label', 'fsdp')
- down_grad: float32 [3584, 18944], P('fsdp', 'label')
- gate_grad: bfloat16 [16, 32, 18944], P(None, 'fsdp', 'label')
- up_grad: bfloat16 [16, 32, 18944], P(None, 'fsdp', 'label')
Inputs may be any that keep to these rules, and one draw needn't show every extreme that they name: `active_blocks`: each query block names 8 different owners; among the 8 query blocks held by one device no owner is named more than 6 times. `positives`: A code k * 128 + j names label j of the k-th active block of the query's block.
All inputs are finite; a program needn't handle non-finite values.
Results may differ from a plain program's by a relative error of at most 0.017.
Values may be sent and summed in bfloat16 or wider, within the bound.
No kernel may reach another device: no remote copies, remote signals or barrier semaphores. Data moves between devices by JAX's collectives and lax.ppermute only.
A program may use at most 64 MiB of HBM per device.

v0:
```python
import jax
import jax.numpy as jnp
from jax import lax
from jax.sharding import PartitionSpec as P

LBLOCK = 128
ACTIVE = 8
POS = 8
QBLOCK = 2


norm_epsilon = 1e-06


def shards(
    final_hidden, norm_gain, label_weights, active_blocks, positives, gate_pre, up_pre, down_weight
):
    owners = lax.axis_size("label")
    hidden_rows = final_hidden[0].astype(jnp.float32)
    query_count = hidden_rows.shape[0]
    feature_width = hidden_rows.shape[1]
    block_count = query_count // QBLOCK
    capacity = max(2, 3 * block_count * ACTIVE // (2 * owners))
    slot_total = owners * capacity
    inverse_rms = lax.rsqrt(
        jnp.mean(hidden_rows * hidden_rows, axis=1, keepdims=True) + norm_epsilon
    )
    normed = hidden_rows * inverse_rms
    embedded = (normed * norm_gain).astype(jnp.bfloat16)
    owner_list = active_blocks[0].reshape(block_count * ACTIVE)
    owner_hits = (owner_list[:, None] == jnp.arange(owners, dtype=jnp.int32)[None, :]).astype(
        jnp.int32
    )
    earlier_hits = jnp.cumsum(owner_hits, axis=0) - owner_hits
    slot_rank = jnp.sum(earlier_hits * owner_hits, axis=1)
    slot_index = owner_list * capacity + slot_rank
    placing = (jnp.arange(slot_total, dtype=jnp.int32)[:, None] == slot_index[None, :]).astype(
        jnp.int32
    )
    block_select = jnp.sum(placing.reshape(slot_total, block_count, ACTIVE), axis=2).astype(
        jnp.bfloat16
    )
    send_rows = jnp.dot(
        block_select,
        embedded.reshape(block_count, QBLOCK * feature_width),
        preferred_element_type=jnp.float32,
    )
    send_rows = send_rows.astype(jnp.bfloat16).reshape(owners, capacity, QBLOCK, feature_width)
    code_table = positives[0].reshape(block_count, 1, QBLOCK, POS)
    block_base = (jnp.arange(ACTIVE, dtype=jnp.int32) * LBLOCK).reshape(1, ACTIVE, 1, 1)
    offsets = code_table - block_base
    offsets = jnp.where((offsets >= 0) & (offsets < LBLOCK), offsets, -1)
    send_marks = jnp.dot(placing, (offsets + 1).reshape(block_count * ACTIVE, QBLOCK * POS)) - 1
    send_marks = send_marks.reshape(owners, capacity, QBLOCK, POS)
    label_rows = label_weights[0]
    query_embed = lax.all_to_all(send_rows, "label", split_axis=0, concat_axis=0, tiled=True)
    query_marks = lax.all_to_all(send_marks, "label", split_axis=0, concat_axis=0, tiled=True)
    scores = jnp.einsum(
        "ncqd,ld->ncql", query_embed, label_rows, preferred_element_type=jnp.float32
    )
    labels_here = jnp.arange(LBLOCK, dtype=jnp.int32)
    positive = jnp.any(query_marks[..., None] == labels_here, axis=3)
    target_sign = jnp.where(positive, 1.0, -1.0)
    margin = jnp.maximum(1.0 - target_sign * scores, 0.0)
    slope = (-2.0 * target_sign * margin).astype(jnp.bfloat16)
    partial_grad = jnp.einsum(
        "ncql,ld->ncqd", slope, label_rows, preferred_element_type=jnp.float32
    ).astype(jnp.bfloat16)
    returned = lax.all_to_all(partial_grad, "label", split_axis=0, concat_axis=0, tiled=True)
    embed_grad = jnp.dot(
        block_select.T,
        returned.reshape(slot_total, QBLOCK * feature_width),
        preferred_element_type=jnp.float32,
    )
    embed_grad = embed_grad.reshape(query_count, feature_width)
    scaled = norm_gain * embed_grad
    resid = inverse_rms * (scaled - normed * jnp.mean(normed * scaled, axis=1, keepdims=True))
    resid_bf = resid.astype(jnp.bfloat16)
    gate_full = gate_pre.astype(jnp.float32)
    up_full = up_pre.astype(jnp.float32)
    sigma = jax.nn.sigmoid(gate_full)
    group_rows = gate_pre.shape[0] * gate_pre.shape[1]
    ff_local = gate_pre.shape[2]
    hidden_act = (gate_full * sigma * up_full).astype(jnp.bfloat16).reshape(group_rows, ff_local)
    row_grads = lax.all_gather(resid_bf[None], "label", axis=0, tiled=True).reshape(
        group_rows, feature_width
    )
    columns = row_grads
    hidden_grad = jnp.dot(
        columns,
        lax.all_gather(down_weight, "fsdp", axis=0, tiled=True),
        preferred_element_type=jnp.float32,
    )
    columns = row_grads
    down_grad = lax.psum_scatter(
        lax.dot_general(
            columns, hidden_act, (((0,), (0,)), ((), ())), preferred_element_type=jnp.float32
        ).astype(jnp.bfloat16),
        "fsdp",
        scatter_dimension=0,
        tiled=True,
    ).astype(jnp.float32)
    hidden_grad = hidden_grad.reshape(gate_pre.shape)
    up_grad = (hidden_grad * gate_full * sigma).astype(jnp.bfloat16)
    gate_grad = (hidden_grad * up_full * sigma * (1.0 + gate_full * (1.0 - sigma))).astype(
        jnp.bfloat16
    )
    return (resid_bf[None], down_grad, gate_grad, up_grad)


def solution(mesh):
    placed = (
        P("label", "fsdp", None),
        P(),
        P("label", None, None),
        P("label", "fsdp", None),
        P("label", "fsdp", None),
        P(None, "fsdp", "label"),
        P(None, "fsdp", "label"),
        P("fsdp", "label"),
    )
    return jax.shard_map(
        shards,
        mesh=mesh,
        in_specs=placed,
        out_specs=(
            P("label", "fsdp", None),
            P("fsdp", "label"),
            P(None, "fsdp", "label"),
            P(None, "fsdp", "label"),
        ),
        check_vma=False,
    )
```

profile of v0, /device:TPU:0, one launch (start us, length us, event | category | flops | bytes accessed | tf_op | source)
XLA Modules:
  0.0 220.4 jit_solution(14514957748237149605)
XLA Ops:
  7.2 0.0 copy-start
  7.2 0.0 copy-start.3
  7.2 0.0 copy-start.2
  7.2 0.8 eq.49
  8.1 0.1 sub.45
  8.1 0.8 copy.35
  8.9 0.1 copy.36
  9.0 0.1 fusion.49
  9.1 0.1 reduce_window_sum.11
  9.2 0.2 select_reduce_fusion
  9.3 0.1 sub.42
  9.4 0.1 sub.43
  9.5 0.1 copy.37
  9.6 0.3 convolution_add_fusion
  9.9 0.1 reshape.140
  10.0 0.9 copy.38
  10.9 8.3 %all-to-all-start = ((s32[16,6,2,8]{3,2,1,0:T(2,128)}), s32[16,6,2,8]{3,2,1,0:T(2,128)S(1)}, u32[]{:S(2)}, u32[]{:S(2)}) async-start(s32[16,6,2,8]{3,2,1,0:T(2,128)} %copy.38), calls=%async_computation | async-start | bytes 196608 | tf_op jit(solution)/shard_map/all_to_all | solution.py:57
  19.2 0.1 reduce_sum.40
  19.3 1.0 fusion.37
  20.4 0.9 reshape.146
  21.3 0.1 rsqrt.13
  21.4 0.1 copy.40
  21.5 0.0 copy-done.2
  21.5 0.0 copy-done.3
  21.6 0.1 convert_reduce_fusion
  21.7 0.1 mul.150
  21.7 0.6 convolution_convert_fusion
  22.3 1.9 reshape.141
  24.2 2.7 %all-to-all-done = s32[16,6,2,8]{3,2,1,0:T(2,128)S(1)} async-done(((s32[16,6,2,8]{3,2,1,0:T(2,128)}), s32[16,6,2,8]{3,2,1,0:T(2,128)S(1)}, u32[]{:S(2)}, u32[]{:S(2)}) %all-to-all-start) | async-done | bytes 6176 | tf_op jit(solution)/shard_map/all_to_all | solution.py:57
  26.9 4.2 %all-to-all-start.1 = ((bf16[16,6,2,3584]{3,2,1,0:T(2,128)(2,1)}), bf16[16,6,2,3584]{3,2,1,0:T(2,128)(2,1)S(1)}, u32[]{:S(2)}, u32[]{:S(2)}) async-start(bf16[16,6,2,3584]{3,2,1,0:T(2,128)(2,1)} %reshape.141), calls=%async_computation.1 | async-start | bytes 2752512 | tf_op jit(solution)/shard_map/all_to_all | solution.py:56
  31.1 0.0 all-gather.3.cloned.1.call-start
  31.2 0.4 fusion.34
  31.5 29.9 %all-to-all-done.1 = bf16[16,6,2,3584]{3,2,1,0:T(2,128)(2,1)S(1)} async-done(((bf16[16,6,2,3584]{3,2,1,0:T(2,128)(2,1)}), bf16[16,6,2,3584]{3,2,1,0:T(2,128)(2,1)S(1)}, u32[]{:S(2)}, u32[]{:S(2)}) %all-to-all-start.1) | async-done | bytes 1376288 | tf_op jit(solution)/shard_map/all_to_all | solution.py:56
  61.4 0.0 copy-done
  61.4 2.7 %convolution_convert_fusion.1 = bf16[16,6,2,3584]{3,0,2,1:T(8,128)(2,1)} fusion(bf16[16,6,2,3584]{3,2,1,0:T(2,128)(2,1)S(1)} %all-to-all-done.1, bf16[1,128,3584]{2,1,0:T(8,128)(2,1)S(1)} %copy-done, pred[16,6,2,128]{3,2,1,0:T(4,128)(4,1)S(1)} %fusion.34), kind=kOutput, calls=%fused_computation.5 | convolution fusion | flops 353181696 | bytes 3694592 | tf_op jit(solution)/shard_map/ncql,ld->ncqd/dot_general | solution.py:66
  64.1 2.8 %copy.42 = bf16[16,6,2,3584]{3,2,1,0:T(2,128)(2,1)S(1)} copy(bf16[16,6,2,3584]{3,0,2,1:T(8,128)(2,1)} %convolution_convert_fusion.1) | data formatting | bytes 2752512 | tf_op jit(solution)/shard_map/convert_element_type | solution.py:68
  66.9 39.3 %all_to_all.15 = bf16[16,6,2,3584]{3,2,1,0:T(2,128)(2,1)S(1)} all-to-all(bf16[16,6,2,3584]{3,2,1,0:T(2,128)(2,1)S(1)} %copy.42), channel_id=1, replica_groups=mesh['label'=16,'fsdp'=2] {'label'}, dimensions={0} | all-to-all | bytes 2752512 | tf_op jit(solution)/shard_map/all_to_all | solution.py:69
  106.2 0.2 copy.44
  106.4 0.0 copy-start.1
  106.4 0.3 fusion.60
  106.8 0.5 copy-done.1
  107.3 0.2 fusion.39
  107.5 0.8 multiply_convert_fusion
  108.3 0.0 all-gather.3.cloned.1.call-update
  108.3 0.0 copy-start.5
  108.3 0.0 copy-start.6
  108.3 0.0 all-gather.5.cloned.1.call-start
  108.4 0.7 all-gather.5.cloned.1.call-update
  109.1 0.0 reduce-scatter.2.cloned.1.call-start
  109.1 56.3 %all-gather.3.cloned.1.call-done = bf16[16,16,3584]{2,1,0:T(8,128)(2,1)} async-done(((bf16[1,16,3584]{2,1,0:T(8,128)(2,1)}), bf16[16,16,3584]{2,1,0:T(8,128)(2,1)}) %all-gather.3.cloned.1.call-update) | async-done | bytes 1835024 | tf_op jit(solution)/shard_map/all_gather | solution.py:85
  165.4 0.0 copy-done.5
  165.4 0.0 copy-done.6
  165.4 7.8 %fusion = bf16[3584,1184]{0,1:T(8,128)(2,1)} fusion(bf16[16,16,3584]{2,1,0:T(8,128)(2,1)} %all-gather.3.cloned.1.call-done, bf16[16,16,1184]{2,1,0:T(8,128)(2,1)S(1)} %copy-done.5, bf16[16,16,1184]{2,1,0:T(8,128)(2,1)S(1)} %copy-done.6), kind=kOutput, calls=%fused_computation.1 | convolution fusion | flops 2179317760 | bytes 11534336 | tf_op jit(solution)/shard_map/dot_general | solution.py:96
  173.2 0.0 copy-start.4
  173.2 0.0 reduce-scatter.2.cloned.1.call-update
  173.2 13.4 %all-gather.5.cloned.1.call-done = bf16[3584,1184]{0,1:T(8,128)(2,1)} async-done(((bf16[1792,1184]{0,1:T(8,128)(2,1)}), bf16[3584,1184]{0,1:T(8,128)(2,1)}) %all-gather.5.cloned.1.call-update) | async-done | bytes 8486928 | tf_op jit(solution)/shard_map/all_gather | solution.py:91
  186.6 0.0 copy-done.4
  186.6 7.4 %fusion.14 = (bf16[16,16,1184]{2,1,0:T(8,128)(2,1)}, bf16[16,16,1184]{2,1,0:T(8,128)(2,1)}) fusion(bf16[16,16,1184]{2,1,0:T(8,128)(2,1)} %param.13, bf16[16,16,1184]{2,1,0:T(8,128)(2,1)S(1)} %copy-done.5, bf16[16,16,3584]{2,1,0:T(8,128)(2,1)S(1)} %copy-done.4, bf16[3584,1184]{0,1:T(8,128)(2,1)} %all-gather.5.cloned.1.call-done), kind=kOutput, calls=%fused_computation.23 | convolution fusion | flops 2177196032 | bytes 12746752 | tf_op jit(solution)/shard_map/dot_general | solution.py:89
  194.0 13.6 %reduce-scatter.2.cloned.1.call-done = bf16[1792,1184]{0,1:T(8,128)(2,1)} async-done(((bf16[3584,1184]{0,1:T(8,128)(2,1)}), bf16[1792,1184]{0,1:T(8,128)(2,1)}) %reduce-scatter.2.cloned.1.call-update) | async-done | bytes 4243472 | tf_op jit(solution)/shard_map/reduce_scatter | solution.py:95
  207.6 6.3 %convert_element_type.80 = f32[1792,1184]{0,1:T(8,128)} convert(bf16[1792,1184]{0,1:T(8,128)(2,1)} %reduce-scatter.2.cloned.1.call-done) | non-fusion elementwise | flops 2121728 | bytes 12730368 | tf_op jit(solution)/shard_map/convert_element_type | solution.py:102
  (10 shorter events, 0.1 us)
Async XLA Ops:
  7.2 54.2 %copy-start = (bf16[1,128,3584]{2,1,0:T(8,128)(2,1)S(1)}, bf16[1,128,3584]{2,1,0:T(8,128)(2,1)}, u32[]{:S(2)}) copy-start(bf16[1,128,3584]{2,1,0:T(8,128)(2,1)} %param.10) | copy-start | bytes 2752516
  7.2 14.4 %copy-start.3 = (s32[1,8,8]{2,1,0:T(8,128)S(1)}, s32[1,8,8]{2,1,0:T(8,128)}, u32[]{:S(2)}) copy-start(s32[1,8,8]{2,1,0:T(8,128)} %param.11) | copy-start | bytes 772
  7.2 14.3 %copy-start.2 = (f32[3584]{0:T(1024)S(1)}, f32[3584]{0:T(1024)}, u32[]{:S(2)}) copy-start(f32[3584]{0:T(1024)} %param.9) | copy-start | bytes 43012
  10.9 16.0 %all-to-all-start = ((s32[16,6,2,8]{3,2,1,0:T(2,128)}), s32[16,6,2,8]{3,2,1,0:T(2,128)S(1)}, u32[]{:S(2)}, u32[]{:S(2)}) async-start(s32[16,6,2,8]{3,2,1,0:T(2,128)} %copy.38), calls=%async_computation | async-start | bytes 196608 | tf_op jit(solution)/shard_map/all_to_all | solution.py:57
  26.9 34.5 %all-to-all-start.1 = ((bf16[16,6,2,3584]{3,2,1,0:T(2,128)(2,1)}), bf16[16,6,2,3584]{3,2,1,0:T(2,128)(2,1)S(1)}, u32[]{:S(2)}, u32[]{:S(2)}) async-start(bf16[16,6,2,3584]{3,2,1,0:T(2,128)(2,1)} %reshape.141), calls=%async_computation.1 | async-start | bytes 2752512 | tf_op jit(solution)/shard_map/all_to_all | solution.py:56
  31.1 134.3 %all-gather.3.cloned.1.call-start = ((), (), s32[]{:S(2)}) async-start(), calls=%async_computation.4 | async-start | bytes 1949696 | tf_op jit(solution)/shard_map/all_gather | solution.py:85
  106.4 0.9 copy-start.1
  108.3 57.2 %copy-start.5 = (bf16[16,16,1184]{2,1,0:T(8,128)(2,1)S(1)}, bf16[16,16,1184]{2,1,0:T(8,128)(2,1)}, u32[]{:S(2)}) copy-start(bf16[16,16,1184]{2,1,0:T(8,128)(2,1)} %param.14) | copy-start | bytes 1818628
  108.3 57.1 %copy-start.6 = (bf16[16,16,1184]{2,1,0:T(8,128)(2,1)S(1)}, bf16[16,16,1184]{2,1,0:T(8,128)(2,1)}, u32[]{:S(2)}) copy-start(bf16[16,16,1184]{2,1,0:T(8,128)(2,1)} %param.13) | copy-start | bytes 1818628
  108.3 78.3 %all-gather.5.cloned.1.call-start = ((), (), s32[]{:S(2)}) async-start(), calls=%async_computation.6 | async-start | bytes 12730368 | tf_op jit(solution)/shard_map/all_gather | solution.py:91
  109.1 98.5 %reduce-scatter.2.cloned.1.call-start = ((), (), s32[]{:S(2)}) async-start(), calls=%async_computation.5 | async-start | bytes 12730368 | tf_op jit(solution)/shard_map/reduce_scatter | solution.py:95
  173.2 13.4 %copy-start.4 = (bf16[16,16,3584]{2,1,0:T(8,128)(2,1)S(1)}, bf16[16,16,3584]{2,1,0:T(8,128)(2,1)}, u32[]{:S(2)}) copy-start(bf16[16,16,3584]{2,1,0:T(8,128)(2,1)} %all-gather.3.cloned.1.call-done) | copy-start | bytes 5505028
Sparse Core Ops, SparseCore 0:
  108.4 56.9 all-gather.2
  167.0 19.5 all-gather.4
  189.5 18.0 reduce-scatter.1
where the time goes:
time: 221 us; the launch traced here: 220 us
  waiting for transfers between devices  117 us (53%)
  blocking collectives  39.3 us (18%)
  matrix products  19 us (9%)
  between operations  13.9 us (6%)
  starting transfers between devices  12.6 us (6%)
  local copies, waits for them, and re-layouts  9.76 us (4%)
  other arithmetic  9.14 us (4%)
    all_gather x1, waiting for transfers between devices, shards(): lax.all_gather(resid_bf[None], 'label', axis=0, tiled=True)  56.3 us
    all_to_all x1, blocking collectives, shards(): lax.all_to_all(partial_grad, 'label', split_axis=0, concat_axis=0, tiled=...  39.3 us
    all_to_all x1, waiting for transfers between devices, shards(): lax.all_to_all(send_rows, 'label', split_axis=0, concat_axis=0, tiled=True)  29.9 us
    reduce_scatter x1, waiting for transfers between devices, shards(): lax.psum_scatter(lax.dot_general(columns, hidden_act, (((0,), (0,)), ((),...  13.6 us
    all_gather x1, waiting for transfers between devices, shards(): lax.all_gather(down_weight, 'fsdp', axis=0, tiled=True)  13.4 us
    all_to_all x1, starting transfers between devices, shards(): lax.all_to_all(send_marks, 'label', split_axis=0, concat_axis=0, tiled=True)  8.31 us
    dot_general x1, matrix products, shards(): lax.dot_general(columns, hidden_act, (((0,), (0,)), ((), ())), preferred_...  7.75 us
    dot_general x1, matrix products, shards(): jnp.dot(columns, lax.all_gather(down_weight, 'fsdp', axis=0, tiled=True),...  7.37 us
  transfers between devices with their start and end apart: 5, of which 5 were waited for; matrix products, arithmetic and copies ran while one was open for 9% of the time, Pallas kernels for 0%

commit v1 on v0

v1 whole, which is shorter than its diff:
```python
import jax
import jax.numpy as jnp
from jax import lax
from jax.sharding import PartitionSpec as P

ACTIVE = 8
QBLOCK = 2
PLANE = 4
META = 128

norm_epsilon = 1e-06


def shards(
    final_hidden, norm_gain, label_weights, active_blocks, positives, gate_pre, up_pre, down_weight
):
    owners = lax.axis_size("label")
    groups = lax.axis_size("fsdp")
    depth = owners // PLANE
    here = lax.axis_index("label")
    core = lax.axis_index("fsdp")
    label_rows = label_weights[0]
    block_labels, width = label_rows.shape
    share = block_labels // groups
    half = width // 2

    def across(array, mask):
        return lax.ppermute(array, "label", [(i, i ^ mask) for i in range(owners)])

    def along(array, step):
        return lax.ppermute(
            array, "label", [(i, (i + PLANE * step) % owners) for i in range(owners)]
        )

    def between(array, step):
        return lax.ppermute(array, "fsdp", [(i, (i + step) % groups) for i in range(groups)])

    mine = lax.dynamic_slice_in_dim(label_rows, core * share, share, 0)
    from_x = across(mine, 1)
    from_y = across(mine, 2)
    from_diagonal = jnp.concatenate(
        [across(from_x[:, :half], 2), across(from_y[:, half:], 1)], axis=1
    )

    hidden_rows = final_hidden[0].astype(jnp.float32)
    query_count = hidden_rows.shape[0]
    inverse_rms = lax.rsqrt(
        jnp.mean(hidden_rows * hidden_rows, axis=1, keepdims=True) + norm_epsilon
    )
    normed = hidden_rows * inverse_rms
    embedded = (normed * norm_gain).astype(jnp.bfloat16)
    owner_rows = jnp.repeat(active_blocks[0], QBLOCK, axis=0)
    codes = positives[0]
    code_block = codes // block_labels
    code_owner = jnp.sum(
        jnp.where(
            code_block[:, :, None] == jnp.arange(ACTIVE, dtype=jnp.int32),
            owner_rows[:, None, :],
            0,
        ),
        axis=2,
    )
    marks = jnp.concatenate([owner_rows, code_owner, codes % block_labels], axis=1)
    marks = jnp.pad(marks, ((0, 0), (0, META - marks.shape[1]))).astype(jnp.bfloat16)
    packet = jnp.concatenate([embedded, marks], axis=1)
    packets = jnp.concatenate(
        [packet] + [along(packet, step) for step in range(1, depth)], axis=0
    )

    fetched = jnp.stack([from_x, from_y, from_diagonal])
    pieces = [fetched] + [between(fetched, step) for step in range(1, groups)]
    plane_rows = jnp.concatenate(
        [label_rows] + [piece[k] for k in range(PLANE - 1) for piece in pieces], axis=0
    )
    within = jnp.arange(share, dtype=jnp.int32)
    fetched_labels = jnp.concatenate(
        [((core - step) % groups) * share + within for step in range(groups)]
    )
    column_label = jnp.concatenate(
        [jnp.arange(block_labels, dtype=jnp.int32)] + [fetched_labels] * (PLANE - 1)
    )
    column_owner = jnp.repeat(here ^ jnp.arange(PLANE, dtype=jnp.int32), block_labels)

    query_embed = packets[:, :width]
    query_marks = packets[:, width : width + 3 * ACTIVE].astype(jnp.int32)
    scores = lax.dot_general(
        query_embed, plane_rows, (((1,), (1,)), ((), ())), preferred_element_type=jnp.float32
    )
    active = jnp.zeros(scores.shape, jnp.bool_)
    positive = jnp.zeros(scores.shape, jnp.bool_)
    for k in range(ACTIVE):
        active |= query_marks[:, k : k + 1] == column_owner
        positive |= (query_marks[:, ACTIVE + k : ACTIVE + k + 1] == column_owner) & (
            query_marks[:, 2 * ACTIVE + k : 2 * ACTIVE + k + 1] == column_label
        )
    target_sign = jnp.where(positive, 1.0, -1.0)
    margin = jnp.maximum(1.0 - target_sign * scores, 0.0)
    slope = jnp.where(active, -2.0 * target_sign * margin, 0.0).astype(jnp.bfloat16)
    partial_grad = jnp.dot(slope, plane_rows, preferred_element_type=jnp.float32).astype(
        jnp.bfloat16
    )
    partial_grad = partial_grad.reshape(depth, query_count, width)
    embed_grad = partial_grad[0].astype(jnp.float32)
    for step in range(1, depth):
        embed_grad += along(partial_grad[step], -step).astype(jnp.float32)

    scaled = norm_gain * embed_grad
    resid = inverse_rms * (scaled - normed * jnp.mean(normed * scaled, axis=1, keepdims=True))
    resid_bf = resid.astype(jnp.bfloat16)

    line = jnp.stack([resid_bf] + [along(resid_bf, step) for step in range(1, depth)])
    line_x = across(line, 1)
    line_y = across(line, 2)
    line_diagonal = jnp.concatenate(
        [across(line_x[..., :half], 2), across(line_y[..., half:], 1)], axis=2
    )
    gathered = jnp.stack([line, line_x, line_y, line_diagonal])
    spots = jnp.arange(owners, dtype=jnp.int32)
    place = ((spots ^ here) % PLANE) * depth + (here // PLANE - spots // PLANE) % depth
    row_grads = jnp.take(
        gathered.reshape(owners, query_count, width), place, axis=0
    ).reshape(owners * query_count, width)

    gate_full = gate_pre.astype(jnp.float32)
    up_full = up_pre.astype(jnp.float32)
    sigma = jax.nn.sigmoid(gate_full)
    group_rows = gate_pre.shape[0] * gate_pre.shape[1]
    ff_local = gate_pre.shape[2]
    hidden_act = (gate_full * sigma * up_full).astype(jnp.bfloat16).reshape(group_rows, ff_local)

    slab = width // groups

    def slab_of(index):
        return lax.dynamic_slice_in_dim(row_grads, (index % groups) * slab, slab, 1)

    hidden_grad = jnp.dot(slab_of(core), down_weight, preferred_element_type=jnp.float32)
    down_grad = lax.dot_general(
        slab_of(core), hidden_act, (((0,), (0,)), ((), ())), preferred_element_type=jnp.float32
    )
    for step in range(1, groups):
        hidden_grad += jnp.dot(
            slab_of(core - step), between(down_weight, step), preferred_element_type=jnp.float32
        )
        down_grad += lax.dot_general(
            between(slab_of(core + step), step),
            between(hidden_act, step),
            (((0,), (0,)), ((), ())),
            preferred_element_type=jnp.float32,
        )
    hidden_grad = hidden_grad.reshape(gate_pre.shape)
    up_grad = (hidden_grad * gate_full * sigma).astype(jnp.bfloat16)
    gate_grad = (hidden_grad * up_full * sigma * (1.0 + gate_full * (1.0 - sigma))).astype(
        jnp.bfloat16
    )
    return (resid_bf[None], down_grad, gate_grad, up_grad)


def solution(mesh):
    placed = (
        P("label", "fsdp", None),
        P(),
        P("label", None, None),
        P("label", "fsdp", None),
        P("label", "fsdp", None),
        P(None, "fsdp", "label"),
        P(None, "fsdp", "label"),
        P("fsdp", "label"),
    )
    return jax.shard_map(
        shards,
        mesh=mesh,
        in_specs=placed,
        out_specs=(
            P("label", "fsdp", None),
            P("fsdp", "label"),
            P(None, "fsdp", "label"),
            P(None, "fsdp", "label"),
        ),
        check_vma=False,
    )
```

time: 221 us -> 111 us (0.50)
  waiting for transfers between devices: 117 us -> 38.7 us
  blocking collectives: 39.3 us -> 0 us
  starting transfers between devices: 12.6 us -> 26.6 us
  between operations: 13.9 us -> 0.89 us
  local copies, waits for them, and re-layouts: 9.76 us -> 14.2 us
    all_gather x2 -> x0, waiting for transfers between devices: 69.7 us -> none  [the longest x1 56.3 us: shards(): lax.all_gather(resid_bf[None], 'label', axis=0, tiled=True)]
    all_to_all x1 -> x0, blocking collectives: 39.3 us -> none  [shards(): lax.all_to_all(partial_grad, 'label', split_axis=0, concat_axis=0, tiled=...]
    ppermute x0 -> x21, waiting for transfers between devices: none -> 38.7 us  [the longest x9 19.9 us: along(): lax.ppermute(array, 'label', [(i, (i + PLANE * step) % owners) for i in r...]
    all_to_all x2 -> x0, waiting for transfers between devices: 32.6 us -> none  [the longest x1 29.9 us: shards(): lax.all_to_all(send_rows, 'label', split_axis=0, concat_axis=0, tiled=True)]
    ppermute x0 -> x21, starting transfers between devices: none -> 26.6 us  [the longest x9 13.9 us: along(): lax.ppermute(array, 'label', [(i, (i + PLANE * step) % owners) for i in r...]
    reduce_scatter x1 -> x0, waiting for transfers between devices: 13.6 us -> none  [shards(): lax.psum_scatter(lax.dot_general(columns, hidden_act, (((0,), (0,)), ((),...]
    all_to_all x2 -> x0, starting transfers between devices: 12.5 us -> none  [the longest x1 8.31 us: shards(): lax.all_to_all(send_marks, 'label', split_axis=0, concat_axis=0, tiled=True)]
    unnamed x16, local copies, waits for them, and re-layouts: 1.48 us -> 5.68 us
  transfers between devices with their start and end apart: 5 -> 21, of which waited for: 5 -> 12; matrix products, arithmetic and copies ran while one was open for 9% -> 24% of each run, Pallas kernels for 0% -> 0%
where the time goes in v1:
time: 111 us; the launch traced here: 110 us
  waiting for transfers between devices  38.7 us (35%)
  starting transfers between devices  26.6 us (24%)
  matrix products  19.5 us (18%)
  local copies, waits for them, and re-layouts  14.2 us (13%)
  other arithmetic  10 us (9%)
    ppermute x9, waiting for transfers between devices, along(): lax.ppermute(array, 'label', [(i, (i + PLANE * step) % owners) for i in r...  19.9 us
    ppermute x8, waiting for transfers between devices, across(): return lax.ppermute(array, 'label', [(i, i ^ mask) for i in range(owners)])  18.5 us
    ppermute x9, starting transfers between devices, along(): lax.ppermute(array, 'label', [(i, (i + PLANE * step) % owners) for i in r...  13.9 us
    ppermute x8, starting transfers between devices, across(): return lax.ppermute(array, 'label', [(i, i ^ mask) for i in range(owners)])  12.2 us
    dot_general x1, matrix products, shards(): lax.dot_general(between(slab_of(core + step), step), between(hidden_act,...  5.87 us
    unnamed x16, local copies, waits for them, and re-layouts  5.68 us
    dot_general x1, matrix products, shards(): jnp.dot(slope, plane_rows, preferred_element_type=jnp.float32)  5.3 us
    dot_general x1, matrix products, shards(): jnp.dot(slab_of(core - step), between(down_weight, step), preferred_eleme...  3.55 us
  transfers between devices with their start and end apart: 21, of which 12 were waited for; matrix products, arithmetic and copies ran while one was open for 24% of the time, Pallas kernels for 0%

profile of v1, /device:TPU:0, one launch (start us, length us, event | category | flops | bytes accessed | tf_op | source)
XLA Modules:
  0.0 110.0 jit_solution(12054723405047453177)
XLA Ops:
  0.6 1.1 dynamic-slice_bitcast_fusion
  1.7 3.0 %collective-permute-start.3 = (bf16[64,3584]{1,0:T(8,128)(2,1)S(1)}, bf16[64,3584]{1,0:T(8,128)(2,1)S(1)}, u32[]{:S(2)}, u32[]{:S(2)}) collective-permute-start(bf16[64,3584]{1,0:T(8,128)(2,1)S(1)} %dynamic-slice_bitcast_fusion), channel_id=1, source_target_pairs={{0,2},{2,0},{4,6},{6,4},{8,10},{10,8},{12,14},{14,12},{16,18},{18,... | collective-permute-start | bytes 1376264 | tf_op jit(solution)/shard_map/ppermute | solution.py:28
  4.7 1.5 %collective-permute-start.4 = (bf16[64,3584]{1,0:T(8,128)(2,1)S(1)}, bf16[64,3584]{1,0:T(8,128)(2,1)S(1)}, u32[]{:S(2)}, u32[]{:S(2)}) collective-permute-start(bf16[64,3584]{1,0:T(8,128)(2,1)S(1)} %dynamic-slice_bitcast_fusion), channel_id=1, source_target_pairs={{0,4},{2,6},{4,0},{6,2},{8,12},{10,14},{12,8},{14,10},{16,20},{18,... | collective-permute-start | bytes 1376264 | tf_op jit(solution)/shard_map/ppermute | solution.py:28
  6.2 0.7 broadcast_in_dim.59
  7.0 0.7 add_select_fusion.1
  7.7 0.1 copy.43
  7.8 1.0 fusion.33
  8.9 1.0 fusion.28
  9.9 5.3 %collective-permute-done.3 = bf16[64,3584]{1,0:T(8,128)(2,1)S(1)} collective-permute-done((bf16[64,3584]{1,0:T(8,128)(2,1)S(1)}, bf16[64,3584]{1,0:T(8,128)(2,1)S(1)}, u32[]{:S(2)}, u32[]{:S(2)}) %collective-permute-start.3) | collective-permute-done | bytes 458784 | tf_op jit(solution)/shard_map/ppermute | solution.py:28
  15.2 1.8 %collective-permute-start.5 = (bf16[64,1792]{1,0:T(8,128)(2,1)S(1)}, bf16[64,1792]{1,0:T(8,128)(2,1)S(1)}, u32[]{:S(2)}, u32[]{:S(2)}) collective-permute-start(bf16[64,1792]{1,0:T(8,128)(2,1)S(1)} %slice.178), channel_id=1, source_target_pairs={{0,4},{2,6},{4,0},{6,2},{8,12},{10,14},{12,8},{14,10},{16,20},{18,... | collective-permute-start | bytes 688136 | tf_op jit(solution)/shard_map/ppermute | solution.py:28
  17.1 1.6 %collective-permute-start.6 = (bf16[64,1792]{1,0:T(8,128)(2,1)S(1)}, bf16[64,1792]{1,0:T(8,128)(2,1)S(1)}, u32[]{:S(2)}, u32[]{:S(2)}) collective-permute-start(bf16[64,1792]{1,0:T(8,128)(2,1)S(1)} %slice.179), channel_id=1, source_target_pairs={{0,2},{2,0},{4,6},{6,4},{8,10},{10,8},{12,14},{14,12},{16,18},{18,... | collective-permute-start | bytes 688136 | tf_op jit(solution)/shard_map/ppermute | solution.py:28
  18.7 1.6 %collective-permute-start = (bf16[16,3712]{1,0:T(8,128)(2,1)S(1)}, bf16[16,3712]{1,0:T(8,128)(2,1)S(1)}, u32[]{:S(2)}, u32[]{:S(2)}) collective-permute-start(bf16[16,3712]{1,0:T(8,128)(2,1)S(1)} %pad_maximum_fusion.15), channel_id=1, source_target_pairs={{0,8},{2,10},{4,12},{6,14},{8,16},{10,18},{12,20},{14,22},{16,24},... | collective-permute-start | bytes 356360 | tf_op jit(solution)/shard_map/ppermute | solution.py:31
  20.3 2.6 %collective-permute-start.1 = (bf16[16,3712]{1,0:T(8,128)(2,1)S(1)}, bf16[16,3712]{1,0:T(8,128)(2,1)S(1)}, u32[]{:S(2)}, u32[]{:S(2)}) collective-permute-start(bf16[16,3712]{1,0:T(8,128)(2,1)S(1)} %pad_maximum_fusion.15), channel_id=1, source_target_pairs={{0,16},{2,18},{4,20},{6,22},{8,24},{10,26},{12,28},{14,30},{16,0},... | collective-permute-start | bytes 356360 | tf_op jit(solution)/shard_map/ppermute | solution.py:31
  22.9 1.3 %collective-permute-start.2 = (bf16[16,3712]{1,0:T(8,128)(2,1)S(1)}, bf16[16,3712]{1,0:T(8,128)(2,1)S(1)}, u32[]{:S(2)}, u32[]{:S(2)}) collective-permute-start(bf16[16,3712]{1,0:T(8,128)(2,1)S(1)} %pad_maximum_fusion.15), channel_id=1, source_target_pairs={{0,24},{2,26},{4,28},{6,30},{8,0},{10,2},{12,4},{14,6},{16,8},{18,... | collective-permute-start | bytes 356360 | tf_op jit(solution)/shard_map/ppermute | solution.py:31
  24.3 1.2 %pad_maximum_fusion.1 = bf16[3,64,3584]{2,1,0:T(8,128)(2,1)} fusion(bf16[1,64,3584]{2,1,0:T(8,128)(2,1)S(1)} %maximum_bitcast_fusion, bf16[1,64,3584]{2,1,0:T(8,128)(2,1)S(1)} %bitcast.84, bf16[1,64,3584]{2,1,0:T(8,128)(2,1)S(1)} %bitcast.85), kind=kLoop, calls=%fused_computation.12 | loop fusion | flops 1376256 | bytes 2752512 | tf_op jit(solution)/shard_map/stack | solution.py:70
  25.5 1.0 bitcast_dynamic-update-slice_fusion
  26.5 0.1 concatenate.27
  26.7 2.9 %collective-permute-done.1 = bf16[16,3712]{1,0:T(8,128)(2,1)S(1)} collective-permute-done((bf16[16,3712]{1,0:T(8,128)(2,1)S(1)}, bf16[16,3712]{1,0:T(8,128)(2,1)S(1)}, u32[]{:S(2)}, u32[]{:S(2)}) %collective-permute-start.1) | collective-permute-done | bytes 118816 | tf_op jit(solution)/shard_map/ppermute | solution.py:31
  29.6 0.3 slice_reduce_fusion.22
  29.9 0.6 slice_reduce_fusion.23
  30.5 0.8 constant_dynamic-update-slice_fusion.2
  31.3 0.8 fusion.22
  32.1 0.8 constant_dynamic-update-slice_fusion.1
  32.9 0.8 fusion.21
  33.7 0.7 constant_dynamic-update-slice_fusion
  34.4 0.7 constant_dynamic-update-slice_fusion.3
  35.1 0.8 fusion.20
  35.9 5.3 %convolution_convert_fusion = bf16[64,3584]{1,0:T(8,128)(2,1)S(1)} fusion(bf16[512,3584]{1,0:T(8,128)(2,1)} %fusion.20, bf16[16,3712]{1,0:T(8,128)(2,1)S(1)} %collective-permute-done.2, bf16[16,3712]{1,0:T(8,128)(2,1)S(1)} %collective-permute-done.1, bf16[16,3712]{1,0:T(8,128)(2,1)S(1)} %collective-permute-done, bf16[16,128]{1,0:T(8,128)(2,1)S(1)} %pad.5.clone, ...), kind=kOutput, calls=%fused_computation.2 | convolution fusion | flops 474054656 | bytes 4614144 | tf_op jit(solution)/shard_map/dot_general | solution.py:99
  41.2 2.8 %collective-permute-start.10 = (bf16[16,3584]{1,0:T(8,128)(2,1)S(1)}, bf16[16,3584]{1,0:T(8,128)(2,1)S(1)}, u32[]{:S(2)}, u32[]{:S(2)}) collective-permute-start(bf16[16,3584]{1,0:T(8,128)(2,1)S(1)} %get-tuple-element.34), channel_id=1, source_target_pairs={{0,8},{2,10},{4,12},{6,14},{8,16},{10,18},{12,20},{14,22},{16,24},... | collective-permute-start | bytes 344072 | tf_op jit(solution)/shard_map/ppermute | solution.py:31
  44.1 1.1 collective-permute-start.8
  45.2 0.5 collective-permute-start.9
  45.7 3.6 %collective-permute-done.10 = bf16[16,3584]{1,0:T(8,128)(2,1)S(1)} collective-permute-done((bf16[16,3584]{1,0:T(8,128)(2,1)S(1)}, bf16[16,3584]{1,0:T(8,128)(2,1)S(1)}, u32[]{:S(2)}, u32[]{:S(2)}) %collective-permute-start.10) | collective-permute-done | bytes 114720 | tf_op jit(solution)/shard_map/ppermute | solution.py:31
  49.2 0.9 collective-permute-done.8
  50.2 4.8 %collective-permute-done.9 = bf16[16,3584]{1,0:T(8,128)(2,1)S(1)} collective-permute-done((bf16[16,3584]{1,0:T(8,128)(2,1)S(1)}, bf16[16,3584]{1,0:T(8,128)(2,1)S(1)}, u32[]{:S(2)}, u32[]{:S(2)}) %collective-permute-start.9) | collective-permute-done | bytes 114720 | tf_op jit(solution)/shard_map/ppermute | solution.py:31
  55.0 0.2 fusion.29
  55.2 0.1 fusion.32
  55.4 2.5 %collective-permute-start.12 = (bf16[16,3584]{1,0:T(8,128)(2,1)S(1)}, bf16[16,3584]{1,0:T(8,128)(2,1)S(1)}, u32[]{:S(2)}, u32[]{:S(2)}) collective-permute-start(bf16[16,3584]{1,0:T(8,128)(2,1)S(1)} %fusion.32), channel_id=1, source_target_pairs={{0,16},{2,18},{4,20},{6,22},{8,24},{10,26},{12,28},{14,30},{16,0},... | collective-permute-start | bytes 344072 | tf_op jit(solution)/shard_map/ppermute | solution.py:31
  57.9 1.3 %collective-permute-start.13 = (bf16[16,3584]{1,0:T(8,128)(2,1)S(1)}, bf16[16,3584]{1,0:T(8,128)(2,1)S(1)}, u32[]{:S(2)}, u32[]{:S(2)}) collective-permute-start(bf16[16,3584]{1,0:T(8,128)(2,1)S(1)} %fusion.32), channel_id=1, source_target_pairs={{0,24},{2,26},{4,28},{6,30},{8,0},{10,2},{12,4},{14,6},{16,8},{18,... | collective-permute-start | bytes 344072 | tf_op jit(solution)/shard_map/ppermute | solution.py:31
  59.3 4.1 %collective-permute-done.11 = bf16[16,3584]{1,0:T(8,128)(2,1)S(1)} collective-permute-done((bf16[16,3584]{1,0:T(8,128)(2,1)S(1)}, bf16[16,3584]{1,0:T(8,128)(2,1)S(1)}, u32[]{:S(2)}, u32[]{:S(2)}) %collective-permute-start.11) | collective-permute-done | bytes 114720 | tf_op jit(solution)/shard_map/ppermute | solution.py:31
  63.4 3.5 %collective-permute-done.12 = bf16[16,3584]{1,0:T(8,128)(2,1)S(1)} collective-permute-done((bf16[16,3584]{1,0:T(8,128)(2,1)S(1)}, bf16[16,3584]{1,0:T(8,128)(2,1)S(1)}, u32[]{:S(2)}, u32[]{:S(2)}) %collective-permute-start.12) | collective-permute-done | bytes 114720 | tf_op jit(solution)/shard_map/ppermute | solution.py:31
  66.9 0.1 fusion.135
  67.0 0.6 collective-permute-start.14
  67.6 0.8 collective-permute-start.15
  68.4 8.9 %collective-permute-done.14 = bf16[4,16,3584]{2,1,0:T(8,128)(2,1)S(1)} collective-permute-done((bf16[4,16,3584]{2,1,0:T(8,128)(2,1)S(1)}, bf16[4,16,3584]{2,1,0:T(8,128)(2,1)S(1)}, u32[]{:S(2)}, u32[]{:S(2)}) %collective-permute-start.14) | collective-permute-done | bytes 458784 | tf_op jit(solution)/shard_map/ppermute | solution.py:28
  77.3 0.4 collective-permute-start.16
  77.7 0.4 collective-permute-done.15
  78.2 2.5 %collective-permute-start.17 = (bf16[4,16,1792]{2,1,0:T(8,128)(2,1)S(1)}, bf16[4,16,1792]{2,1,0:T(8,128)(2,1)S(1)}, u32[]{:S(2)}, u32[]{:S(2)}) collective-permute-start(bf16[4,16,1792]{2,1,0:T(8,128)(2,1)S(1)} %slice.188), channel_id=1, source_target_pairs={{0,2},{2,0},{4,6},{6,4},{8,10},{10,8},{12,14},{14,12},{16,18},{18,... | collective-permute-start | bytes 688136 | tf_op jit(solution)/shard_map/ppermute | solution.py:28
  80.7 0.1 broadcast_in_dim.66
  80.8 0.1 broadcast_in_dim.67
  80.9 2.5 %collective-permute-done.16 = bf16[4,16,1792]{2,1,0:T(8,128)(2,1)S(1)} collective-permute-done((bf16[4,16,1792]{2,1,0:T(8,128)(2,1)S(1)}, bf16[4,16,1792]{2,1,0:T(8,128)(2,1)S(1)}, u32[]{:S(2)}, u32[]{:S(2)}) %collective-permute-start.16) | collective-permute-done | bytes 229408 | tf_op jit(solution)/shard_map/ppermute | solution.py:28
  83.4 1.3 %collective-permute-done.17 = bf16[4,16,1792]{2,1,0:T(8,128)(2,1)S(1)} collective-permute-done((bf16[4,16,1792]{2,1,0:T(8,128)(2,1)S(1)}, bf16[4,16,1792]{2,1,0:T(8,128)(2,1)S(1)}, u32[]{:S(2)}, u32[]{:S(2)}) %collective-permute-start.17) | collective-permute-done | bytes 229408 | tf_op jit(solution)/shard_map/ppermute | solution.py:28
  84.7 0.2 pad_maximum_fusion
  85.0 1.9 %gather_fusion = bf16[16,16,3584]{2,1,0:T(8,128)(2,1)} fusion(bf16[16,16,3584]{2,1,0:T(8,128)(2,1)S(1)} %bitcast.80, s32[1024]{0:T(1024)S(1)} %pad_clamp_fusion), kind=kCustom, calls=%fused_computation | custom fusion | bytes 3670080 | tf_op jit(solution)/shard_map/jit(_take)/gather | solution.py:120
  86.9 1.7 %bitcast_select_fusion = bf16[256,3584]{1,0:T(8,128)(2,1)S(1)} fusion(bf16[16,16,3584]{2,1,0:T(8,128)(2,1)} %gather_fusion, pred[256]{0:T(512)(128)(4,1)S(1)} %broadcast_in_dim.67), kind=kLoop, calls=%fused_computation.9 | loop fusion | flops 917504 | bytes 3670272 | tf_op jit(solution)/shard_map/jit(_take)/select_n | solution.py:120
  88.6 1.0 constant_dynamic-slice_fusion
  89.6 3.5 %fusion.16 = f32[256,1184]{0,1:T(8,128)S(1)} fusion(bf16[1792,1184]{0,1:T(8,128)(2,1)} %param.15, bf16[256,3584]{1,0:T(8,128)(2,1)S(1)} %bitcast_select_fusion, s32[]{:T(128)S(6)} %select_n.151), kind=kOutput, calls=%fused_computation.31 | convolution fusion | flops 1086324736 | bytes 6373380 | tf_op jit(solution)/shard_map/dot_general | solution.py:136
  93.1 3.6 %convolution_add_fusion.1 = f32[256,1184]{0,1:T(8,128)S(1)} fusion(f32[256,1184]{0,1:T(8,128)S(1)} %fusion.16, bf16[1792,1184]{0,1:T(8,128)(2,1)} %collective-permute-done.20, bf16[256,3584]{1,0:T(8,128)(2,1)S(1)} %bitcast_select_fusion, s32[]{:T(128)S(6)} %select_n.154), kind=kOutput, calls=%fused_computation.3 | convolution fusion | flops 1086627840 | bytes 7585796 | tf_op jit(solution)/shard_map/dot_general | solution.py:141
  96.7 1.5 %copy.42 = f32[256,1184]{1,0:T(8,128)} copy(f32[256,1184]{0,1:T(8,128)S(1)} %convolution_add_fusion.1) | data formatting | bytes 2424832 | tf_op jit(solution)/shard_map/add | solution.py:141
  98.1 3.5 %fusion.9 = (bf16[16,16,1184]{2,1,0:T(8,128)(2,1)}, bf16[16,16,1184]{2,1,0:T(8,128)(2,1)}, bf16[16,16,1184]{2,1,0:T(8,128)(2,1)S(1)}) fusion(f32[16,16,1184]{2,1,0:T(8,128)} %bitcast.83, bf16[16,16,1184]{2,1,0:T(8,128)(2,1)} %param.13, bf16[16,16,1184]{2,1,0:T(8,128)(2,1)} %param.14), kind=kLoop, calls=%fused_computation.22 | loop fusion | flops 5455872 | bytes 4243456 | tf_op jit(solution)/shard_map/convert_element_type | solution.py:151
  101.6 0.2 copy.41
  101.9 0.6 collective-permute-start.19
  102.4 1.3 %fusion.18 = f32[1792,1184]{0,1:T(8,128)S(1)} fusion(bf16[256,1184]{1,0:T(8,128)(2,1)S(1)} %bitcast.82, bf16[256,3584]{1,0:T(8,128)(2,1)S(1)} %bitcast_select_fusion, s32[]{:T(128)S(6)} %select_n.151), kind=kOutput, calls=%fused_computation.33 | convolution fusion | flops 1086324736 | bytes 10059780 | tf_op jit(solution)/shard_map/dot_general | solution.py:137
  103.8 0.3 collective-permute-done.19
  104.1 5.9 %convolution_add_fusion = f32[1792,1184]{0,1:T(8,128)} fusion(f32[1792,1184]{0,1:T(8,128)S(1)} %fusion.18, bf16[256,1184]{0,1:T(8,128)(2,1)S(1)} %collective-permute-done.19, bf16[256,1792]{1,0:T(8,128)(2,1)} %collective-permute-done.18), kind=kOutput, calls=%fused_computation.1 | convolution fusion | flops 1088446464 | bytes 18497536 | tf_op jit(solution)/shard_map/dot_general | solution.py:144
  (45 shorter events, 0.6 us)
Async XLA Ops:
  1.7 13.5 %collective-permute-start.3 = (bf16[64,3584]{1,0:T(8,128)(2,1)S(1)}, bf16[64,3584]{1,0:T(8,128)(2,1)S(1)}, u32[]{:S(2)}, u32[]{:S(2)}) collective-permute-start(bf16[64,3584]{1,0:T(8,128)(2,1)S(1)} %dynamic-slice_bitcast_fusion), channel_id=1, source_target_pairs={{0,2},{2,0},{4,6},{6,4},{8,10},{10,8},{12,14},{14,12},{16,18},{18,... | collective-permute-start | bytes 1376264 | tf_op jit(solution)/shard_map/ppermute | solution.py:28
  4.7 12.4 %collective-permute-start.4 = (bf16[64,3584]{1,0:T(8,128)(2,1)S(1)}, bf16[64,3584]{1,0:T(8,128)(2,1)S(1)}, u32[]{:S(2)}, u32[]{:S(2)}) collective-permute-start(bf16[64,3584]{1,0:T(8,128)(2,1)S(1)} %dynamic-slice_bitcast_fusion), channel_id=1, source_target_pairs={{0,4},{2,6},{4,0},{6,2},{8,12},{10,14},{12,8},{14,10},{16,20},{18,... | collective-permute-start | bytes 1376264 | tf_op jit(solution)/shard_map/ppermute | solution.py:28
  15.2 9.0 %collective-permute-start.5 = (bf16[64,1792]{1,0:T(8,128)(2,1)S(1)}, bf16[64,1792]{1,0:T(8,128)(2,1)S(1)}, u32[]{:S(2)}, u32[]{:S(2)}) collective-permute-start(bf16[64,1792]{1,0:T(8,128)(2,1)S(1)} %slice.178), channel_id=1, source_target_pairs={{0,4},{2,6},{4,0},{6,2},{8,12},{10,14},{12,8},{14,10},{16,20},{18,... | collective-permute-start | bytes 688136 | tf_op jit(solution)/shard_map/ppermute | solution.py:28
  17.1 7.2 %collective-permute-start.6 = (bf16[64,1792]{1,0:T(8,128)(2,1)S(1)}, bf16[64,1792]{1,0:T(8,128)(2,1)S(1)}, u32[]{:S(2)}, u32[]{:S(2)}) collective-permute-start(bf16[64,1792]{1,0:T(8,128)(2,1)S(1)} %slice.179), channel_id=1, source_target_pairs={{0,2},{2,0},{4,6},{6,4},{8,10},{10,8},{12,14},{14,12},{16,18},{18,... | collective-permute-start | bytes 688136 | tf_op jit(solution)/shard_map/ppermute | solution.py:28
  18.7 6.9 %copy-start = (bf16[1,128,3584]{2,1,0:T(8,128)(2,1)S(1)}, bf16[1,128,3584]{2,1,0:T(8,128)(2,1)}, u32[]{:S(2)}) copy-start(bf16[1,128,3584]{2,1,0:T(8,128)(2,1)} %param.10) | copy-start | bytes 2752516
  18.7 8.0 %collective-permute-start = (bf16[16,3712]{1,0:T(8,128)(2,1)S(1)}, bf16[16,3712]{1,0:T(8,128)(2,1)S(1)}, u32[]{:S(2)}, u32[]{:S(2)}) collective-permute-start(bf16[16,3712]{1,0:T(8,128)(2,1)S(1)} %pad_maximum_fusion.15), channel_id=1, source_target_pairs={{0,8},{2,10},{4,12},{6,14},{8,16},{10,18},{12,20},{14,22},{16,24},... | collective-permute-start | bytes 356360 | tf_op jit(solution)/shard_map/ppermute | solution.py:31
  20.3 9.3 %collective-permute-start.1 = (bf16[16,3712]{1,0:T(8,128)(2,1)S(1)}, bf16[16,3712]{1,0:T(8,128)(2,1)S(1)}, u32[]{:S(2)}, u32[]{:S(2)}) collective-permute-start(bf16[16,3712]{1,0:T(8,128)(2,1)S(1)} %pad_maximum_fusion.15), channel_id=1, source_target_pairs={{0,16},{2,18},{4,20},{6,22},{8,24},{10,26},{12,28},{14,30},{16,0},... | collective-permute-start | bytes 356360 | tf_op jit(solution)/shard_map/ppermute | solution.py:31
  22.9 6.7 %collective-permute-start.2 = (bf16[16,3712]{1,0:T(8,128)(2,1)S(1)}, bf16[16,3712]{1,0:T(8,128)(2,1)S(1)}, u32[]{:S(2)}, u32[]{:S(2)}) collective-permute-start(bf16[16,3712]{1,0:T(8,128)(2,1)S(1)} %pad_maximum_fusion.15), channel_id=1, source_target_pairs={{0,24},{2,26},{4,28},{6,30},{8,0},{10,2},{12,4},{14,6},{16,8},{18,... | collective-permute-start | bytes 356360 | tf_op jit(solution)/shard_map/ppermute | solution.py:31
  25.5 5.8 %collective-permute-start.7 = (bf16[3,64,3584]{2,1,0:T(8,128)(2,1)}, bf16[3,64,3584]{2,1,0:T(8,128)(2,1)S(1)}, u32[]{:S(2)}, u32[]{:S(2)}) collective-permute-start(bf16[3,64,3584]{2,1,0:T(8,128)(2,1)} %pad_maximum_fusion.1), channel_id=1, source_target_pairs={{0,1},{1,0},{2,3},{3,2},{4,5},{5,4},{6,7},{7,6},{8,9},{9,8},{10,11... | collective-permute-start | bytes 4128776 | tf_op jit(solution)/shard_map/ppermute | solution.py:36
  35.9 19.1 %copy-start.1 = (bf16[1,16,3584]{2,1,0:T(8,128)(2,1)S(1)}, bf16[1,16,3584]{2,1,0:T(8,128)(2,1)}, u32[]{:S(2)}) copy-start(bf16[1,16,3584]{2,1,0:T(8,128)(2,1)} %param.8) | copy-start | bytes 344068
  35.9 19.1 %copy-start.3 = (f32[3584]{0:T(1024)S(1)}, f32[3584]{0:T(1024)}, u32[]{:S(2)}) copy-start(f32[3584]{0:T(1024)} %param.9) | copy-start | bytes 43012
  41.2 8.0 %collective-permute-start.10 = (bf16[16,3584]{1,0:T(8,128)(2,1)S(1)}, bf16[16,3584]{1,0:T(8,128)(2,1)S(1)}, u32[]{:S(2)}, u32[]{:S(2)}) collective-permute-start(bf16[16,3584]{1,0:T(8,128)(2,1)S(1)} %get-tuple-element.34), channel_id=1, source_target_pairs={{0,8},{2,10},{4,12},{6,14},{8,16},{10,18},{12,20},{14,22},{16,24},... | collective-permute-start | bytes 344072 | tf_op jit(solution)/shard_map/ppermute | solution.py:31
  44.1 6.1 %collective-permute-start.8 = (bf16[16,3584]{1,0:T(8,128)(2,1)S(1)}, bf16[16,3584]{1,0:T(8,128)(2,1)S(1)}, u32[]{:S(2)}, u32[]{:S(2)}) collective-permute-start(bf16[16,3584]{1,0:T(8,128)(2,1)S(1)} %get-tuple-element.33), channel_id=1, source_target_pairs={{0,24},{2,26},{4,28},{6,30},{8,0},{10,2},{12,4},{14,6},{16,8},{18,... | collective-permute-start | bytes 344072 | tf_op jit(solution)/shard_map/ppermute | solution.py:31
  45.2 9.8 %collective-permute-start.9 = (bf16[16,3584]{1,0:T(8,128)(2,1)S(1)}, bf16[16,3584]{1,0:T(8,128)(2,1)S(1)}, u32[]{:S(2)}, u32[]{:S(2)}) collective-permute-start(bf16[16,3584]{1,0:T(8,128)(2,1)S(1)} %get-tuple-element.35), channel_id=1, source_target_pairs={{0,16},{2,18},{4,20},{6,22},{8,24},{10,26},{12,28},{14,30},{16,0},... | collective-permute-start | bytes 344072 | tf_op jit(solution)/shard_map/ppermute | solution.py:31
  45.7 47.4 %collective-permute-start.20 = (bf16[1792,1184]{0,1:T(8,128)(2,1)}, bf16[1792,1184]{0,1:T(8,128)(2,1)}, u32[]{:S(2)}, u32[]{:S(2)}) collective-permute-start(bf16[1792,1184]{0,1:T(8,128)(2,1)} %param.15), channel_id=1, source_target_pairs={{0,1},{1,0},{2,3},{3,2},{4,5},{5,4},{6,7},{7,6},{8,9},{9,8},{10,11... | collective-permute-start | bytes 12730376 | tf_op jit(solution)/shard_map/ppermute | solution.py:36
  55.4 29.6 %copy-start.2 = (bf16[16,3584]{1,0:T(8,128)(2,1)}, bf16[16,3584]{1,0:T(8,128)(2,1)S(1)}, u32[]{:S(2)}) copy-start(bf16[16,3584]{1,0:T(8,128)(2,1)S(1)} %fusion.32) | copy-start | bytes 344068
  55.4 8.0 %collective-permute-start.11 = (bf16[16,3584]{1,0:T(8,128)(2,1)S(1)}, bf16[16,3584]{1,0:T(8,128)(2,1)S(1)}, u32[]{:S(2)}, u32[]{:S(2)}) collective-permute-start(bf16[16,3584]{1,0:T(8,128)(2,1)S(1)} %fusion.32), channel_id=1, source_target_pairs={{0,8},{2,10},{4,12},{6,14},{8,16},{10,18},{12,20},{14,22},{16,24},... | collective-permute-start | bytes 344072 | tf_op jit(solution)/shard_map/ppermute | solution.py:31
  55.4 11.4 %collective-permute-start.12 = (bf16[16,3584]{1,0:T(8,128)(2,1)S(1)}, bf16[16,3584]{1,0:T(8,128)(2,1)S(1)}, u32[]{:S(2)}, u32[]{:S(2)}) collective-permute-start(bf16[16,3584]{1,0:T(8,128)(2,1)S(1)} %fusion.32), channel_id=1, source_target_pairs={{0,16},{2,18},{4,20},{6,22},{8,24},{10,26},{12,28},{14,30},{16,0},... | collective-permute-start | bytes 344072 | tf_op jit(solution)/shard_map/ppermute | solution.py:31
  57.9 8.9 %collective-permute-start.13 = (bf16[16,3584]{1,0:T(8,128)(2,1)S(1)}, bf16[16,3584]{1,0:T(8,128)(2,1)S(1)}, u32[]{:S(2)}, u32[]{:S(2)}) collective-permute-start(bf16[16,3584]{1,0:T(8,128)(2,1)S(1)} %fusion.32), channel_id=1, source_target_pairs={{0,24},{2,26},{4,28},{6,30},{8,0},{10,2},{12,4},{14,6},{16,8},{18,... | collective-permute-start | bytes 344072 | tf_op jit(solution)/shard_map/ppermute | solution.py:31
  67.0 10.4 %collective-permute-start.14 = (bf16[4,16,3584]{2,1,0:T(8,128)(2,1)S(1)}, bf16[4,16,3584]{2,1,0:T(8,128)(2,1)S(1)}, u32[]{:S(2)}, u32[]{:S(2)}) collective-permute-start(bf16[4,16,3584]{2,1,0:T(8,128)(2,1)S(1)} %get-tuple-element.32), channel_id=1, source_target_pairs={{0,2},{2,0},{4,6},{6,4},{8,10},{10,8},{12,14},{14,12},{16,18},{18,... | collective-permute-start | bytes 1376264 | tf_op jit(solution)/shard_map/ppermute | solution.py:28
  67.6 10.6 %collective-permute-start.15 = (bf16[4,16,3584]{2,1,0:T(8,128)(2,1)S(1)}, bf16[4,16,3584]{2,1,0:T(8,128)(2,1)S(1)}, u32[]{:S(2)}, u32[]{:S(2)}) collective-permute-start(bf16[4,16,3584]{2,1,0:T(8,128)(2,1)S(1)} %get-tuple-element.32), channel_id=1, source_target_pairs={{0,4},{2,6},{4,0},{6,2},{8,12},{10,14},{12,8},{14,10},{16,20},{18,... | collective-permute-start | bytes 1376264 | tf_op jit(solution)/shard_map/ppermute | solution.py:28
  77.3 6.1 %collective-permute-start.16 = (bf16[4,16,1792]{2,1,0:T(8,128)(2,1)S(1)}, bf16[4,16,1792]{2,1,0:T(8,128)(2,1)S(1)}, u32[]{:S(2)}, u32[]{:S(2)}) collective-permute-start(bf16[4,16,1792]{2,1,0:T(8,128)(2,1)S(1)} %slice.187), channel_id=1, source_target_pairs={{0,4},{2,6},{4,0},{6,2},{8,12},{10,14},{12,8},{14,10},{16,20},{18,... | collective-permute-start | bytes 688136 | tf_op jit(solution)/shard_map/ppermute | solution.py:28
  78.2 6.5 %collective-permute-start.17 = (bf16[4,16,1792]{2,1,0:T(8,128)(2,1)S(1)}, bf16[4,16,1792]{2,1,0:T(8,128)(2,1)S(1)}, u32[]{:S(2)}, u32[]{:S(2)}) collective-permute-start(bf16[4,16,1792]{2,1,0:T(8,128)(2,1)S(1)} %slice.188), channel_id=1, source_target_pairs={{0,2},{2,0},{4,6},{6,4},{8,10},{10,8},{12,14},{14,12},{16,18},{18,... | collective-permute-start | bytes 688136 | tf_op jit(solution)/shard_map/ppermute | solution.py:28
  89.6 14.2 %collective-permute-start.18 = (bf16[256,1792]{1,0:T(8,128)(2,1)}, bf16[256,1792]{1,0:T(8,128)(2,1)}, u32[]{:S(2)}, u32[]{:S(2)}) collective-permute-start(bf16[256,1792]{1,0:T(8,128)(2,1)} %constant_dynamic-slice_fusion), channel_id=1, source_target_pairs={{0,1},{1,0},{2,3},{3,2},{4,5},{5,4},{6,7},{7,6},{8,9},{9,8},{10,11... | collective-permute-start | bytes 2752520 | tf_op jit(solution)/shard_map/ppermute | solution.py:36
  101.9 2.2 %collective-permute-start.19 = (bf16[256,1184]{0,1:T(8,128)(2,1)S(1)}, bf16[256,1184]{0,1:T(8,128)(2,1)S(1)}, u32[]{:S(2)}, u32[]{:S(2)}) collective-permute-start(bf16[256,1184]{0,1:T(8,128)(2,1)S(1)} %copy.41), channel_id=1, source_target_pairs={{0,1},{1,0},{2,3},{3,2},{4,5},{5,4},{6,7},{7,6},{8,9},{9,8},{10,11... | collective-permute-start | bytes 1818632 | tf_op jit(solution)/shard_map/ppermute | solution.py:36

commit v2 on v0

v2 whole, which is shorter than its diff:
```python
import functools

import jax
import jax.numpy as jnp
from jax import lax
from jax.experimental import pallas as pl
from jax.experimental.pallas import tpu as pltpu
from jax.sharding import PartitionSpec as P

ACTIVE = 8
LBLOCK = 128
QBLOCK = 2
PLANE = 4
LANES = 128
FF_BLOCK = 256
COLUMNS = 512

norm_epsilon = 1e-06


def packet_kernel(hidden, gain, blocks, codes, packet):
    width = hidden.shape[1]
    rows = hidden[...].astype(jnp.float32)
    scale = lax.rsqrt(jnp.mean(rows * rows, axis=1, keepdims=True) + norm_epsilon)
    packet[:, :width] = (rows * scale * gain[...]).astype(jnp.bfloat16)

    def ones(shape, hit):
        at = [lax.broadcasted_iota(jnp.int32, shape, d) for d in range(2)]
        return hit(*at).astype(jnp.bfloat16)

    def times(left, right):
        return jnp.dot(left, right, preferred_element_type=jnp.float32)

    block_of = ones((rows.shape[0], blocks.shape[0]), lambda r, c: r // QBLOCK == c)
    owners = times(block_of, blocks[...].astype(jnp.bfloat16)).astype(jnp.bfloat16)
    found = codes[...]
    high = (found // LBLOCK).astype(jnp.bfloat16)
    low = (found % LBLOCK).astype(jnp.bfloat16)
    marks = sum(
        times(values, ones((values.shape[1], LANES), lambda r, c, n=n: c == r + n * ACTIVE))
        for n, values in enumerate((owners, high, low))
    )
    packet[:, width:] = marks.astype(jnp.bfloat16)


def slopes(embed, marks, rows, owner, first_label):
    scores = lax.dot_general(
        embed, rows, (((1,), (1,)), ((), ())), preferred_element_type=jnp.float32
    )
    slot = sum(
        jnp.where(marks[:, k : k + 1] == owner, k + 1, 0) for k in range(ACTIVE)
    )
    codes = marks[:, ACTIVE : 2 * ACTIVE] * LBLOCK + marks[:, 2 * ACTIVE : 3 * ACTIVE]
    label = lax.broadcasted_iota(jnp.int32, scores.shape, 1) + first_label
    code = (slot - 1) * LBLOCK + label
    positive = codes[:, 0:1] == code
    for k in range(1, ACTIVE):
        positive |= codes[:, k : k + 1] == code
    target_sign = jnp.where(positive, 1.0, -1.0)
    margin = jnp.maximum(1.0 - target_sign * scores, 0.0)
    return jnp.where(slot > 0, -2.0 * target_sign * margin, 0.0).astype(jnp.bfloat16)


def unpack(packets, width):
    embed = jnp.concatenate([packet[:, :width] for packet in packets], axis=0)
    marks = jnp.concatenate([packet[:, width:] for packet in packets], axis=0)
    return embed, marks.astype(jnp.int32)


def near_kernel(place, own, near, across, *refs):
    packets, (total, embed_out, marks_out) = refs[:-3], refs[-3:]
    width = own.shape[1]
    embed, marks = unpack(packets, width)
    embed_out[...] = embed
    marks_out[...] = marks
    here, parity = place[0], place[1]
    fetched = ((own, here), (near, here ^ (1 + parity)), (across, here ^ (2 - parity)))
    found = [(slopes(embed, marks, rows[...], owner, 0), rows) for rows, owner in fetched]
    for start in range(0, width, COLUMNS):
        span = slice(start, min(start + COLUMNS, width))
        total[:, span] = sum(
            jnp.dot(slope, rows[:, span], preferred_element_type=jnp.float32)
            for slope, rows in found
        )


def far_kernel(place, far, across, total, embed, marks, parts):
    width = far.shape[1]
    share = far.shape[0]
    embed, marks = embed[...], marks[...]
    here, parity = place[0], place[1]
    found = [
        slopes(embed, marks, far[...], here ^ 3, parity * share),
        slopes(embed, marks, across[...], here ^ 3, (1 - parity) * share),
    ]
    for start in range(0, width, COLUMNS):
        span = slice(start, min(start + COLUMNS, width))
        added = total[:, span] + sum(
            jnp.dot(slope, rows[:, span], preferred_element_type=jnp.float32)
            for slope, rows in zip(found, (far, across))
        )
        parts[:, :, span] = added.astype(jnp.bfloat16).reshape(
            parts.shape[0], parts.shape[1], added.shape[1]
        )


def pieces(extent):
    return [(start, min(start + FF_BLOCK, extent)) for start in range(0, extent, FF_BLOCK)]


def part_of(ref, rows, begin, columns):
    if columns == ref.shape[1]:
        return ref.at[slice(*rows)]
    return ref.at[slice(*rows), begin : begin + columns]


def hidden_kernel(groups, begin, first, last, *refs):
    refs = list(refs)
    order = refs.pop(0) if last else None
    share = None if first else refs.pop(0)
    grads = refs.pop(0)
    weights, refs = refs[:groups], refs[groups:]
    if last:
        gate, up, gate_grad, up_grad = refs
    else:
        (out,) = refs
    columns = grads.shape[2]
    for start, stop in pieces(weights[0].shape[0]):
        hidden_grad = sum(
            lax.dot_general(
                grads[n],
                weights[n][start:stop, begin : begin + columns],
                (((1,), (1,)), ((), ())),
                preferred_element_type=jnp.float32,
            )
            for n in range(groups)
        )
        if not first:
            hidden_grad = hidden_grad + share[:, start:stop]
        if not last:
            out[:, start:stop] = hidden_grad
            continue
        rows = gate.shape[1]
        for i in range(gate.shape[0]):
            block = order[i]
            part = hidden_grad[i * rows : (i + 1) * rows]
            gate_full = gate[block, :, start:stop].astype(jnp.float32)
            up_full = up[block, :, start:stop].astype(jnp.float32)
            sigma = jax.nn.sigmoid(gate_full)
            up_grad[block, :, start:stop] = (part * gate_full * sigma).astype(jnp.bfloat16)
            gate_grad[block, :, start:stop] = (
                part * up_full * sigma * (1.0 + gate_full * (1.0 - sigma))
            ).astype(jnp.bfloat16)


def down_kernel(groups, begin, kept, *refs):
    acts, slabs, refs = refs[:groups], refs[groups : 2 * groups], refs[2 * groups :]
    held, sems = refs[-2:]
    columns = slabs[0].shape[1]
    copies = []
    if kept:
        down_grad = refs[kept]
        for n in range(kept):
            copies.append(
                pltpu.make_async_copy(refs[n], refs[kept + 1 + n], sems.at[sems.shape[0] - 1 - n])
            )
            copies[-1].start()
    else:
        down_grad = refs[-3]
    for i, (start, stop) in enumerate(pieces(held.shape[0])):
        held[start:stop] = sum(
            jnp.dot(act[start:stop], slab[...], preferred_element_type=jnp.float32)
            for act, slab in zip(acts, slabs)
        )
        copies.append(
            pltpu.make_async_copy(
                held.at[start:stop],
                part_of(down_grad, (start, stop), begin, columns),
                sems.at[i],
            )
        )
        copies[-1].start()
    for copy in copies:
        copy.wait()


def params(megabytes):
    return pltpu.CompilerParams(vmem_limit_bytes=megabytes * 2**20)


def shards(
    final_hidden, norm_gain, label_weights, active_blocks, positives, gate_pre, up_pre, down_weight
):
    owners = lax.axis_size("label")
    groups = lax.axis_size("fsdp")
    depth = owners // PLANE
    here = lax.axis_index("label")
    core = lax.axis_index("fsdp")
    parity = core % 2
    label_rows = label_weights[0]
    block_labels, width = label_rows.shape
    share = block_labels // 2
    smem = pl.BlockSpec(memory_space=pltpu.SMEM)
    vmem = pl.BlockSpec(memory_space=pltpu.VMEM)
    anywhere = pl.BlockSpec(memory_space=pl.ANY)

    def swap(array, even, odd):
        pairs = [
            (i * groups + f, (i ^ (odd if f % 2 else even)) * groups + f)
            for i in range(owners)
            for f in range(groups)
        ]
        return lax.ppermute(array, ("label", "fsdp"), pairs)

    def mate(array):
        return lax.ppermute(array, "fsdp", [(f, f ^ 1) for f in range(groups)])

    def between(array, step):
        return lax.ppermute(array, "fsdp", [(i, (i + step) % groups) for i in range(groups)])

    near = swap(label_rows, 1, 2)
    near_mate = mate(near)
    far = swap(jnp.where(parity == 0, near[:share], near[share:]), 2, 1)

    query_count = final_hidden.shape[1]
    packet = pl.pallas_call(
        packet_kernel,
        out_shape=jax.ShapeDtypeStruct((query_count, width + LANES), jnp.bfloat16),
        in_specs=[vmem] * 4,
        out_specs=vmem,
        compiler_params=params(16),
    )(final_hidden[0], norm_gain[None], active_blocks[0], positives[0])
    packets = [packet] + [swap(packet, PLANE * s, PLANE * s) for s in range(1, depth)]

    plane_masks = jnp.stack([0 * parity, 1 + parity, 2 - parity, 0 * parity + 3])
    order = here ^ (
        plane_masks[:, None] + PLANE * jnp.arange(depth, dtype=jnp.int32)[None, :]
    ).reshape(owners)
    order = order.astype(jnp.int32)
    gate_full = gate_pre.astype(jnp.float32)
    sigma = jax.nn.sigmoid(gate_full)
    hidden_act = (gate_full * sigma * up_pre.astype(jnp.float32)).astype(jnp.bfloat16)
    group_rows = owners * query_count
    ff_local = gate_pre.shape[2]
    act = jnp.take(hidden_act, order, axis=0).reshape(group_rows, ff_local).T
    weights = [down_weight.T] + [between(down_weight, n).T for n in range(1, groups)]

    place = jnp.stack([here, parity]).astype(jnp.int32)
    line_rows = depth * query_count
    total, embed, marks = pl.pallas_call(
        near_kernel,
        out_shape=[
            jax.ShapeDtypeStruct((line_rows, width), jnp.float32),
            jax.ShapeDtypeStruct((line_rows, width), jnp.bfloat16),
            jax.ShapeDtypeStruct((line_rows, LANES), jnp.int32),
        ],
        in_specs=[smem] + [vmem] * (3 + depth),
        out_specs=[vmem] * 3,
        compiler_params=params(24),
        cost_estimate=pl.CostEstimate(
            flops=12 * line_rows * block_labels * width,
            bytes_accessed=6 * block_labels * width,
            transcendentals=0,
        ),
    )(place, label_rows, near, near_mate, *packets)
    far_mate = mate(far)
    parts = pl.pallas_call(
        far_kernel,
        out_shape=jax.ShapeDtypeStruct((depth, query_count, width), jnp.bfloat16),
        in_specs=[smem] + [vmem] * 5,
        out_specs=vmem,
        compiler_params=params(24),
    )(place, far, far_mate, total, embed, marks)
    embed_grad = parts[0].astype(jnp.float32)
    for s in range(1, depth):
        embed_grad += swap(parts[s], PLANE * s, PLANE * s).astype(jnp.float32)

    embed_grad, act = lax.optimization_barrier((embed_grad, act))
    acts = [act] + [between(act, n) for n in range(1, groups)]
    hidden_rows = final_hidden[0].astype(jnp.float32)
    inverse_rms = lax.rsqrt(
        jnp.mean(hidden_rows * hidden_rows, axis=1, keepdims=True) + norm_epsilon
    )
    normed = hidden_rows * inverse_rms
    scaled = norm_gain * embed_grad
    resid = inverse_rms * (scaled - normed * jnp.mean(normed * scaled, axis=1, keepdims=True))
    resid_bf = resid.astype(jnp.bfloat16)

    slab = width // groups
    cuts = [0, slab // 2, slab] if slab % (2 * LANES) == 0 else [0, slab]
    own = jnp.stack(
        [
            lax.dynamic_slice_in_dim(resid_bf, ((core - n) % groups) * slab, slab, 1)
            for n in range(groups)
        ]
    )
    lines = [
        [own[..., begin:end]]
        + [swap(own[..., begin:end], PLANE * s, PLANE * s) for s in range(1, depth)]
        for begin, end in zip(cuts, cuts[1:])
    ]

    def hidden(part, begin, share, final, weights):
        columns = part.shape[2]
        shapes = [jax.ShapeDtypeStruct((group_rows, ff_local), jnp.float32)]
        operands, smems = [part, *weights], 0
        if share is not None:
            operands = [share] + operands
        if final:
            shapes = [jax.ShapeDtypeStruct(gate_pre.shape, jnp.bfloat16)] * 2
            operands, smems = [order] + operands + [gate_pre, up_pre], 1
        return pl.pallas_call(
            functools.partial(hidden_kernel, groups, begin, share is None, final),
            out_shape=shapes,
            in_specs=[smem] * smems + [vmem] * (len(operands) - smems),
            out_specs=[vmem] * len(shapes),
            compiler_params=params(16),
            cost_estimate=matmul_cost(columns, 2 * ff_local * columns * groups),
        )(*operands)

    def matmul_cost(columns, more):
        return pl.CostEstimate(
            flops=2 * groups * group_rows * columns * ff_local,
            bytes_accessed=more,
            transcendentals=0,
        )

    def down(part, begin, so_far, kept):
        columns = part.shape[2]
        slabs = [part[0]] + [between(part[groups - n], n) for n in range(1, groups)]
        outs = pl.pallas_call(
            functools.partial(down_kernel, groups, begin, len(kept)),
            out_shape=[jax.ShapeDtypeStruct((ff_local, slab), jnp.float32)]
            + [jax.ShapeDtypeStruct(array.shape, array.dtype) for array in kept],
            in_specs=[vmem] * (2 * groups) + [anywhere] * (len(so_far) + len(kept)),
            out_specs=[anywhere] + [vmem] * len(kept),
            scratch_shapes=[
                pltpu.VMEM((ff_local, columns), jnp.float32),
                pltpu.SemaphoreType.DMA((len(pieces(ff_local)) + len(kept),)),
            ],
            input_output_aliases={2 * groups: 0} if so_far else {},
            compiler_params=params(24),
            cost_estimate=matmul_cost(columns, 4 * ff_local * columns),
        )(*acts, *slabs, *so_far, *kept)
        return list(outs[:1]), list(outs[1:])

    def begin_plane(line):
        line = jnp.concatenate(line, axis=1)
        return line, swap(line, 1, 2), swap(line, 2, 1)

    share, so_far = None, []
    line, first, second = begin_plane(lines[0])
    for k, (begin, end) in enumerate(zip(cuts, cuts[1:])):
        final = k == len(lines) - 1
        if not final:
            first, lines[k + 1] = lax.optimization_barrier((first, lines[k + 1]))
        third = swap(first, 2, 1)
        if not final:
            ahead = begin_plane(lines[k + 1])
            third, ahead = lax.optimization_barrier((third, ahead))
        elif so_far:
            third, share, so_far = lax.optimization_barrier((third, share, so_far))
        part = jnp.concatenate([line, first, second, third], axis=1)
        if final:
            gate_grad, up_grad = hidden(part, begin, share, final, weights)
            so_far, _ = down(part, begin, so_far, [])
        else:
            so_far, kept = down(part, begin, so_far, weights[1:])
            weights = weights[:1] + kept
            (share,) = hidden(part, begin, share, final, weights)
            line, first, second = ahead
    return (resid_bf[None], so_far[0].T, gate_grad, up_grad)


def solution(mesh):
    placed = (
        P("label", "fsdp", None),
        P(),
        P("label", None, None),
        P("label", "fsdp", None),
        P("label", "fsdp", None),
        P(None, "fsdp", "label"),
        P(None, "fsdp", "label"),
        P("fsdp", "label"),
    )
    return jax.shard_map(
        shards,
        mesh=mesh,
        in_specs=placed,
        out_specs=(
            P("label", "fsdp", None),
            P("fsdp", "label"),
            P(None, "fsdp", "label"),
            P(None, "fsdp", "label"),
        ),
        check_vma=False,
    )
```

time: 221 us -> 89.9 us (0.41)
  waiting for transfers between devices: 117 us -> 28.1 us
  blocking collectives: 39.3 us -> 0 us
  starting transfers between devices: 12.6 us -> 33.9 us
  matrix products: 19 us -> 0 us
  Pallas kernels: 0 us -> 16.2 us
  between operations: 13.9 us -> 1.03 us
  other arithmetic: 9.14 us -> 3.7 us
  local copies, waits for them, and re-layouts: 9.76 us -> 6.62 us
    all_gather x2 -> x0, waiting for transfers between devices: 69.7 us -> none  [the longest x1 56.3 us: shards(): lax.all_gather(resid_bf[None], 'label', axis=0, tiled=True)]
    all_to_all x1 -> x0, blocking collectives: 39.3 us -> none  [shards(): lax.all_to_all(partial_grad, 'label', split_axis=0, concat_axis=0, tiled=...]
    ppermute x0 -> x26, starting transfers between devices: none -> 33.9 us  [the longest x20 33.1 us: swap(): return lax.ppermute(array, ('label', 'fsdp'), pairs)]
    all_to_all x2 -> x0, waiting for transfers between devices: 32.6 us -> none  [the longest x1 29.9 us: shards(): lax.all_to_all(send_rows, 'label', split_axis=0, concat_axis=0, tiled=True)]
    ppermute x0 -> x26, waiting for transfers between devices: none -> 28.1 us  [the longest x20 28.1 us: swap(): return lax.ppermute(array, ('label', 'fsdp'), pairs)]
    dot_general x6 -> x0, matrix products: 19 us -> none  [the longest x1 7.75 us: shards(): lax.dot_general(columns, hidden_act, (((0,), (0,)), ((), ())), preferred_...]
    pallas_call x0 -> x7, Pallas kernels: none -> 16.2 us  [the longest x2 5.36 us: down(): pl.pallas_call(functools.partial(down_kernel, groups, begin, len(kept)),...]
    reduce_scatter x1 -> x0, waiting for transfers between devices: 13.6 us -> none  [shards(): lax.psum_scatter(lax.dot_general(columns, hidden_act, (((0,), (0,)), ((),...]
  transfers between devices with their start and end apart: 5 -> 26, of which waited for: 5 -> 10; matrix products, arithmetic and copies ran while one was open for 9% -> 8% of each run, Pallas kernels for 0% -> 15%
where the time goes in v2:
time: 89.9 us; the launch traced here: 89.5 us
  starting transfers between devices  33.9 us (38%)
  waiting for transfers between devices  28.1 us (31%)
  Pallas kernels  16.2 us (18%)
  local copies, waits for them, and re-layouts  6.62 us (7%)
  other arithmetic  3.7 us (4%)
  between operations  1.03 us (1%)
    ppermute x20, starting transfers between devices, swap(): return lax.ppermute(array, ('label', 'fsdp'), pairs)  33.1 us
    ppermute x20, waiting for transfers between devices, swap(): return lax.ppermute(array, ('label', 'fsdp'), pairs)  28.1 us
    pallas_call x2, Pallas kernels, down(): pl.pallas_call(functools.partial(down_kernel, groups, begin, len(kept)),...  5.36 us
    pallas_call x2, Pallas kernels, hidden(): pl.pallas_call(functools.partial(hidden_kernel, groups, begin, share is N...  4.96 us
    pallas_call x1, Pallas kernels, shards(): pl.pallas_call(near_kernel, out_shape=[jax.ShapeDtypeStruct((line_rows, w...  3.04 us
    unnamed x31, local copies, waits for them, and re-layouts  2.88 us
    pallas_call x1, Pallas kernels, shards(): pl.pallas_call(far_kernel, out_shape=jax.ShapeDtypeStruct((depth, query_c...  1.92 us
  transfers between devices with their start and end apart: 26, of which 10 were waited for; matrix products, arithmetic and copies ran while one was open for 8% of the time, Pallas kernels for 15%

profile of v2, /device:TPU:0, one launch (start us, length us, event | category | flops | bytes accessed | tf_op | source)
XLA Modules:
  0.0 89.5 jit_solution(10095740555258356319)
XLA Ops:
  0.6 3.0 %collective-permute-start = (bf16[128,3584]{1,0:T(8,128)(2,1)}, bf16[128,3584]{1,0:T(8,128)(2,1)S(1)}, u32[]{:S(2)}, u32[]{:S(2)}) collective-permute-start(bf16[128,3584]{1,0:T(8,128)(2,1)} %bitcast.49), channel_id=1, source_target_pairs={{0,2},{1,5},{2,0},{3,7},{4,6},{5,1},{6,4},{7,3},{8,10},{9,13},{10,... | collective-permute-start | bytes 2752520 | tf_op jit(solution)/shard_map/ppermute | solution.py:213
  3.6 0.7 broadcast_in_dim.25.gain
  4.4 0.8 copy.15.codes
  5.1 0.9 %copy-done.2 = bf16[1,16,3584]{2,1,0:T(8,128)(2,1)S(1)} copy-done((bf16[1,16,3584]{2,1,0:T(8,128)(2,1)S(1)}, bf16[1,16,3584]{2,1,0:T(8,128)(2,1)}, u32[]{:S(2)}) %copy-start.2) | copy-done | bytes 114712
  6.0 0.7 copy-done.5
  6.7 0.9 shard_map.111.refs_0_
  7.6 1.6 %collective-permute-start.4 = (bf16[16,3712]{1,0:T(8,128)(2,1)}, bf16[16,3712]{1,0:T(8,128)(2,1)}, u32[]{:S(2)}, u32[]{:S(2)}) collective-permute-start(bf16[16,3712]{1,0:T(8,128)(2,1)} %shard_map.111.refs_0_), channel_id=1, source_target_pairs={{0,8},{1,9},{2,10},{3,11},{4,12},{5,13},{6,14},{7,15},{8,0},{9,1},... | collective-permute-start | bytes 356360 | tf_op jit(solution)/shard_map/ppermute | solution.py:213
  9.2 2.6 %collective-permute-start.5 = (bf16[16,3712]{1,0:T(8,128)(2,1)}, bf16[16,3712]{1,0:T(8,128)(2,1)}, u32[]{:S(2)}, u32[]{:S(2)}) collective-permute-start(bf16[16,3712]{1,0:T(8,128)(2,1)} %shard_map.111.refs_0_), channel_id=1, source_target_pairs={{0,16},{1,17},{2,18},{3,19},{4,20},{5,21},{6,22},{7,23},{8,24},{9,... | collective-permute-start | bytes 356360 | tf_op jit(solution)/shard_map/ppermute | solution.py:213
  11.8 0.2 collective-permute-start.6
  12.0 0.1 pad_add_fusion.1
  12.1 0.1 add_xor_fusion
  12.1 0.1 xor.13
  12.2 0.1 xor.12.refs_0_
  12.3 1.7 %fusion.4 = bf16[16,16,1184]{2,1,0:T(8,128)(2,1)S(1)} fusion(bf16[16,16,1184]{2,1,0:T(8,128)(2,1)} %refs_6_.1, bf16[16,16,1184]{2,1,0:T(8,128)(2,1)} %refs_5_.1), kind=kLoop, calls=%fused_computation.7 | loop fusion | flops 2424832 | bytes 1818624 | tf_op jit(solution)/shard_map/convert_element_type | solution.py:242
  14.0 1.2 %collective-permute-done.near = bf16[128,3584]{1,0:T(8,128)(2,1)S(1)} collective-permute-done((bf16[128,3584]{1,0:T(8,128)(2,1)}, bf16[128,3584]{1,0:T(8,128)(2,1)S(1)}, u32[]{:S(2)}, u32[]{:S(2)}) %collective-permute-start) | collective-permute-done | bytes 917536 | tf_op jit(solution)/shard_map/ppermute | solution.py:213
  15.3 2.1 %collective-permute-start.1 = (bf16[64,3584]{1,0:T(8,128)(2,1)S(1)}, bf16[64,3584]{1,0:T(8,128)(2,1)}, u32[]{:S(2)}, u32[]{:S(2)}) collective-permute-start(bf16[64,3584]{1,0:T(8,128)(2,1)S(1)} %slice_select_fusion), channel_id=1, source_target_pairs={{0,4},{1,3},{2,6},{3,1},{4,0},{5,7},{6,2},{7,5},{8,12},{9,11},{10,... | collective-permute-start | bytes 1376264 | tf_op jit(solution)/shard_map/ppermute | solution.py:213
  17.4 0.6 gather_fusion
  18.0 1.1 %copy.16 = bf16[256,1184]{0,1:T(8,128)(2,1)} copy(bf16[256,1184]{1,0:T(8,128)(2,1)S(1)} %bitcast.53) | data formatting | bytes 1212416 | tf_op jit(solution)/shard_map/jit(_take)/gather | solution.py:245
  19.1 0.1 broadcast_in_dim.26
  19.2 0.1 broadcast_in_dim.27
  19.3 4.7 %collective-permute-done.1.far = bf16[64,3584]{1,0:T(8,128)(2,1)} collective-permute-done((bf16[64,3584]{1,0:T(8,128)(2,1)S(1)}, bf16[64,3584]{1,0:T(8,128)(2,1)}, u32[]{:S(2)}, u32[]{:S(2)}) %collective-permute-start.1) | collective-permute-done | bytes 458784 | tf_op jit(solution)/shard_map/ppermute | solution.py:213
  24.0 1.1 %select_bitcast_fusion.refs_0_ = bf16[1184,256]{1,0:T(8,128)(2,1)S(1)} fusion(bf16[256,1184]{0,1:T(8,128)(2,1)} %copy.16, pred[256]{0:T(512)(128)(4,1)S(1)} %broadcast_in_dim.27), kind=kLoop, calls=%fused_computation.8 | loop fusion | flops 303104 | bytes 1212672 | tf_op jit(solution)/shard_map/transpose | solution.py:245
  25.1 0.1 pad_add_fusion.place
  25.2 0.1 fusion.11
  25.3 0.6 collective-permute-start.24
  25.9 3.0 %shard_map.112 = (f32[64,3584]{1,0:T(8,128)S(1)}, bf16[64,3584]{1,0:T(8,128)(2,1)S(1)}, s32[64,128]{1,0:T(8,128)S(1)}) custom-call(s32[2]{0:T(128)S(1)} %pad_add_fusion.place, bf16[128,3584]{1,0:T(8,128)(2,1)S(1)} %bitcast.50, bf16[128,3584]{1,0:T(8,128)(2,1)S(1)} %collective-permute-done.near, bf16[128,3584]{1,0:T(8,128)(2,1)S(1)} %collective-permute-done.3.across, ...), custom_call_target="tpu_custom_call" | custom-call | flops 352321536 | bytes 2752512 | tf_op jit(solution)/shard_map/pallas_call | solution.py:250
  29.0 1.9 %shard_map.113 = bf16[4,16,3584]{2,1,0:T(8,128)(2,1)S(1)} custom-call(s32[2]{0:T(128)S(1)} %pad_add_fusion.place, bf16[64,3584]{1,0:T(8,128)(2,1)} %collective-permute-done.1.far, bf16[64,3584]{1,0:T(8,128)(2,1)} %collective-permute-done.2.across, f32[64,3584]{1,0:T(8,128)S(1)} %get-tuple-element.25.total, bf16[64,3584]{1,0:T(8,128)(2,1)S(1)} %get-tuple-element.26.embed, ...), custom_call_target="tpu_custom_call" | custom-call | tf_op jit(solution)/shard_map/pallas_call | solution.py:267
  31.0 2.1 %collective-permute-start.7 = (bf16[16,3584]{1,0:T(8,128)(2,1)S(1)}, bf16[16,3584]{1,0:T(8,128)(2,1)S(1)}, u32[]{:S(2)}, u32[]{:S(2)}) collective-permute-start(bf16[16,3584]{1,0:T(8,128)(2,1)S(1)} %get-tuple-element.52), channel_id=1, source_target_pairs={{0,8},{1,9},{2,10},{3,11},{4,12},{5,13},{6,14},{7,15},{8,0},{9,1},... | collective-permute-start | bytes 344072 | tf_op jit(solution)/shard_map/ppermute | solution.py:213
  33.1 2.6 %collective-permute-start.8 = (bf16[16,3584]{1,0:T(8,128)(2,1)S(1)}, bf16[16,3584]{1,0:T(8,128)(2,1)S(1)}, u32[]{:S(2)}, u32[]{:S(2)}) collective-permute-start(bf16[16,3584]{1,0:T(8,128)(2,1)S(1)} %get-tuple-element.54), channel_id=1, source_target_pairs={{0,16},{1,17},{2,18},{3,19},{4,20},{5,21},{6,22},{7,23},{8,24},{9,... | collective-permute-start | bytes 344072 | tf_op jit(solution)/shard_map/ppermute | solution.py:213
  35.7 0.8 collective-permute-done.7
  36.5 8.5 %collective-permute-done.8 = bf16[16,3584]{1,0:T(8,128)(2,1)S(1)} collective-permute-done((bf16[16,3584]{1,0:T(8,128)(2,1)S(1)}, bf16[16,3584]{1,0:T(8,128)(2,1)S(1)}, u32[]{:S(2)}, u32[]{:S(2)}) %collective-permute-start.8) | collective-permute-done | bytes 114720 | tf_op jit(solution)/shard_map/ppermute | solution.py:213
  45.0 0.1 fusion.13
  45.1 0.2 fusion.7
  45.3 0.1 fusion.10
  45.5 1.9 %collective-permute-start.11 = (bf16[2,16,896]{2,1,0:T(8,128)(2,1)S(1)}, bf16[2,16,896]{2,1,0:T(8,128)(2,1)S(1)}, u32[]{:S(2)}, u32[]{:S(2)}) collective-permute-start(bf16[2,16,896]{2,1,0:T(8,128)(2,1)S(1)} %get-tuple-element.47), channel_id=1, source_target_pairs={{0,8},{1,9},{2,10},{3,11},{4,12},{5,13},{6,14},{7,15},{8,0},{9,1},... | collective-permute-start | bytes 172040 | tf_op jit(solution)/shard_map/ppermute | solution.py:213
  47.4 1.1 %collective-permute-start.12 = (bf16[2,16,896]{2,1,0:T(8,128)(2,1)S(1)}, bf16[2,16,896]{2,1,0:T(8,128)(2,1)S(1)}, u32[]{:S(2)}, u32[]{:S(2)}) collective-permute-start(bf16[2,16,896]{2,1,0:T(8,128)(2,1)S(1)} %get-tuple-element.47), channel_id=1, source_target_pairs={{0,16},{1,17},{2,18},{3,19},{4,20},{5,21},{6,22},{7,23},{8,24},{9,... | collective-permute-start | bytes 172040 | tf_op jit(solution)/shard_map/ppermute | solution.py:213
  48.5 1.4 %collective-permute-start.13 = (bf16[2,16,896]{2,1,0:T(8,128)(2,1)S(1)}, bf16[2,16,896]{2,1,0:T(8,128)(2,1)S(1)}, u32[]{:S(2)}, u32[]{:S(2)}) collective-permute-start(bf16[2,16,896]{2,1,0:T(8,128)(2,1)S(1)} %get-tuple-element.47), channel_id=1, source_target_pairs={{0,24},{1,25},{2,26},{3,27},{4,28},{5,29},{6,30},{7,31},{8,16},{9,... | collective-permute-start | bytes 172040 | tf_op jit(solution)/shard_map/ppermute | solution.py:213
  49.9 0.9 %collective-permute-start.15 = (bf16[2,16,896]{2,1,0:T(8,128)(2,1)S(1)}, bf16[2,16,896]{2,1,0:T(8,128)(2,1)S(1)}, u32[]{:S(2)}, u32[]{:S(2)}) collective-permute-start(bf16[2,16,896]{2,1,0:T(8,128)(2,1)S(1)} %get-tuple-element.31), channel_id=1, source_target_pairs={{0,8},{1,9},{2,10},{3,11},{4,12},{5,13},{6,14},{7,15},{8,0},{9,1},... | collective-permute-start | bytes 172040 | tf_op jit(solution)/shard_map/ppermute | solution.py:213
  50.8 2.1 %collective-permute-start.16 = (bf16[2,16,896]{2,1,0:T(8,128)(2,1)S(1)}, bf16[2,16,896]{2,1,0:T(8,128)(2,1)S(1)}, u32[]{:S(2)}, u32[]{:S(2)}) collective-permute-start(bf16[2,16,896]{2,1,0:T(8,128)(2,1)S(1)} %get-tuple-element.31), channel_id=1, source_target_pairs={{0,16},{1,17},{2,18},{3,19},{4,20},{5,21},{6,22},{7,23},{8,24},{9,... | collective-permute-start | bytes 172040 | tf_op jit(solution)/shard_map/ppermute | solution.py:213
  53.0 2.3 %collective-permute-done.12 = bf16[2,16,896]{2,1,0:T(8,128)(2,1)S(1)} collective-permute-done((bf16[2,16,896]{2,1,0:T(8,128)(2,1)S(1)}, bf16[2,16,896]{2,1,0:T(8,128)(2,1)S(1)}, u32[]{:S(2)}, u32[]{:S(2)}) %collective-permute-start.12) | collective-permute-done | bytes 57376 | tf_op jit(solution)/shard_map/ppermute | solution.py:213
  55.3 2.0 %collective-permute-start.17 = (bf16[2,16,896]{2,1,0:T(8,128)(2,1)S(1)}, bf16[2,16,896]{2,1,0:T(8,128)(2,1)S(1)}, u32[]{:S(2)}, u32[]{:S(2)}) collective-permute-start(bf16[2,16,896]{2,1,0:T(8,128)(2,1)S(1)} %get-tuple-element.31), channel_id=1, source_target_pairs={{0,24},{1,25},{2,26},{3,27},{4,28},{5,29},{6,30},{7,31},{8,16},{9,... | collective-permute-start | bytes 172040 | tf_op jit(solution)/shard_map/ppermute | solution.py:213
  57.3 1.6 %collective-permute-start.14 = (bf16[2,64,896]{2,1,0:T(8,128)(2,1)S(1)}, bf16[2,64,896]{2,1,0:T(8,128)(2,1)S(1)}, u32[]{:S(2)}, u32[]{:S(2)}) collective-permute-start(bf16[2,64,896]{2,1,0:T(8,128)(2,1)S(1)} %pad_maximum_fusion), channel_id=1, source_target_pairs={{0,2},{1,5},{2,0},{3,7},{4,6},{5,1},{6,4},{7,3},{8,10},{9,13},{10,... | collective-permute-start | bytes 688136 | tf_op jit(solution)/shard_map/ppermute | solution.py:213
  58.9 1.6 %collective-permute-start.22 = (bf16[2,64,896]{2,1,0:T(8,128)(2,1)S(1)}, bf16[2,64,896]{2,1,0:T(8,128)(2,1)S(1)}, u32[]{:S(2)}, u32[]{:S(2)}) collective-permute-start(bf16[2,64,896]{2,1,0:T(8,128)(2,1)S(1)} %pad_maximum_fusion), channel_id=1, source_target_pairs={{0,4},{1,3},{2,6},{3,1},{4,0},{5,7},{6,2},{7,5},{8,12},{9,11},{10,... | collective-permute-start | bytes 688136 | tf_op jit(solution)/shard_map/ppermute | solution.py:213
  60.5 0.8 collective-permute-done.17
  61.3 3.6 %collective-permute-done.14 = bf16[2,64,896]{2,1,0:T(8,128)(2,1)S(1)} collective-permute-done((bf16[2,64,896]{2,1,0:T(8,128)(2,1)S(1)}, bf16[2,64,896]{2,1,0:T(8,128)(2,1)S(1)}, u32[]{:S(2)}, u32[]{:S(2)}) %collective-permute-start.14) | collective-permute-done | bytes 229408 | tf_op jit(solution)/shard_map/ppermute | solution.py:213
  64.9 1.6 %collective-permute-start.19 = (bf16[2,64,896]{2,1,0:T(8,128)(2,1)S(1)}, bf16[2,64,896]{2,1,0:T(8,128)(2,1)S(1)}, u32[]{:S(2)}, u32[]{:S(2)}) collective-permute-start(bf16[2,64,896]{2,1,0:T(8,128)(2,1)S(1)} %constant_dynamic-update-slice_fusion), channel_id=1, source_target_pairs={{0,2},{1,5},{2,0},{3,7},{4,6},{5,1},{6,4},{7,3},{8,10},{9,13},{10,... | collective-permute-start | bytes 688136 | tf_op jit(solution)/shard_map/ppermute | solution.py:213
  66.4 2.5 %collective-permute-start.20 = (bf16[2,64,896]{2,1,0:T(8,128)(2,1)S(1)}, bf16[2,64,896]{2,1,0:T(8,128)(2,1)S(1)}, u32[]{:S(2)}, u32[]{:S(2)}) collective-permute-start(bf16[2,64,896]{2,1,0:T(8,128)(2,1)S(1)} %constant_dynamic-update-slice_fusion), channel_id=1, source_target_pairs={{0,4},{1,3},{2,6},{3,1},{4,0},{5,7},{6,2},{7,5},{8,12},{9,11},{10,... | collective-permute-start | bytes 688136 | tf_op jit(solution)/shard_map/ppermute | solution.py:213
  69.0 0.0 collective-permute-start.18
  69.0 0.1 collective-permute-start.10
  69.2 1.8 %collective-permute-done.19 = bf16[2,64,896]{2,1,0:T(8,128)(2,1)S(1)} collective-permute-done((bf16[2,64,896]{2,1,0:T(8,128)(2,1)S(1)}, bf16[2,64,896]{2,1,0:T(8,128)(2,1)S(1)}, u32[]{:S(2)}, u32[]{:S(2)}) %collective-permute-start.19) | collective-permute-done | bytes 229408 | tf_op jit(solution)/shard_map/ppermute | solution.py:213
  71.0 2.0 %collective-permute-done.20 = bf16[2,64,896]{2,1,0:T(8,128)(2,1)S(1)} collective-permute-done((bf16[2,64,896]{2,1,0:T(8,128)(2,1)S(1)}, bf16[2,64,896]{2,1,0:T(8,128)(2,1)S(1)}, u32[]{:S(2)}, u32[]{:S(2)}) %collective-permute-start.20) | collective-permute-done | bytes 229408 | tf_op jit(solution)/shard_map/ppermute | solution.py:213
  73.0 2.5 %collective-permute-done.18 = bf16[2,64,896]{2,1,0:T(8,128)(2,1)S(1)} collective-permute-done((bf16[2,64,896]{2,1,0:T(8,128)(2,1)S(1)}, bf16[2,64,896]{2,1,0:T(8,128)(2,1)S(1)}, u32[]{:S(2)}, u32[]{:S(2)}) %collective-permute-start.18) | collective-permute-done | bytes 229408 | tf_op jit(solution)/shard_map/ppermute | solution.py:213
  75.4 0.1 slice_bitcast_fusion.2
  75.5 0.0 slice-start.1
  75.5 0.1 collective-permute-start.23
  75.6 2.1 %collective-permute-start.21 = (bf16[2,64,896]{2,1,0:T(8,128)(2,1)S(1)}, bf16[2,64,896]{2,1,0:T(8,128)(2,1)S(1)}, u32[]{:S(2)}, u32[]{:S(2)}) collective-permute-start(bf16[2,64,896]{2,1,0:T(8,128)(2,1)S(1)} %collective-permute-done.19), channel_id=1, source_target_pairs={{0,4},{1,3},{2,6},{3,1},{4,0},{5,7},{6,2},{7,5},{8,12},{9,11},{10,... | collective-permute-start | bytes 688136 | tf_op jit(solution)/shard_map/ppermute | solution.py:213
  77.8 2.9 %shard_map.114 = (f32[1184,1792]{1,0:T(8,128)}, bf16[1184,1792]{1,0:T(8,128)(2,1)S(1)}) custom-call(bf16[1184,256]{1,0:T(8,128)(2,1)S(1)} %select_bitcast_fusion.refs_0_, bf16[1184,256]{1,0:T(8,128)(2,1)S(1)} %collective-permute-done.10.refs_1_, bf16[256,896]{1,0:T(8,128)(2,1)S(1)} %get-tuple-element.51.refs_2_, ...), custom_call_target="tpu_custom_call" | custom-call | flops 1086324736 | bytes 4243456 | tf_op jit(solution)/shard_map/pallas_call | solution.py:331
  80.7 1.5 %shard_map.115.refs_1_ = f32[256,1184]{1,0:T(8,128)S(1)} custom-call(bf16[2,256,896]{2,1,0:T(8,128)(2,1)S(1)} %constant_dynamic-update-slice_fusion.4.refs_0_, bf16[1184,1792]{1,0:T(8,128)(2,1)S(1)} %bitcast.45, bf16[1184,1792]{1,0:T(8,128)(2,1)S(1)} %get-tuple-element.39.refs_2_.refs_4_), custom_call_target="tpu_custom_call" | custom-call | flops 1086324736 | bytes 4243456 | tf_op jit(solution)/shard_map/pallas_call | solution.py:312
  82.3 0.1 slice_bitcast_fusion
  82.4 0.1 collective-permute-start.25
  82.5 0.9 copy-done
  83.3 0.2 copy-done.1
  83.5 3.4 %shard_map.117 = (bf16[16,16,1184]{2,1,0:T(8,128)(2,1)}, bf16[16,16,1184]{2,1,0:T(8,128)(2,1)}) custom-call(s32[16]{0:T(128)S(1)} %xor.12.refs_0_, f32[256,1184]{1,0:T(8,128)S(1)} %shard_map.115.refs_1_, bf16[2,256,896]{2,1,0:T(8,128)(2,1)S(1)} %constant_dynamic-update-slice_fusion.11.refs_2_, bf16[1184,1792]{1,0:T(8,128)(2,1)S(1)} %bitcast.46, ...), custom_call_target="tpu_custom_call" | custom-call | flops 1086324736 | bytes 4243456 | tf_op jit(solution)/shard_map/pallas_call | solution.py:312
  87.0 2.5 %shard_map.116 = f32[1184,1792]{1,0:T(8,128)} custom-call(bf16[1184,256]{1,0:T(8,128)(2,1)S(1)} %select_bitcast_fusion.refs_0_, bf16[1184,256]{1,0:T(8,128)(2,1)S(1)} %collective-permute-done.10.refs_1_, bf16[256,896]{1,0:T(8,128)(2,1)S(1)} %get-tuple-element.49.refs_2_, ...), custom_call_target="tpu_custom_call", output_to_operand_aliasing={{}: (4, {})} | custom-call | flops 1086324736 | bytes 4243456 | tf_op jit(solution)/shard_map/pallas_call | solution.py:331
  (59 shorter events, 0.5 us)
Async XLA Ops:
  0.6 14.6 %collective-permute-start = (bf16[128,3584]{1,0:T(8,128)(2,1)}, bf16[128,3584]{1,0:T(8,128)(2,1)S(1)}, u32[]{:S(2)}, u32[]{:S(2)}) collective-permute-start(bf16[128,3584]{1,0:T(8,128)(2,1)} %bitcast.49), channel_id=1, source_target_pairs={{0,2},{1,5},{2,0},{3,7},{4,6},{5,1},{6,4},{7,3},{8,10},{9,13},{10,... | collective-permute-start | bytes 2752520 | tf_op jit(solution)/shard_map/ppermute | solution.py:213
  5.1 0.9 %copy-start.2 = (bf16[1,16,3584]{2,1,0:T(8,128)(2,1)S(1)}, bf16[1,16,3584]{2,1,0:T(8,128)(2,1)}, u32[]{:S(2)}) copy-start(bf16[1,16,3584]{2,1,0:T(8,128)(2,1)} %param.8) | copy-start | bytes 344068
  6.0 0.7 copy-start.5
  7.6 17.7 %collective-permute-start.4 = (bf16[16,3712]{1,0:T(8,128)(2,1)}, bf16[16,3712]{1,0:T(8,128)(2,1)}, u32[]{:S(2)}, u32[]{:S(2)}) collective-permute-start(bf16[16,3712]{1,0:T(8,128)(2,1)} %shard_map.111.refs_0_), channel_id=1, source_target_pairs={{0,8},{1,9},{2,10},{3,11},{4,12},{5,13},{6,14},{7,15},{8,0},{9,1},... | collective-permute-start | bytes 356360 | tf_op jit(solution)/shard_map/ppermute | solution.py:213
  9.2 16.7 %collective-permute-start.5 = (bf16[16,3712]{1,0:T(8,128)(2,1)}, bf16[16,3712]{1,0:T(8,128)(2,1)}, u32[]{:S(2)}, u32[]{:S(2)}) collective-permute-start(bf16[16,3712]{1,0:T(8,128)(2,1)} %shard_map.111.refs_0_), channel_id=1, source_target_pairs={{0,16},{1,17},{2,18},{3,19},{4,20},{5,21},{6,22},{7,23},{8,24},{9,... | collective-permute-start | bytes 356360 | tf_op jit(solution)/shard_map/ppermute | solution.py:213
  11.8 14.2 %collective-permute-start.6 = (bf16[16,3712]{1,0:T(8,128)(2,1)}, bf16[16,3712]{1,0:T(8,128)(2,1)}, u32[]{:S(2)}, u32[]{:S(2)}) collective-permute-start(bf16[16,3712]{1,0:T(8,128)(2,1)} %shard_map.111.refs_0_), channel_id=1, source_target_pairs={{0,24},{1,25},{2,26},{3,27},{4,28},{5,29},{6,30},{7,31},{8,16},{9,... | collective-permute-start | bytes 356360 | tf_op jit(solution)/shard_map/ppermute | solution.py:213
  15.3 8.7 %collective-permute-start.1 = (bf16[64,3584]{1,0:T(8,128)(2,1)S(1)}, bf16[64,3584]{1,0:T(8,128)(2,1)}, u32[]{:S(2)}, u32[]{:S(2)}) collective-permute-start(bf16[64,3584]{1,0:T(8,128)(2,1)S(1)} %slice_select_fusion), channel_id=1, source_target_pairs={{0,4},{1,3},{2,6},{3,1},{4,0},{5,7},{6,2},{7,5},{8,12},{9,11},{10,... | collective-permute-start | bytes 1376264 | tf_op jit(solution)/shard_map/ppermute | solution.py:213
  18.0 7.2 %copy-start.3 = (bf16[1,16,3584]{2,1,0:T(8,128)(2,1)S(1)}, bf16[1,16,3584]{2,1,0:T(8,128)(2,1)}, u32[]{:S(2)}) copy-start(bf16[1,16,3584]{2,1,0:T(8,128)(2,1)} %param.8) | copy-start | bytes 344068
  18.0 7.9 %copy-start.4 = (bf16[1,128,3584]{2,1,0:T(8,128)(2,1)S(1)}, bf16[1,128,3584]{2,1,0:T(8,128)(2,1)}, u32[]{:S(2)}) copy-start(bf16[1,128,3584]{2,1,0:T(8,128)(2,1)} %param.10) | copy-start | bytes 2752516
  19.1 6.8 %collective-permute-start.3 = (bf16[128,3584]{1,0:T(8,128)(2,1)S(1)}, bf16[128,3584]{1,0:T(8,128)(2,1)S(1)}, u32[]{:S(2)}, u32[]{:S(2)}) collective-permute-start(bf16[128,3584]{1,0:T(8,128)(2,1)S(1)} %collective-permute-done.near), channel_id=1, source_target_pairs={{0,1},{1,0},{2,3},{3,2},{4,5},{5,4},{6,7},{7,6},{8,9},{9,8},{10,11... | collective-permute-start | bytes 2752520 | tf_op jit(solution)/shard_map/ppermute | solution.py:216
  24.0 5.0 %collective-permute-start.2 = (bf16[64,3584]{1,0:T(8,128)(2,1)}, bf16[64,3584]{1,0:T(8,128)(2,1)}, u32[]{:S(2)}, u32[]{:S(2)}) collective-permute-start(bf16[64,3584]{1,0:T(8,128)(2,1)} %collective-permute-done.1.far), channel_id=1, source_target_pairs={{0,1},{1,0},{2,3},{3,2},{4,5},{5,4},{6,7},{7,6},{8,9},{9,8},{10,11... | collective-permute-start | bytes 1376264 | tf_op jit(solution)/shard_map/ppermute | solution.py:216
  25.3 52.5 %collective-permute-start.24 = (bf16[1792,1184]{0,1:T(8,128)(2,1)}, bf16[1792,1184]{0,1:T(8,128)(2,1)S(1)}, u32[]{:S(2)}, u32[]{:S(2)}) collective-permute-start(bf16[1792,1184]{0,1:T(8,128)(2,1)} %param.15), channel_id=1, source_target_pairs={{0,1},{1,0},{2,3},{3,2},{4,5},{5,4},{6,7},{7,6},{8,9},{9,8},{10,11... | collective-permute-start | bytes 12730376 | tf_op jit(solution)/shard_map/ppermute | solution.py:219
  29.0 16.0 %copy-start.7 = (f32[3584]{0:T(1024)S(1)}, f32[3584]{0:T(1024)}, u32[]{:S(2)}) copy-start(f32[3584]{0:T(1024)} %param.9) | copy-start | bytes 43012
  30.9 49.8 %slice-start = ((s8[4243456]{0:T(1024)(128)(4,1)}), s8[4194304]{0:T(1024)(128)(4,1)S(1)}, s32[]{:S(2)}) async-start(s8[4243456]{0:T(1024)(128)(4,1)} %bitcast.43), calls=%async_computation | async-start | bytes 8388608
  31.0 5.5 %collective-permute-start.7 = (bf16[16,3584]{1,0:T(8,128)(2,1)S(1)}, bf16[16,3584]{1,0:T(8,128)(2,1)S(1)}, u32[]{:S(2)}, u32[]{:S(2)}) collective-permute-start(bf16[16,3584]{1,0:T(8,128)(2,1)S(1)} %get-tuple-element.52), channel_id=1, source_target_pairs={{0,8},{1,9},{2,10},{3,11},{4,12},{5,13},{6,14},{7,15},{8,0},{9,1},... | collective-permute-start | bytes 344072 | tf_op jit(solution)/shard_map/ppermute | solution.py:213
  33.1 11.9 %collective-permute-start.8 = (bf16[16,3584]{1,0:T(8,128)(2,1)S(1)}, bf16[16,3584]{1,0:T(8,128)(2,1)S(1)}, u32[]{:S(2)}, u32[]{:S(2)}) collective-permute-start(bf16[16,3584]{1,0:T(8,128)(2,1)S(1)} %get-tuple-element.54), channel_id=1, source_target_pairs={{0,16},{1,17},{2,18},{3,19},{4,20},{5,21},{6,22},{7,23},{8,24},{9,... | collective-permute-start | bytes 344072 | tf_op jit(solution)/shard_map/ppermute | solution.py:213
  35.7 9.3 %collective-permute-start.9 = (bf16[16,3584]{1,0:T(8,128)(2,1)S(1)}, bf16[16,3584]{1,0:T(8,128)(2,1)S(1)}, u32[]{:S(2)}, u32[]{:S(2)}) collective-permute-start(bf16[16,3584]{1,0:T(8,128)(2,1)S(1)} %get-tuple-element.53), channel_id=1, source_target_pairs={{0,24},{1,25},{2,26},{3,27},{4,28},{5,29},{6,30},{7,31},{8,16},{9,... | collective-permute-start | bytes 344072 | tf_op jit(solution)/shard_map/ppermute | solution.py:213
  45.4 23.7 %copy-start.6 = (bf16[16,3584]{1,0:T(8,128)(2,1)}, bf16[16,3584]{1,0:T(8,128)(2,1)S(1)}, u32[]{:S(2)}) copy-start(bf16[16,3584]{1,0:T(8,128)(2,1)S(1)} %fusion.10) | copy-start | bytes 344068
  45.5 5.4 %collective-permute-start.11 = (bf16[2,16,896]{2,1,0:T(8,128)(2,1)S(1)}, bf16[2,16,896]{2,1,0:T(8,128)(2,1)S(1)}, u32[]{:S(2)}, u32[]{:S(2)}) collective-permute-start(bf16[2,16,896]{2,1,0:T(8,128)(2,1)S(1)} %get-tuple-element.47), channel_id=1, source_target_pairs={{0,8},{1,9},{2,10},{3,11},{4,12},{5,13},{6,14},{7,15},{8,0},{9,1},... | collective-permute-start | bytes 172040 | tf_op jit(solution)/shard_map/ppermute | solution.py:213
  47.4 7.9 %collective-permute-start.12 = (bf16[2,16,896]{2,1,0:T(8,128)(2,1)S(1)}, bf16[2,16,896]{2,1,0:T(8,128)(2,1)S(1)}, u32[]{:S(2)}, u32[]{:S(2)}) collective-permute-start(bf16[2,16,896]{2,1,0:T(8,128)(2,1)S(1)} %get-tuple-element.47), channel_id=1, source_target_pairs={{0,16},{1,17},{2,18},{3,19},{4,20},{5,21},{6,22},{7,23},{8,24},{9,... | collective-permute-start | bytes 172040 | tf_op jit(solution)/shard_map/ppermute | solution.py:213
  48.5 8.8 %collective-permute-start.13 = (bf16[2,16,896]{2,1,0:T(8,128)(2,1)S(1)}, bf16[2,16,896]{2,1,0:T(8,128)(2,1)S(1)}, u32[]{:S(2)}, u32[]{:S(2)}) collective-permute-start(bf16[2,16,896]{2,1,0:T(8,128)(2,1)S(1)} %get-tuple-element.47), channel_id=1, source_target_pairs={{0,24},{1,25},{2,26},{3,27},{4,28},{5,29},{6,30},{7,31},{8,16},{9,... | collective-permute-start | bytes 172040 | tf_op jit(solution)/shard_map/ppermute | solution.py:213
  49.9 9.0 %collective-permute-start.15 = (bf16[2,16,896]{2,1,0:T(8,128)(2,1)S(1)}, bf16[2,16,896]{2,1,0:T(8,128)(2,1)S(1)}, u32[]{:S(2)}, u32[]{:S(2)}) collective-permute-start(bf16[2,16,896]{2,1,0:T(8,128)(2,1)S(1)} %get-tuple-element.31), channel_id=1, source_target_pairs={{0,8},{1,9},{2,10},{3,11},{4,12},{5,13},{6,14},{7,15},{8,0},{9,1},... | collective-permute-start | bytes 172040 | tf_op jit(solution)/shard_map/ppermute | solution.py:213
  50.8 9.6 %collective-permute-start.16 = (bf16[2,16,896]{2,1,0:T(8,128)(2,1)S(1)}, bf16[2,16,896]{2,1,0:T(8,128)(2,1)S(1)}, u32[]{:S(2)}, u32[]{:S(2)}) collective-permute-start(bf16[2,16,896]{2,1,0:T(8,128)(2,1)S(1)} %get-tuple-element.31), channel_id=1, source_target_pairs={{0,16},{1,17},{2,18},{3,19},{4,20},{5,21},{6,22},{7,23},{8,24},{9,... | collective-permute-start | bytes 172040 | tf_op jit(solution)/shard_map/ppermute | solution.py:213
  55.3 6.0 %collective-permute-start.17 = (bf16[2,16,896]{2,1,0:T(8,128)(2,1)S(1)}, bf16[2,16,896]{2,1,0:T(8,128)(2,1)S(1)}, u32[]{:S(2)}, u32[]{:S(2)}) collective-permute-start(bf16[2,16,896]{2,1,0:T(8,128)(2,1)S(1)} %get-tuple-element.31), channel_id=1, source_target_pairs={{0,24},{1,25},{2,26},{3,27},{4,28},{5,29},{6,30},{7,31},{8,16},{9,... | collective-permute-start | bytes 172040 | tf_op jit(solution)/shard_map/ppermute | solution.py:213
  57.3 7.5 %collective-permute-start.14 = (bf16[2,64,896]{2,1,0:T(8,128)(2,1)S(1)}, bf16[2,64,896]{2,1,0:T(8,128)(2,1)S(1)}, u32[]{:S(2)}, u32[]{:S(2)}) collective-permute-start(bf16[2,64,896]{2,1,0:T(8,128)(2,1)S(1)} %pad_maximum_fusion), channel_id=1, source_target_pairs={{0,2},{1,5},{2,0},{3,7},{4,6},{5,1},{6,4},{7,3},{8,10},{9,13},{10,... | collective-permute-start | bytes 688136 | tf_op jit(solution)/shard_map/ppermute | solution.py:213
  58.9 10.1 %collective-permute-start.22 = (bf16[2,64,896]{2,1,0:T(8,128)(2,1)S(1)}, bf16[2,64,896]{2,1,0:T(8,128)(2,1)S(1)}, u32[]{:S(2)}, u32[]{:S(2)}) collective-permute-start(bf16[2,64,896]{2,1,0:T(8,128)(2,1)S(1)} %pad_maximum_fusion), channel_id=1, source_target_pairs={{0,4},{1,3},{2,6},{3,1},{4,0},{5,7},{6,2},{7,5},{8,12},{9,11},{10,... | collective-permute-start | bytes 688136 | tf_op jit(solution)/shard_map/ppermute | solution.py:213
  64.9 6.1 %collective-permute-start.19 = (bf16[2,64,896]{2,1,0:T(8,128)(2,1)S(1)}, bf16[2,64,896]{2,1,0:T(8,128)(2,1)S(1)}, u32[]{:S(2)}, u32[]{:S(2)}) collective-permute-start(bf16[2,64,896]{2,1,0:T(8,128)(2,1)S(1)} %constant_dynamic-update-slice_fusion), channel_id=1, source_target_pairs={{0,2},{1,5},{2,0},{3,7},{4,6},{5,1},{6,4},{7,3},{8,10},{9,13},{10,... | collective-permute-start | bytes 688136 | tf_op jit(solution)/shard_map/ppermute | solution.py:213
  66.4 6.5 %collective-permute-start.20 = (bf16[2,64,896]{2,1,0:T(8,128)(2,1)S(1)}, bf16[2,64,896]{2,1,0:T(8,128)(2,1)S(1)}, u32[]{:S(2)}, u32[]{:S(2)}) collective-permute-start(bf16[2,64,896]{2,1,0:T(8,128)(2,1)S(1)} %constant_dynamic-update-slice_fusion), channel_id=1, source_target_pairs={{0,4},{1,3},{2,6},{3,1},{4,0},{5,7},{6,2},{7,5},{8,12},{9,11},{10,... | collective-permute-start | bytes 688136 | tf_op jit(solution)/shard_map/ppermute | solution.py:213
  69.0 6.5 %collective-permute-start.18 = (bf16[2,64,896]{2,1,0:T(8,128)(2,1)S(1)}, bf16[2,64,896]{2,1,0:T(8,128)(2,1)S(1)}, u32[]{:S(2)}, u32[]{:S(2)}) collective-permute-start(bf16[2,64,896]{2,1,0:T(8,128)(2,1)S(1)} %collective-permute-done.14), channel_id=1, source_target_pairs={{0,4},{1,3},{2,6},{3,1},{4,0},{5,7},{6,2},{7,5},{8,12},{9,11},{10,... | collective-permute-start | bytes 688136 | tf_op jit(solution)/shard_map/ppermute | solution.py:213
  69.0 8.8 %collective-permute-start.10 = (bf16[1184,256]{1,0:T(8,128)(2,1)S(1)}, bf16[1184,256]{1,0:T(8,128)(2,1)S(1)}, u32[]{:S(2)}, u32[]{:S(2)}) collective-permute-start(bf16[1184,256]{1,0:T(8,128)(2,1)S(1)} %select_bitcast_fusion.refs_0_), channel_id=1, source_target_pairs={{0,1},{1,0},{2,3},{3,2},{4,5},{5,4},{6,7},{7,6},{8,9},{9,8},{10,11... | collective-permute-start | bytes 1818632 | tf_op jit(solution)/shard_map/ppermute | solution.py:219
  75.5 5.2 %slice-start.1 = ((s8[4243456]{0:T(1024)(128)(4,1)}), s8[49152]{0:T(1024)(128)(4,1)S(1)}, s32[]{:S(2)}) async-start(s8[4243456]{0:T(1024)(128)(4,1)} %bitcast.43), calls=%async_computation.1 | async-start | bytes 98304
  75.5 2.3 %collective-permute-start.23 = (bf16[256,896]{1,0:T(8,128)(2,1)S(1)}, bf16[256,896]{1,0:T(8,128)(2,1)S(1)}, u32[]{:S(2)}, u32[]{:S(2)}) collective-permute-start(bf16[256,896]{1,0:T(8,128)(2,1)S(1)} %get-tuple-element.50), channel_id=1, source_target_pairs={{0,1},{1,0},{2,3},{3,2},{4,5},{5,4},{6,7},{7,6},{8,9},{9,8},{10,11... | collective-permute-start | bytes 1376264 | tf_op jit(solution)/shard_map/ppermute | solution.py:219
  75.6 6.7 %collective-permute-start.21 = (bf16[2,64,896]{2,1,0:T(8,128)(2,1)S(1)}, bf16[2,64,896]{2,1,0:T(8,128)(2,1)S(1)}, u32[]{:S(2)}, u32[]{:S(2)}) collective-permute-start(bf16[2,64,896]{2,1,0:T(8,128)(2,1)S(1)} %collective-permute-done.19), channel_id=1, source_target_pairs={{0,4},{1,3},{2,6},{3,1},{4,0},{5,7},{6,2},{7,5},{8,12},{9,11},{10,... | collective-permute-start | bytes 688136 | tf_op jit(solution)/shard_map/ppermute | solution.py:213
  82.3 1.1 %copy-start = (bf16[16,16,1184]{2,1,0:T(8,128)(2,1)S(1)}, bf16[16,16,1184]{2,1,0:T(8,128)(2,1)}, u32[]{:S(2)}) copy-start(bf16[16,16,1184]{2,1,0:T(8,128)(2,1)} %refs_6_.1) | copy-start | bytes 1818628
  82.3 1.3 %copy-start.1 = (bf16[16,16,1184]{2,1,0:T(8,128)(2,1)S(1)}, bf16[16,16,1184]{2,1,0:T(8,128)(2,1)}, u32[]{:S(2)}) copy-start(bf16[16,16,1184]{2,1,0:T(8,128)(2,1)} %refs_5_.1) | copy-start | bytes 1818628
  82.4 4.6 %collective-permute-start.25 = (bf16[256,896]{1,0:T(8,128)(2,1)S(1)}, bf16[256,896]{1,0:T(8,128)(2,1)S(1)}, u32[]{:S(2)}, u32[]{:S(2)}) collective-permute-start(bf16[256,896]{1,0:T(8,128)(2,1)S(1)} %get-tuple-element.48), channel_id=1, source_target_pairs={{0,1},{1,0},{2,3},{3,2},{4,5},{5,4},{6,7},{7,6},{8,9},{9,8},{10,11... | collective-permute-start | bytes 1376264 | tf_op jit(solution)/shard_map/ppermute | solution.py:219

commit v3 on v2

v3 whole, which is shorter than its diff:
```python
import functools

import jax
import jax.numpy as jnp
from jax import lax
from jax.experimental import pallas as pl
from jax.experimental.pallas import tpu as pltpu
from jax.sharding import PartitionSpec as P

ACTIVE = 8
LBLOCK = 128
QBLOCK = 2
PLANE = 4
LANES = 128
FF_BLOCK = 256
COLUMNS = 512

norm_epsilon = 1e-06


def packet_kernel(hidden, gain, blocks, codes, packet):
    width = hidden.shape[1]
    rows = hidden[...].astype(jnp.float32)
    scale = lax.rsqrt(jnp.mean(rows * rows, axis=1, keepdims=True) + norm_epsilon)
    packet[:, :width] = (rows * scale * gain[...]).astype(jnp.bfloat16)

    def ones(shape, hit):
        at = [lax.broadcasted_iota(jnp.int32, shape, d) for d in range(2)]
        return hit(*at).astype(jnp.bfloat16)

    def times(left, right):
        return jnp.dot(left, right, preferred_element_type=jnp.float32)

    block_of = ones((rows.shape[0], blocks.shape[0]), lambda r, c: r // QBLOCK == c)
    owners = times(block_of, blocks[...].astype(jnp.bfloat16)).astype(jnp.bfloat16)
    found = codes[...]
    high = (found // LBLOCK).astype(jnp.bfloat16)
    low = (found % LBLOCK).astype(jnp.bfloat16)
    marks = sum(
        times(values, ones((values.shape[1], LANES), lambda r, c, n=n: c == r + n * ACTIVE))
        for n, values in enumerate((owners, high, low))
    )
    packet[:, width:] = marks.astype(jnp.bfloat16)


def slopes(embed, marks, rows, owner, first_label):
    scores = lax.dot_general(
        embed, rows, (((1,), (1,)), ((), ())), preferred_element_type=jnp.float32
    )
    slot = sum(
        jnp.where(marks[:, k : k + 1] == owner, k + 1, 0) for k in range(ACTIVE)
    )
    codes = marks[:, ACTIVE : 2 * ACTIVE] * LBLOCK + marks[:, 2 * ACTIVE : 3 * ACTIVE]
    label = lax.broadcasted_iota(jnp.int32, scores.shape, 1) + first_label
    code = (slot - 1) * LBLOCK + label
    positive = codes[:, 0:1] == code
    for k in range(1, ACTIVE):
        positive |= codes[:, k : k + 1] == code
    target_sign = jnp.where(positive, 1.0, -1.0)
    margin = jnp.maximum(1.0 - target_sign * scores, 0.0)
    return jnp.where(slot > 0, -2.0 * target_sign * margin, 0.0).astype(jnp.bfloat16)


def unpack(packets, width):
    embed = jnp.concatenate([packet[:, :width] for packet in packets], axis=0)
    marks = jnp.concatenate([packet[:, width:] for packet in packets], axis=0)
    return embed, marks.astype(jnp.int32)


def near_kernel(place, own, near, across, *refs):
    packets, (total, embed_out, marks_out) = refs[:-3], refs[-3:]
    width = own.shape[1]
    embed, marks = unpack(packets, width)
    embed_out[...] = embed
    marks_out[...] = marks
    here, parity = place[0], place[1]
    fetched = ((own, here), (near, here ^ (1 + parity)), (across, here ^ (2 - parity)))
    found = [(slopes(embed, marks, rows[...], owner, 0), rows) for rows, owner in fetched]
    for start in range(0, width, COLUMNS):
        span = slice(start, min(start + COLUMNS, width))
        total[:, span] = sum(
            jnp.dot(slope, rows[:, span], preferred_element_type=jnp.float32)
            for slope, rows in found
        )


def far_kernel(depth, place, far, across, total, embed, marks, *refs):
    parts = refs[-depth:]
    width = far.shape[1]
    share = far.shape[0]
    embed, marks = embed[...], marks[...]
    here, parity = place[0], place[1]
    found = [
        slopes(embed, marks, far[...], here ^ 3, parity * share),
        slopes(embed, marks, across[...], here ^ 3, (1 - parity) * share),
    ]
    for start in range(0, width, COLUMNS):
        span = slice(start, min(start + COLUMNS, width))
        added = total[:, span] + sum(
            jnp.dot(slope, rows[:, span], preferred_element_type=jnp.float32)
            for slope, rows in zip(found, (far, across))
        )
        rows = parts[0].shape[0]
        for s, part in enumerate(parts):
            part[:, span] = added[s * rows : (s + 1) * rows].astype(jnp.bfloat16)


def resid_kernel(hidden, gain, ready, *refs):
    parts, out = refs[:-1], refs[-1]
    rows = hidden[...].astype(jnp.float32)
    scale = lax.rsqrt(jnp.mean(rows * rows, axis=1, keepdims=True) + norm_epsilon)
    normed = rows * scale
    scaled = gain[...] * sum(part[...].astype(jnp.float32) for part in parts)
    out[...] = (
        scale * (scaled - normed * jnp.mean(normed * scaled, axis=1, keepdims=True))
    ).astype(jnp.bfloat16)


def pieces(extent):
    return [(start, min(start + FF_BLOCK, extent)) for start in range(0, extent, FF_BLOCK)]


def hold_kernel(*refs):
    sems, half = refs[-1], len(refs) // 2
    copies = [
        pltpu.make_async_copy(refs[n], refs[half + n], sems.at[n]) for n in range(half)
    ]
    for copy in copies:
        copy.start()
    for copy in copies:
        copy.wait()


def act_kernel(order, gate, up, act, rows_held):
    rows = gate.shape[1]
    for i in range(gate.shape[0]):
        gate_full = gate[order[i]].astype(jnp.float32)
        up_full = up[order[i]].astype(jnp.float32)
        rows_held[i * rows : (i + 1) * rows] = gate_full * jax.nn.sigmoid(gate_full) * up_full
    for start, stop in pieces(rows_held.shape[1]):
        act[start:stop] = rows_held[:, start:stop].T.astype(jnp.bfloat16)


def hidden_kernel(groups, grads, *refs):
    weights, hidden_grad = refs[:groups], refs[groups]
    for start, stop in pieces(hidden_grad.shape[1]):
        hidden_grad[:, start:stop] = sum(
            lax.dot_general(
                grads[n],
                weights[n][start:stop],
                (((1,), (1,)), ((), ())),
                preferred_element_type=jnp.float32,
            )
            for n in range(groups)
        )


def last_kernel(groups, order, hidden_grad, gate, up, *refs):
    acts, slabs, refs = refs[:groups], refs[groups : 2 * groups], refs[2 * groups :]
    down_grad, gate_grad, up_grad, gate_held, up_held, held, sems = refs
    spans = pieces(held.shape[0])
    rows, blocks = gate.shape[1], gate.shape[0]
    copies = []
    for n, (start, stop) in enumerate(spans):
        held[start:stop] = sum(
            jnp.dot(act[start:stop], slab[...], preferred_element_type=jnp.float32)
            for act, slab in zip(acts, slabs)
        )
        copies.append(
            pltpu.make_async_copy(held.at[start:stop], down_grad.at[start:stop], sems.at[n])
        )
        copies[-1].start()
        turns = max(1, len(spans) - 1)
        for i in range(n * blocks // turns, min(blocks, (n + 1) * blocks // turns)):
            block = order[i]
            part = hidden_grad[i * rows : (i + 1) * rows]
            gate_full = gate[block].astype(jnp.float32)
            up_full = up[block].astype(jnp.float32)
            sigma = jax.nn.sigmoid(gate_full)
            up_held[block] = (part * gate_full * sigma).astype(jnp.bfloat16)
            gate_held[block] = (
                part * up_full * sigma * (1.0 + gate_full * (1.0 - sigma))
            ).astype(jnp.bfloat16)
        if n == turns - 1:
            copies.append(pltpu.make_async_copy(gate_held, gate_grad, sems.at[len(spans)]))
            copies.append(pltpu.make_async_copy(up_held, up_grad, sems.at[len(spans) + 1]))
            copies[-2].start()
            copies[-1].start()
    for copy in copies:
        copy.wait()


def params(megabytes):
    return pltpu.CompilerParams(vmem_limit_bytes=megabytes * 2**20)


def shards(
    final_hidden, norm_gain, label_weights, active_blocks, positives, gate_pre, up_pre, down_weight
):
    owners = lax.axis_size("label")
    groups = lax.axis_size("fsdp")
    depth = owners // PLANE
    here = lax.axis_index("label")
    core = lax.axis_index("fsdp")
    parity = core % 2
    label_rows = label_weights[0]
    block_labels, width = label_rows.shape
    share = block_labels // 2
    smem = pl.BlockSpec(memory_space=pltpu.SMEM)
    vmem = pl.BlockSpec(memory_space=pltpu.VMEM)
    anywhere = pl.BlockSpec(memory_space=pl.ANY)

    def swap(array, even, odd):
        pairs = [
            (i * groups + f, (i ^ (odd if f % 2 else even)) * groups + f)
            for i in range(owners)
            for f in range(groups)
        ]
        return lax.ppermute(array, ("label", "fsdp"), pairs)

    def mate(array):
        return lax.ppermute(array, "fsdp", [(f, f ^ 1) for f in range(groups)])

    def between(array, step):
        return lax.ppermute(array, "fsdp", [(i, (i + step) % groups) for i in range(groups)])

    query_count = final_hidden.shape[1]
    packet = pl.pallas_call(
        packet_kernel,
        out_shape=jax.ShapeDtypeStruct((query_count, width + LANES), jnp.bfloat16),
        in_specs=[vmem] * 4,
        out_specs=vmem,
        compiler_params=params(16),
    )(final_hidden[0], norm_gain[None], active_blocks[0], positives[0])

    def along(piece):
        line = [piece]
        for s in range(1, depth):
            step = s & -s
            line.append(swap(line[s - step], PLANE * step, PLANE * step))
        return line

    packets = along(packet)

    near = swap(label_rows, 1, 2)
    near_mate = mate(near)
    passing = jnp.where(parity == 0, near[:share], near[share:])
    passing, ready = lax.optimization_barrier((passing, [packets[depth // 2][:8, :LANES]]))
    far = swap(passing, 2, 1)
    place = jnp.stack([here, parity]).astype(jnp.int32)

    plane_masks = jnp.stack([0 * parity, 1 + parity, 2 - parity, 0 * parity + 3])
    order = here ^ (
        PLANE * jnp.arange(depth, dtype=jnp.int32)[:, None] + plane_masks[None, :]
    ).reshape(owners)
    order = order.astype(jnp.int32)
    group_rows = owners * query_count
    ff_local = gate_pre.shape[2]
    weights = [down_weight.T] + [between(down_weight, n).T for n in range(1, groups)]
    others = pl.pallas_call(
        hold_kernel,
        out_shape=[jax.ShapeDtypeStruct(other.shape, other.dtype) for other in weights[1:]],
        in_specs=[anywhere] * (groups - 1),
        out_specs=[vmem] * (groups - 1),
        scratch_shapes=[pltpu.SemaphoreType.DMA((groups,))],
        compiler_params=params(16),
        cost_estimate=pl.CostEstimate(
            flops=0, bytes_accessed=4 * ff_local * width, transcendentals=0
        ),
    )(*weights[1:])
    weights = weights[:1] + list(others)
    act = pl.pallas_call(
        act_kernel,
        out_shape=jax.ShapeDtypeStruct((ff_local, group_rows), jnp.bfloat16),
        in_specs=[smem, vmem, vmem],
        out_specs=vmem,
        scratch_shapes=[pltpu.VMEM((group_rows, ff_local), jnp.float32)],
        compiler_params=params(16),
        cost_estimate=pl.CostEstimate(
            flops=8 * group_rows * ff_local,
            bytes_accessed=8 * group_rows * ff_local,
            transcendentals=group_rows * ff_local,
        ),
    )(order, gate_pre, up_pre)
    acts = [act] + [between(act, n) for n in range(1, groups)]

    far, more = lax.optimization_barrier(
        (far, [array[:8, :LANES] for array in [act, *packets[1:]]])
    )
    far_mate = mate(far)
    ready = ready + more
    line_rows = depth * query_count
    total, embed, marks = pl.pallas_call(
        near_kernel,
        out_shape=[
            jax.ShapeDtypeStruct((line_rows, width), jnp.float32),
            jax.ShapeDtypeStruct((line_rows, width), jnp.bfloat16),
            jax.ShapeDtypeStruct((line_rows, LANES), jnp.int32),
        ],
        in_specs=[smem] + [vmem] * (3 + depth),
        out_specs=[vmem] * 3,
        compiler_params=params(16),
        cost_estimate=pl.CostEstimate(
            flops=12 * line_rows * block_labels * width,
            bytes_accessed=6 * block_labels * width,
            transcendentals=0,
        ),
    )(place, label_rows, near, near_mate, *packets)
    parts = pl.pallas_call(
        functools.partial(far_kernel, depth),
        out_shape=[jax.ShapeDtypeStruct((query_count, width), jnp.bfloat16)] * depth,
        in_specs=[smem] + [vmem] * 5 + [anywhere] * len(ready),
        out_specs=[vmem] * depth,
        compiler_params=params(16),
    )(place, far, far_mate, total, embed, marks, *ready)
    resid_bf = pl.pallas_call(
        resid_kernel,
        out_shape=jax.ShapeDtypeStruct((query_count, width), jnp.bfloat16),
        in_specs=[vmem, vmem, anywhere] + [vmem] * depth,
        out_specs=vmem,
        compiler_params=params(16),
    )(
        final_hidden[0],
        norm_gain[None],
        weights[-1],
        parts[0],
        *[swap(parts[s], PLANE * s, PLANE * s) for s in range(1, depth)],
    )

    slab = width // groups
    own = jnp.stack(
        [
            lax.dynamic_slice_in_dim(resid_bf, ((core - n) % groups) * slab, slab, 1)
            for n in range(groups)
        ]
    )
    line = along(own)
    rows = []
    for some in [line[: depth // 2]] + [[piece] for piece in line[depth // 2 :]]:
        some = jnp.concatenate(some, axis=1)
        first, second = swap(some, 1, 2), swap(some, 2, 1)
        found = (some, first, second, swap(first, 2, 1))
        for start in range(0, some.shape[1], query_count):
            rows.append(
                jnp.concatenate([part[:, start : start + query_count] for part in found], axis=1)
            )
    early = jnp.concatenate(rows[: depth // 2], axis=1)
    late = jnp.concatenate(rows[depth // 2 :], axis=1)
    grads = jnp.concatenate([early, late], axis=1)
    slabs = [grads[0]] + [
        jnp.concatenate([between(half[groups - n], n) for half in (early, late)], axis=0)
        for n in range(1, groups)
    ]

    hidden_grad = pl.pallas_call(
        functools.partial(hidden_kernel, groups),
        out_shape=jax.ShapeDtypeStruct((group_rows, ff_local), jnp.float32),
        in_specs=[vmem] * (1 + groups),
        out_specs=vmem,
        compiler_params=params(16),
        cost_estimate=pl.CostEstimate(
            flops=2 * group_rows * width * ff_local,
            bytes_accessed=2 * ff_local * width,
            transcendentals=0,
        ),
    )(grads, *weights)
    down_grad, gate_grad, up_grad = pl.pallas_call(
        functools.partial(last_kernel, groups),
        out_shape=[jax.ShapeDtypeStruct((ff_local, slab), jnp.float32)]
        + [jax.ShapeDtypeStruct(gate_pre.shape, jnp.bfloat16)] * 2,
        in_specs=[smem] + [vmem] * (3 + 2 * groups),
        out_specs=[anywhere] * 3,
        scratch_shapes=[pltpu.VMEM(gate_pre.shape, jnp.bfloat16)] * 2
        + [
            pltpu.VMEM((ff_local, slab), jnp.float32),
            pltpu.SemaphoreType.DMA((len(pieces(ff_local)) + 2,)),
        ],
        compiler_params=params(20),
        cost_estimate=pl.CostEstimate(
            flops=2 * group_rows * width * ff_local,
            bytes_accessed=4 * ff_local * slab + 8 * group_rows * ff_local,
            transcendentals=group_rows * ff_local,
        ),
    )(order, hidden_grad, gate_pre, up_pre, *acts, *slabs)
    return (resid_bf[None], down_grad.T, gate_grad, up_grad)


def solution(mesh):
    placed = (
        P("label", "fsdp", None),
        P(),
        P("label", None, None),
        P("label", "fsdp", None),
        P("label", "fsdp", None),
        P(None, "fsdp", "label"),
        P(None, "fsdp", "label"),
        P("fsdp", "label"),
    )
    return jax.shard_map(
        shards,
        mesh=mesh,
        in_specs=placed,
        out_specs=(
            P("label", "fsdp", None),
            P("fsdp", "label"),
            P(None, "fsdp", "label"),
            P(None, "fsdp", "label"),
        ),
        check_vma=False,
    )
```

time: 89.9 us -> 86.1 us (0.958)
  starting transfers between devices: 33.9 us -> 26.5 us
  waiting for transfers between devices: 28.1 us -> 31.6 us
  other arithmetic: 3.7 us -> 1.15 us
  local copies, waits for them, and re-layouts: 6.62 us -> 8.5 us
    ppermute x20, starting transfers between devices: 33.1 us -> 25.9 us  [swap(): return lax.ppermute(array, ('label', 'fsdp'), pairs)]
    ppermute x20, waiting for transfers between devices: 28.1 us -> 31.6 us  [swap(): return lax.ppermute(array, ('label', 'fsdp'), pairs)]
    convert_element_type x2 -> x0, other arithmetic: 1.81 us -> none  [the longest x1 1.69 us: shards(): (gate_full * sigma * up_pre.astype(jnp.float32)).astype(jnp.bfloat16)]
    gather x2 -> x0, local copies, waits for them, and re-layouts: 1.65 us -> none  [shards(): act = jnp.take(hidden_act, order, axis=0).reshape(group_rows, ff_local).T]
    unnamed x31 -> x39, local copies, waits for them, and re-layouts: 2.88 us -> 4.49 us
    pallas_call x5 -> x6, Pallas kernels: 12.2 us -> 13.6 us  [the longest x1 5.07 us: shards(): pl.pallas_call(functools.partial(last_kernel, groups), out_shape=[jax.Sha...]
    slice x0 -> x4, local copies, waits for them, and re-layouts: none -> 1.35 us  [the longest x3 1.35 us: shards(): array[:8, :LANES]]
    transpose x1 -> x0, other arithmetic: 1.13 us -> none  [shards(): act = jnp.take(hidden_act, order, axis=0).reshape(group_rows, ff_local).T]
  transfers between devices with their start and end apart: 26 -> 26, of which waited for: 10 -> 12; matrix products, arithmetic and copies ran while one was open for 8% -> 5% of each run, Pallas kernels for 15% -> 13%
where the time goes in v3:
time: 86.1 us; the launch traced here: 85.6 us
  waiting for transfers between devices  31.6 us (37%)
  starting transfers between devices  26.5 us (31%)
  Pallas kernels  16.8 us (20%)
  local copies, waits for them, and re-layouts  8.5 us (10%)
  other arithmetic  1.15 us (1%)
  between operations  1 us (1%)
    ppermute x20, waiting for transfers between devices, swap(): return lax.ppermute(array, ('label', 'fsdp'), pairs)  31.6 us
    ppermute x20, starting transfers between devices, swap(): return lax.ppermute(array, ('label', 'fsdp'), pairs)  25.9 us
    pallas_call x1, Pallas kernels, shards(): pl.pallas_call(functools.partial(last_kernel, groups), out_shape=[jax.Sha...  5.07 us
    unnamed x39, local copies, waits for them, and re-layouts  4.49 us
    pallas_call x1, Pallas kernels, shards(): pl.pallas_call(near_kernel, out_shape=[jax.ShapeDtypeStruct((line_rows, w...  2.92 us
    pallas_call x1, Pallas kernels, shards(): pl.pallas_call(functools.partial(hidden_kernel, groups), out_shape=jax.Sh...  2.55 us
    pallas_call x1, Pallas kernels, shards(): pl.pallas_call(hold_kernel, out_shape=[jax.ShapeDtypeStruct(other.shape,...  2.37 us
    pallas_call x1, Pallas kernels, shards(): pl.pallas_call(functools.partial(far_kernel, depth), out_shape=[jax.Shape...  1.8 us
  transfers between devices with their start and end apart: 26, of which 12 were waited for; matrix products, arithmetic and copies ran while one was open for 5% of the time, Pallas kernels for 13%

profile of v3, /device:TPU:0, one launch (start us, length us, event | category | flops | bytes accessed | tf_op | source)
XLA Modules:
  0.0 85.6 jit_solution(10139152522476183946)
XLA Ops:
  0.6 0.5 collective-permute-start
  1.2 2.6 %collective-permute-start.1 = (bf16[128,3584]{1,0:T(8,128)(2,1)}, bf16[128,3584]{1,0:T(8,128)(2,1)S(1)}, u32[]{:S(2)}, u32[]{:S(2)}) collective-permute-start(bf16[128,3584]{1,0:T(8,128)(2,1)} %bitcast.25), channel_id=1, source_target_pairs={{0,2},{1,5},{2,0},{3,7},{4,6},{5,1},{6,4},{7,3},{8,10},{9,13},{10,... | collective-permute-start | bytes 2752520 | tf_op jit(solution)/shard_map/ppermute | solution.py:219
  3.7 0.8 copy.12.codes
  4.5 0.8 broadcast_in_dim.4.gain
  5.3 0.0 copy-start.6
  5.3 0.9 %copy-done.6 = bf16[1,16,3584]{2,1,0:T(8,128)(2,1)S(1)} copy-done((bf16[1,16,3584]{2,1,0:T(8,128)(2,1)S(1)}, bf16[1,16,3584]{2,1,0:T(8,128)(2,1)}, u32[]{:S(2)}) %copy-start.6) | copy-done | bytes 114712
  6.2 0.7 copy-done.10
  6.9 0.2 shard_map.112.refs_0_
  7.1 2.6 %collective-permute-start.2 = (bf16[16,3712]{1,0:T(8,128)(2,1)S(1)}, bf16[16,3712]{1,0:T(8,128)(2,1)S(1)}, u32[]{:S(2)}, u32[]{:S(2)}) collective-permute-start(bf16[16,3712]{1,0:T(8,128)(2,1)S(1)} %shard_map.112.refs_0_), channel_id=1, source_target_pairs={{0,16},{1,17},{2,18},{3,19},{4,20},{5,21},{6,22},{7,23},{8,24},{9,... | collective-permute-start | bytes 356360 | tf_op jit(solution)/shard_map/ppermute | solution.py:219
  9.7 6.2 %collective-permute-done.2.refs_2_ = bf16[16,3712]{1,0:T(8,128)(2,1)S(1)} collective-permute-done((bf16[16,3712]{1,0:T(8,128)(2,1)S(1)}, bf16[16,3712]{1,0:T(8,128)(2,1)S(1)}, u32[]{:S(2)}, u32[]{:S(2)}) %collective-permute-start.2) | collective-permute-done | bytes 118816 | tf_op jit(solution)/shard_map/ppermute | solution.py:219
  15.9 0.6 copy-done.8
  16.5 0.8 slice_select_fusion
  17.4 0.8 collective-permute-start.3
  18.2 1.6 %collective-permute-start.4 = (bf16[16,3712]{1,0:T(8,128)(2,1)S(1)}, bf16[16,3712]{1,0:T(8,128)(2,1)}, u32[]{:S(2)}, u32[]{:S(2)}) collective-permute-start(bf16[16,3712]{1,0:T(8,128)(2,1)S(1)} %shard_map.112.refs_0_), channel_id=1, source_target_pairs={{0,8},{1,9},{2,10},{3,11},{4,12},{5,13},{6,14},{7,15},{8,0},{9,1},... | collective-permute-start | bytes 356360 | tf_op jit(solution)/shard_map/ppermute | solution.py:219
  19.8 0.1 pad_add_fusion.1
  19.8 0.5 collective-permute-start.5
  20.3 0.1 add_xor_fusion
  20.4 0.1 xor.10.order
  20.4 1.1 %copy-done.2 = bf16[16,16,1184]{2,1,0:T(8,128)(2,1)S(1)} copy-done((bf16[16,16,1184]{2,1,0:T(8,128)(2,1)S(1)}, bf16[16,16,1184]{2,1,0:T(8,128)(2,1)}, u32[]{:S(2)}) %copy-start.2) | copy-done | bytes 606232
  21.5 0.9 %shard_map.113.refs_0_ = bf16[1184,256]{1,0:T(8,128)(2,1)S(1)} custom-call(s32[16]{0:T(128)S(1)} %xor.10.order, bf16[16,16,1184]{2,1,0:T(8,128)(2,1)S(1)} %copy-done.1, bf16[16,16,1184]{2,1,0:T(8,128)(2,1)S(1)} %copy-done.2), custom_call_target="tpu_custom_call" | custom-call | flops 2424832 | bytes 2424832 | tf_op jit(solution)/shard_map/pallas_call | solution.py:272
  22.5 0.0 copy-start.4
  22.5 1.9 %collective-permute-done.4.refs_1_ = bf16[16,3712]{1,0:T(8,128)(2,1)} collective-permute-done((bf16[16,3712]{1,0:T(8,128)(2,1)S(1)}, bf16[16,3712]{1,0:T(8,128)(2,1)}, u32[]{:S(2)}, u32[]{:S(2)}) %collective-permute-start.4) | collective-permute-done | bytes 118816 | tf_op jit(solution)/shard_map/ppermute | solution.py:219
  24.4 0.7 slice.65.refs_2_
  25.0 1.1 %collective-permute-done.5.refs_3_ = bf16[16,3712]{1,0:T(8,128)(2,1)} collective-permute-done((bf16[16,3712]{1,0:T(8,128)(2,1)}, bf16[16,3712]{1,0:T(8,128)(2,1)}, u32[]{:S(2)}, u32[]{:S(2)}) %collective-permute-start.5) | collective-permute-done | bytes 118816 | tf_op jit(solution)/shard_map/ppermute | solution.py:219
  26.2 0.7 slice.66.refs_4_
  26.8 0.1 pad_add_fusion.place
  26.9 2.9 %shard_map.114 = (f32[64,3584]{1,0:T(8,128)S(1)}, bf16[64,3584]{1,0:T(8,128)(2,1)S(1)}, s32[64,128]{1,0:T(8,128)S(1)}) custom-call(s32[2]{0:T(128)S(1)} %pad_add_fusion.place, bf16[128,3584]{1,0:T(8,128)(2,1)S(1)} %bitcast.26, bf16[128,3584]{1,0:T(8,128)(2,1)S(1)} %collective-permute-done.1.near, bf16[128,3584]{1,0:T(8,128)(2,1)S(1)} %collective-permute-done.7.across, ...), custom_call_target="tpu_custom_call" | custom-call | flops 352321536 | bytes 2752512 | tf_op jit(solution)/shard_map/pallas_call | solution.py:293
  29.9 1.8 %shard_map.115 = (bf16[16,3584]{1,0:T(8,128)(2,1)S(1)}, bf16[16,3584]{1,0:T(8,128)(2,1)S(1)}, bf16[16,3584]{1,0:T(8,128)(2,1)S(1)}, bf16[16,3584]{1,0:T(8,128)(2,1)S(1)}) custom-call(s32[2]{0:T(128)S(1)} %pad_add_fusion.place, bf16[64,3584]{1,0:T(8,128)(2,1)} %collective-permute-done.3.far, bf16[64,3584]{1,0:T(8,128)(2,1)S(1)} %collective-permute-done.6.across, ...), custom_call_target="tpu_custom_call" | custom-call | tf_op jit(solution)/shard_map/pallas_call | solution.py:309
  31.7 1.6 %collective-permute-start.8 = (bf16[16,3584]{1,0:T(8,128)(2,1)S(1)}, bf16[16,3584]{1,0:T(8,128)(2,1)S(1)}, u32[]{:S(2)}, u32[]{:S(2)}) collective-permute-start(bf16[16,3584]{1,0:T(8,128)(2,1)S(1)} %get-tuple-element.32), channel_id=1, source_target_pairs={{0,8},{1,9},{2,10},{3,11},{4,12},{5,13},{6,14},{7,15},{8,0},{9,1},... | collective-permute-start | bytes 344072 | tf_op jit(solution)/shard_map/ppermute | solution.py:219
  33.3 3.0 %collective-permute-start.9 = (bf16[16,3584]{1,0:T(8,128)(2,1)S(1)}, bf16[16,3584]{1,0:T(8,128)(2,1)S(1)}, u32[]{:S(2)}, u32[]{:S(2)}) collective-permute-start(bf16[16,3584]{1,0:T(8,128)(2,1)S(1)} %get-tuple-element.33), channel_id=1, source_target_pairs={{0,16},{1,17},{2,18},{3,19},{4,20},{5,21},{6,22},{7,23},{8,24},{9,... | collective-permute-start | bytes 344072 | tf_op jit(solution)/shard_map/ppermute | solution.py:219
  36.4 0.0 slice-start
  36.4 2.4 %shard_map.111.ready.refs_1_ = bf16[1184,1792]{1,0:T(8,128)(2,1)S(1)} custom-call(bf16[1184,1792]{1,0:T(8,128)(2,1)} %bitcast.1.refs_0_), custom_call_target="tpu_custom_call" | custom-call | bytes 16973824 | tf_op jit(solution)/shard_map/pallas_call | solution.py:260
  38.8 6.4 %collective-permute-done.9.refs_2_ = bf16[16,3584]{1,0:T(8,128)(2,1)S(1)} collective-permute-done((bf16[16,3584]{1,0:T(8,128)(2,1)S(1)}, bf16[16,3584]{1,0:T(8,128)(2,1)S(1)}, u32[]{:S(2)}, u32[]{:S(2)}) %collective-permute-start.9) | collective-permute-done | bytes 114720 | tf_op jit(solution)/shard_map/ppermute | solution.py:219
  45.2 0.0 slice-start.1
  45.2 0.9 %shard_map.116 = bf16[16,3584]{1,0:T(8,128)(2,1)} custom-call(bf16[16,3584]{1,0:T(8,128)(2,1)S(1)} %bitcast.28, f32[1,3584]{1,0:T(1,128)S(1)} %broadcast_in_dim.4.gain, bf16[1184,1792]{1,0:T(8,128)(2,1)S(1)} %shard_map.111.ready.refs_1_, bf16[16,3584]{1,0:T(8,128)(2,1)S(1)} %get-tuple-element.31.refs_0_, ...), custom_call_target="tpu_custom_call" | custom-call | tf_op jit(solution)/shard_map/pallas_call | solution.py:316
  46.1 0.9 dynamic-slice_bitcast_fusion.1
  47.0 2.7 %collective-permute-start.11 = (bf16[2,16,1792]{2,1,0:T(8,128)(2,1)S(1)}, bf16[2,16,1792]{2,1,0:T(8,128)(2,1)S(1)}, u32[]{:S(2)}, u32[]{:S(2)}) collective-permute-start(bf16[2,16,1792]{2,1,0:T(8,128)(2,1)S(1)} %get-tuple-element.54), channel_id=1, source_target_pairs={{0,8},{1,9},{2,10},{3,11},{4,12},{5,13},{6,14},{7,15},{8,0},{9,1},... | collective-permute-start | bytes 344072 | tf_op jit(solution)/shard_map/ppermute | solution.py:219
  49.7 1.1 %collective-permute-start.15 = (bf16[2,16,1792]{2,1,0:T(8,128)(2,1)S(1)}, bf16[2,16,1792]{2,1,0:T(8,128)(2,1)S(1)}, u32[]{:S(2)}, u32[]{:S(2)}) collective-permute-start(bf16[2,16,1792]{2,1,0:T(8,128)(2,1)S(1)} %get-tuple-element.54), channel_id=1, source_target_pairs={{0,16},{1,17},{2,18},{3,19},{4,20},{5,21},{6,22},{7,23},{8,24},{9,... | collective-permute-start | bytes 344072 | tf_op jit(solution)/shard_map/ppermute | solution.py:219
  50.8 2.5 %collective-permute-done.11 = bf16[2,16,1792]{2,1,0:T(8,128)(2,1)S(1)} collective-permute-done((bf16[2,16,1792]{2,1,0:T(8,128)(2,1)S(1)}, bf16[2,16,1792]{2,1,0:T(8,128)(2,1)S(1)}, u32[]{:S(2)}, u32[]{:S(2)}) %collective-permute-start.11) | collective-permute-done | bytes 114720 | tf_op jit(solution)/shard_map/ppermute | solution.py:219
  53.2 0.8 collective-permute-start.12
  54.1 3.4 %collective-permute-done.15 = bf16[2,16,1792]{2,1,0:T(8,128)(2,1)S(1)} collective-permute-done((bf16[2,16,1792]{2,1,0:T(8,128)(2,1)S(1)}, bf16[2,16,1792]{2,1,0:T(8,128)(2,1)S(1)}, u32[]{:S(2)}, u32[]{:S(2)}) %collective-permute-start.15) | collective-permute-done | bytes 114720 | tf_op jit(solution)/shard_map/ppermute | solution.py:219
  57.5 0.2 collective-permute-start.19
  57.7 1.1 %collective-permute-start.13 = (bf16[2,32,1792]{2,1,0:T(8,128)(2,1)S(1)}, bf16[2,32,1792]{2,1,0:T(8,128)(2,1)S(1)}, u32[]{:S(2)}, u32[]{:S(2)}) collective-permute-start(bf16[2,32,1792]{2,1,0:T(8,128)(2,1)S(1)} %pad_maximum_fusion.1), channel_id=1, source_target_pairs={{0,4},{1,3},{2,6},{3,1},{4,0},{5,7},{6,2},{7,5},{8,12},{9,11},{10,... | collective-permute-start | bytes 688136 | tf_op jit(solution)/shard_map/ppermute | solution.py:219
  58.8 1.0 %collective-permute-start.17 = (bf16[2,16,1792]{2,1,0:T(8,128)(2,1)S(1)}, bf16[2,16,1792]{2,1,0:T(8,128)(2,1)S(1)}, u32[]{:S(2)}, u32[]{:S(2)}) collective-permute-start(bf16[2,16,1792]{2,1,0:T(8,128)(2,1)S(1)} %collective-permute-done.15), channel_id=1, source_target_pairs={{0,4},{1,3},{2,6},{3,1},{4,0},{5,7},{6,2},{7,5},{8,12},{9,11},{10,... | collective-permute-start | bytes 344072 | tf_op jit(solution)/shard_map/ppermute | solution.py:219
  59.7 2.6 %collective-permute-done.19 = bf16[2,16,1792]{2,1,0:T(8,128)(2,1)S(1)} collective-permute-done((bf16[2,16,1792]{2,1,0:T(8,128)(2,1)S(1)}, bf16[2,16,1792]{2,1,0:T(8,128)(2,1)S(1)}, u32[]{:S(2)}, u32[]{:S(2)}) %collective-permute-start.19) | collective-permute-done | bytes 114720 | tf_op jit(solution)/shard_map/ppermute | solution.py:219
  62.3 0.8 collective-permute-start.16
  63.1 1.3 %collective-permute-start.20 = (bf16[2,16,1792]{2,1,0:T(8,128)(2,1)S(1)}, bf16[2,16,1792]{2,1,0:T(8,128)(2,1)S(1)}, u32[]{:S(2)}, u32[]{:S(2)}) collective-permute-start(bf16[2,16,1792]{2,1,0:T(8,128)(2,1)S(1)} %collective-permute-done.19), channel_id=1, source_target_pairs={{0,2},{1,5},{2,0},{3,7},{4,6},{5,1},{6,4},{7,3},{8,10},{9,13},{10,... | collective-permute-start | bytes 344072 | tf_op jit(solution)/shard_map/ppermute | solution.py:219
  64.4 0.8 collective-permute-done.13
  65.2 1.1 %collective-permute-start.14 = (bf16[2,32,1792]{2,1,0:T(8,128)(2,1)S(1)}, bf16[2,32,1792]{2,1,0:T(8,128)(2,1)S(1)}, u32[]{:S(2)}, u32[]{:S(2)}) collective-permute-start(bf16[2,32,1792]{2,1,0:T(8,128)(2,1)S(1)} %collective-permute-done.12), channel_id=1, source_target_pairs={{0,4},{1,3},{2,6},{3,1},{4,0},{5,7},{6,2},{7,5},{8,12},{9,11},{10,... | collective-permute-start | bytes 688136 | tf_op jit(solution)/shard_map/ppermute | solution.py:219
  66.3 1.9 %collective-permute-done.16 = bf16[2,16,1792]{2,1,0:T(8,128)(2,1)S(1)} collective-permute-done((bf16[2,16,1792]{2,1,0:T(8,128)(2,1)S(1)}, bf16[2,16,1792]{2,1,0:T(8,128)(2,1)S(1)}, u32[]{:S(2)}, u32[]{:S(2)}) %collective-permute-start.16) | collective-permute-done | bytes 114720 | tf_op jit(solution)/shard_map/ppermute | solution.py:219
  68.2 1.3 %collective-permute-start.21 = (bf16[2,16,1792]{2,1,0:T(8,128)(2,1)S(1)}, bf16[2,16,1792]{2,1,0:T(8,128)(2,1)S(1)}, u32[]{:S(2)}, u32[]{:S(2)}) collective-permute-start(bf16[2,16,1792]{2,1,0:T(8,128)(2,1)S(1)} %collective-permute-done.19), channel_id=1, source_target_pairs={{0,4},{1,3},{2,6},{3,1},{4,0},{5,7},{6,2},{7,5},{8,12},{9,11},{10,... | collective-permute-start | bytes 344072 | tf_op jit(solution)/shard_map/ppermute | solution.py:219
  69.5 1.2 %collective-permute-done.20 = bf16[2,16,1792]{2,1,0:T(8,128)(2,1)S(1)} collective-permute-done((bf16[2,16,1792]{2,1,0:T(8,128)(2,1)S(1)}, bf16[2,16,1792]{2,1,0:T(8,128)(2,1)S(1)}, u32[]{:S(2)}, u32[]{:S(2)}) %collective-permute-start.20) | collective-permute-done | bytes 114720 | tf_op jit(solution)/shard_map/ppermute | solution.py:219
  70.7 1.3 %collective-permute-start.18 = (bf16[2,16,1792]{2,1,0:T(8,128)(2,1)S(1)}, bf16[2,16,1792]{2,1,0:T(8,128)(2,1)S(1)}, u32[]{:S(2)}, u32[]{:S(2)}) collective-permute-start(bf16[2,16,1792]{2,1,0:T(8,128)(2,1)S(1)} %collective-permute-done.16), channel_id=1, source_target_pairs={{0,4},{1,3},{2,6},{3,1},{4,0},{5,7},{6,2},{7,5},{8,12},{9,11},{10,... | collective-permute-start | bytes 344072 | tf_op jit(solution)/shard_map/ppermute | solution.py:219
  72.0 0.8 collective-permute-start.22
  72.9 0.1 collective-permute-start.24
  73.1 2.4 %collective-permute-done.18 = bf16[2,16,1792]{2,1,0:T(8,128)(2,1)S(1)} collective-permute-done((bf16[2,16,1792]{2,1,0:T(8,128)(2,1)S(1)}, bf16[2,16,1792]{2,1,0:T(8,128)(2,1)S(1)}, u32[]{:S(2)}, u32[]{:S(2)}) %collective-permute-start.18) | collective-permute-done | bytes 114720 | tf_op jit(solution)/shard_map/ppermute | solution.py:219
  75.6 1.2 %collective-permute-done.22 = bf16[2,16,1792]{2,1,0:T(8,128)(2,1)S(1)} collective-permute-done((bf16[2,16,1792]{2,1,0:T(8,128)(2,1)S(1)}, bf16[2,16,1792]{2,1,0:T(8,128)(2,1)S(1)}, u32[]{:S(2)}, u32[]{:S(2)}) %collective-permute-start.22) | collective-permute-done | bytes 114720 | tf_op jit(solution)/shard_map/ppermute | solution.py:219
  76.8 0.1 collective-permute-start.25
  76.9 2.6 %shard_map.117.hidden_grad = f32[256,1184]{1,0:T(8,128)S(1)} custom-call(bf16[2,256,1792]{2,1,0:T(8,128)(2,1)S(1)} %get-tuple-element.56.grads, bf16[1184,1792]{1,0:T(8,128)(2,1)S(1)} %bitcast.24, bf16[1184,1792]{1,0:T(8,128)(2,1)S(1)} %shard_map.111.ready.refs_1_), custom_call_target="tpu_custom_call" | custom-call | flops 2172649472 | bytes 8486912 | tf_op jit(solution)/shard_map/pallas_call | solution.py:355
  79.5 0.0 copy-start.3
  79.5 0.1 slice_bitcast_fusion.refs_2_
  79.6 0.1 pad_maximum_fusion.refs_3_
  79.7 0.9 %copy-done.3 = bf16[16,16,1184]{2,1,0:T(8,128)(2,1)S(1)} copy-done((bf16[16,16,1184]{2,1,0:T(8,128)(2,1)S(1)}, bf16[16,16,1184]{2,1,0:T(8,128)(2,1)}, u32[]{:S(2)}) %copy-start.3) | copy-done | bytes 606232
  80.6 5.1 %shard_map.118 = (f32[1184,1792]{1,0:T(8,128)}, bf16[16,16,1184]{2,1,0:T(8,128)(2,1)}, bf16[16,16,1184]{2,1,0:T(8,128)(2,1)}) custom-call(s32[16]{0:T(128)S(1)} %xor.10.order, f32[256,1184]{1,0:T(8,128)S(1)} %shard_map.117.hidden_grad, bf16[16,16,1184]{2,1,0:T(8,128)(2,1)S(1)} %copy-done.1, bf16[16,16,1184]{2,1,0:T(8,128)(2,1)S(1)} %copy-done.3, ...), custom_call_target="tpu_custom_call" | custom-call | flops 2172649472 | bytes 10911744 | tf_op jit(solution)/shard_map/pallas_call | solution.py:367
  (56 shorter events, 0.4 us)
Async XLA Ops:
  0.6 19.8 %copy-start.1 = (bf16[16,16,1184]{2,1,0:T(8,128)(2,1)S(1)}, bf16[16,16,1184]{2,1,0:T(8,128)(2,1)}, u32[]{:S(2)}) copy-start(bf16[16,16,1184]{2,1,0:T(8,128)(2,1)} %gate.3) | copy-start | bytes 1818628
  0.6 35.7 %collective-permute-start = (bf16[1792,1184]{0,1:T(8,128)(2,1)}, bf16[1792,1184]{0,1:T(8,128)(2,1)}, u32[]{:S(2)}, u32[]{:S(2)}) collective-permute-start(bf16[1792,1184]{0,1:T(8,128)(2,1)} %param.15), channel_id=1, source_target_pairs={{0,1},{1,0},{2,3},{3,2},{4,5},{5,4},{6,7},{7,6},{8,9},{9,8},{10,11... | collective-permute-start | bytes 12730376 | tf_op jit(solution)/shard_map/ppermute | solution.py:225
  1.2 15.4 %collective-permute-start.1 = (bf16[128,3584]{1,0:T(8,128)(2,1)}, bf16[128,3584]{1,0:T(8,128)(2,1)S(1)}, u32[]{:S(2)}, u32[]{:S(2)}) collective-permute-start(bf16[128,3584]{1,0:T(8,128)(2,1)} %bitcast.25), channel_id=1, source_target_pairs={{0,2},{1,5},{2,0},{3,7},{4,6},{5,1},{6,4},{7,3},{8,10},{9,13},{10,... | collective-permute-start | bytes 2752520 | tf_op jit(solution)/shard_map/ppermute | solution.py:219
  4.5 22.4 %copy-start = (bf16[1,128,3584]{2,1,0:T(8,128)(2,1)S(1)}, bf16[1,128,3584]{2,1,0:T(8,128)(2,1)}, u32[]{:S(2)}) copy-start(bf16[1,128,3584]{2,1,0:T(8,128)(2,1)} %param.10) | copy-start | bytes 2752516
  5.3 0.9 %copy-start.6 = (bf16[1,16,3584]{2,1,0:T(8,128)(2,1)S(1)}, bf16[1,16,3584]{2,1,0:T(8,128)(2,1)}, u32[]{:S(2)}) copy-start(bf16[1,16,3584]{2,1,0:T(8,128)(2,1)} %param.8) | copy-start | bytes 344068
  6.2 0.7 copy-start.10
  7.1 8.8 %collective-permute-start.2 = (bf16[16,3712]{1,0:T(8,128)(2,1)S(1)}, bf16[16,3712]{1,0:T(8,128)(2,1)S(1)}, u32[]{:S(2)}, u32[]{:S(2)}) collective-permute-start(bf16[16,3712]{1,0:T(8,128)(2,1)S(1)} %shard_map.112.refs_0_), channel_id=1, source_target_pairs={{0,16},{1,17},{2,18},{3,19},{4,20},{5,21},{6,22},{7,23},{8,24},{9,... | collective-permute-start | bytes 356360 | tf_op jit(solution)/shard_map/ppermute | solution.py:219
  15.9 0.6 copy-start.8
  16.5 10.4 %collective-permute-start.7 = (bf16[128,3584]{1,0:T(8,128)(2,1)S(1)}, bf16[128,3584]{1,0:T(8,128)(2,1)S(1)}, u32[]{:S(2)}, u32[]{:S(2)}) collective-permute-start(bf16[128,3584]{1,0:T(8,128)(2,1)S(1)} %collective-permute-done.1.near), channel_id=1, source_target_pairs={{0,1},{1,0},{2,3},{3,2},{4,5},{5,4},{6,7},{7,6},{8,9},{9,8},{10,11... | collective-permute-start | bytes 2752520 | tf_op jit(solution)/shard_map/ppermute | solution.py:222
  17.4 9.5 %collective-permute-start.3 = (bf16[64,3584]{1,0:T(8,128)(2,1)}, bf16[64,3584]{1,0:T(8,128)(2,1)}, u32[]{:S(2)}, u32[]{:S(2)}) collective-permute-start(bf16[64,3584]{1,0:T(8,128)(2,1)} %slice_select_fusion), channel_id=1, source_target_pairs={{0,4},{1,3},{2,6},{3,1},{4,0},{5,7},{6,2},{7,5},{8,12},{9,11},{10,... | collective-permute-start | bytes 1376264 | tf_op jit(solution)/shard_map/ppermute | solution.py:219
  18.2 6.2 %collective-permute-start.4 = (bf16[16,3712]{1,0:T(8,128)(2,1)S(1)}, bf16[16,3712]{1,0:T(8,128)(2,1)}, u32[]{:S(2)}, u32[]{:S(2)}) collective-permute-start(bf16[16,3712]{1,0:T(8,128)(2,1)S(1)} %shard_map.112.refs_0_), channel_id=1, source_target_pairs={{0,8},{1,9},{2,10},{3,11},{4,12},{5,13},{6,14},{7,15},{8,0},{9,1},... | collective-permute-start | bytes 356360 | tf_op jit(solution)/shard_map/ppermute | solution.py:219
  19.8 6.3 %collective-permute-start.5 = (bf16[16,3712]{1,0:T(8,128)(2,1)}, bf16[16,3712]{1,0:T(8,128)(2,1)}, u32[]{:S(2)}, u32[]{:S(2)}) collective-permute-start(bf16[16,3712]{1,0:T(8,128)(2,1)} %copy-done.8), channel_id=1, source_target_pairs={{0,8},{1,9},{2,10},{3,11},{4,12},{5,13},{6,14},{7,15},{8,0},{9,1},... | collective-permute-start | bytes 356360 | tf_op jit(solution)/shard_map/ppermute | solution.py:219
  20.4 1.1 %copy-start.2 = (bf16[16,16,1184]{2,1,0:T(8,128)(2,1)S(1)}, bf16[16,16,1184]{2,1,0:T(8,128)(2,1)}, u32[]{:S(2)}) copy-start(bf16[16,16,1184]{2,1,0:T(8,128)(2,1)} %up.3) | copy-start | bytes 1818628
  21.5 5.4 %copy-start.9 = (bf16[16,3712]{1,0:T(8,128)(2,1)S(1)}, bf16[16,3712]{1,0:T(8,128)(2,1)}, u32[]{:S(2)}) copy-start(bf16[16,3712]{1,0:T(8,128)(2,1)} %copy-done.8) | copy-start | bytes 356356
  22.5 7.4 %copy-start.4 = (bf16[1184,256]{1,0:T(8,128)(2,1)}, bf16[1184,256]{1,0:T(8,128)(2,1)S(1)}, u32[]{:S(2)}) copy-start(bf16[1184,256]{1,0:T(8,128)(2,1)S(1)} %shard_map.113.refs_0_) | copy-start | bytes 1818628
  26.8 3.0 %collective-permute-start.6 = (bf16[64,3584]{1,0:T(8,128)(2,1)}, bf16[64,3584]{1,0:T(8,128)(2,1)S(1)}, u32[]{:S(2)}, u32[]{:S(2)}) collective-permute-start(bf16[64,3584]{1,0:T(8,128)(2,1)} %collective-permute-done.3.far), channel_id=1, source_target_pairs={{0,1},{1,0},{2,3},{3,2},{4,5},{5,4},{6,7},{7,6},{8,9},{9,8},{10,11... | collective-permute-start | bytes 1376264 | tf_op jit(solution)/shard_map/ppermute | solution.py:222
  31.7 7.1 %collective-permute-start.8 = (bf16[16,3584]{1,0:T(8,128)(2,1)S(1)}, bf16[16,3584]{1,0:T(8,128)(2,1)S(1)}, u32[]{:S(2)}, u32[]{:S(2)}) collective-permute-start(bf16[16,3584]{1,0:T(8,128)(2,1)S(1)} %get-tuple-element.32), channel_id=1, source_target_pairs={{0,8},{1,9},{2,10},{3,11},{4,12},{5,13},{6,14},{7,15},{8,0},{9,1},... | collective-permute-start | bytes 344072 | tf_op jit(solution)/shard_map/ppermute | solution.py:219
  33.3 11.8 %collective-permute-start.9 = (bf16[16,3584]{1,0:T(8,128)(2,1)S(1)}, bf16[16,3584]{1,0:T(8,128)(2,1)S(1)}, u32[]{:S(2)}, u32[]{:S(2)}) collective-permute-start(bf16[16,3584]{1,0:T(8,128)(2,1)S(1)} %get-tuple-element.33), channel_id=1, source_target_pairs={{0,16},{1,17},{2,18},{3,19},{4,20},{5,21},{6,22},{7,23},{8,24},{9,... | collective-permute-start | bytes 344072 | tf_op jit(solution)/shard_map/ppermute | solution.py:219
  36.3 8.8 %collective-permute-start.10 = (bf16[16,3584]{1,0:T(8,128)(2,1)S(1)}, bf16[16,3584]{1,0:T(8,128)(2,1)S(1)}, u32[]{:S(2)}, u32[]{:S(2)}) collective-permute-start(bf16[16,3584]{1,0:T(8,128)(2,1)S(1)} %get-tuple-element.34), channel_id=1, source_target_pairs={{0,24},{1,25},{2,26},{3,27},{4,28},{5,29},{6,30},{7,31},{8,16},{9,... | collective-permute-start | bytes 344072 | tf_op jit(solution)/shard_map/ppermute | solution.py:219
  36.3 8.8 %copy-start.7 = (bf16[1,16,3584]{2,1,0:T(8,128)(2,1)S(1)}, bf16[1,16,3584]{2,1,0:T(8,128)(2,1)}, u32[]{:S(2)}) copy-start(bf16[1,16,3584]{2,1,0:T(8,128)(2,1)} %param.8) | copy-start | bytes 344068
  36.4 40.5 %slice-start = ((s8[4243456]{0:T(1024)(128)(4,1)}), s8[4194304]{0:T(1024)(128)(4,1)S(1)}, s32[]{:S(2)}) async-start(s8[4243456]{0:T(1024)(128)(4,1)} %bitcast.22), calls=%async_computation | async-start | bytes 8388608
  45.2 12.5 %copy-start.5 = (bf16[1184,256]{1,0:T(8,128)(2,1)S(1)}, bf16[1184,256]{1,0:T(8,128)(2,1)}, u32[]{:S(2)}) copy-start(bf16[1184,256]{1,0:T(8,128)(2,1)} %copy-done.4) | copy-start | bytes 1818628
  45.2 31.7 %slice-start.1 = ((s8[4243456]{0:T(1024)(128)(4,1)}), s8[49152]{0:T(1024)(128)(4,1)S(1)}, s32[]{:S(2)}) async-start(s8[4243456]{0:T(1024)(128)(4,1)} %bitcast.22), calls=%async_computation.1 | async-start | bytes 98304
  47.0 6.2 %collective-permute-start.11 = (bf16[2,16,1792]{2,1,0:T(8,128)(2,1)S(1)}, bf16[2,16,1792]{2,1,0:T(8,128)(2,1)S(1)}, u32[]{:S(2)}, u32[]{:S(2)}) collective-permute-start(bf16[2,16,1792]{2,1,0:T(8,128)(2,1)S(1)} %get-tuple-element.54), channel_id=1, source_target_pairs={{0,8},{1,9},{2,10},{3,11},{4,12},{5,13},{6,14},{7,15},{8,0},{9,1},... | collective-permute-start | bytes 344072 | tf_op jit(solution)/shard_map/ppermute | solution.py:219
  49.7 7.8 %collective-permute-start.15 = (bf16[2,16,1792]{2,1,0:T(8,128)(2,1)S(1)}, bf16[2,16,1792]{2,1,0:T(8,128)(2,1)S(1)}, u32[]{:S(2)}, u32[]{:S(2)}) collective-permute-start(bf16[2,16,1792]{2,1,0:T(8,128)(2,1)S(1)} %get-tuple-element.54), channel_id=1, source_target_pairs={{0,16},{1,17},{2,18},{3,19},{4,20},{5,21},{6,22},{7,23},{8,24},{9,... | collective-permute-start | bytes 344072 | tf_op jit(solution)/shard_map/ppermute | solution.py:219
  53.2 9.8 %collective-permute-start.12 = (bf16[2,32,1792]{2,1,0:T(8,128)(2,1)S(1)}, bf16[2,32,1792]{2,1,0:T(8,128)(2,1)S(1)}, u32[]{:S(2)}, u32[]{:S(2)}) collective-permute-start(bf16[2,32,1792]{2,1,0:T(8,128)(2,1)S(1)} %pad_maximum_fusion.1), channel_id=1, source_target_pairs={{0,2},{1,5},{2,0},{3,7},{4,6},{5,1},{6,4},{7,3},{8,10},{9,13},{10,... | collective-permute-start | bytes 688136 | tf_op jit(solution)/shard_map/ppermute | solution.py:219
  57.5 4.8 %collective-permute-start.19 = (bf16[2,16,1792]{2,1,0:T(8,128)(2,1)S(1)}, bf16[2,16,1792]{2,1,0:T(8,128)(2,1)S(1)}, u32[]{:S(2)}, u32[]{:S(2)}) collective-permute-start(bf16[2,16,1792]{2,1,0:T(8,128)(2,1)S(1)} %collective-permute-done.15), channel_id=1, source_target_pairs={{0,8},{1,9},{2,10},{3,11},{4,12},{5,13},{6,14},{7,15},{8,0},{9,1},... | collective-permute-start | bytes 344072 | tf_op jit(solution)/shard_map/ppermute | solution.py:219
  57.7 22.0 %collective-permute-start.23 = (bf16[1184,256]{1,0:T(8,128)(2,1)S(1)}, bf16[1184,256]{1,0:T(8,128)(2,1)S(1)}, u32[]{:S(2)}, u32[]{:S(2)}) collective-permute-start(bf16[1184,256]{1,0:T(8,128)(2,1)S(1)} %copy-done.5), channel_id=1, source_target_pairs={{0,1},{1,0},{2,3},{3,2},{4,5},{5,4},{6,7},{7,6},{8,9},{9,8},{10,11... | collective-permute-start | bytes 1818632 | tf_op jit(solution)/shard_map/ppermute | solution.py:225
  57.7 7.5 %collective-permute-start.13 = (bf16[2,32,1792]{2,1,0:T(8,128)(2,1)S(1)}, bf16[2,32,1792]{2,1,0:T(8,128)(2,1)S(1)}, u32[]{:S(2)}, u32[]{:S(2)}) collective-permute-start(bf16[2,32,1792]{2,1,0:T(8,128)(2,1)S(1)} %pad_maximum_fusion.1), channel_id=1, source_target_pairs={{0,4},{1,3},{2,6},{3,1},{4,0},{5,7},{6,2},{7,5},{8,12},{9,11},{10,... | collective-permute-start | bytes 688136 | tf_op jit(solution)/shard_map/ppermute | solution.py:219
  58.8 14.2 %collective-permute-start.17 = (bf16[2,16,1792]{2,1,0:T(8,128)(2,1)S(1)}, bf16[2,16,1792]{2,1,0:T(8,128)(2,1)S(1)}, u32[]{:S(2)}, u32[]{:S(2)}) collective-permute-start(bf16[2,16,1792]{2,1,0:T(8,128)(2,1)S(1)} %collective-permute-done.15), channel_id=1, source_target_pairs={{0,4},{1,3},{2,6},{3,1},{4,0},{5,7},{6,2},{7,5},{8,12},{9,11},{10,... | collective-permute-start | bytes 344072 | tf_op jit(solution)/shard_map/ppermute | solution.py:219
  62.3 5.9 %collective-permute-start.16 = (bf16[2,16,1792]{2,1,0:T(8,128)(2,1)S(1)}, bf16[2,16,1792]{2,1,0:T(8,128)(2,1)S(1)}, u32[]{:S(2)}, u32[]{:S(2)}) collective-permute-start(bf16[2,16,1792]{2,1,0:T(8,128)(2,1)S(1)} %collective-permute-done.15), channel_id=1, source_target_pairs={{0,2},{1,5},{2,0},{3,7},{4,6},{5,1},{6,4},{7,3},{8,10},{9,13},{10,... | collective-permute-start | bytes 344072 | tf_op jit(solution)/shard_map/ppermute | solution.py:219
  63.1 7.6 %collective-permute-start.20 = (bf16[2,16,1792]{2,1,0:T(8,128)(2,1)S(1)}, bf16[2,16,1792]{2,1,0:T(8,128)(2,1)S(1)}, u32[]{:S(2)}, u32[]{:S(2)}) collective-permute-start(bf16[2,16,1792]{2,1,0:T(8,128)(2,1)S(1)} %collective-permute-done.19), channel_id=1, source_target_pairs={{0,2},{1,5},{2,0},{3,7},{4,6},{5,1},{6,4},{7,3},{8,10},{9,13},{10,... | collective-permute-start | bytes 344072 | tf_op jit(solution)/shard_map/ppermute | solution.py:219
  65.2 6.8 %collective-permute-start.14 = (bf16[2,32,1792]{2,1,0:T(8,128)(2,1)S(1)}, bf16[2,32,1792]{2,1,0:T(8,128)(2,1)S(1)}, u32[]{:S(2)}, u32[]{:S(2)}) collective-permute-start(bf16[2,32,1792]{2,1,0:T(8,128)(2,1)S(1)} %collective-permute-done.12), channel_id=1, source_target_pairs={{0,4},{1,3},{2,6},{3,1},{4,0},{5,7},{6,2},{7,5},{8,12},{9,11},{10,... | collective-permute-start | bytes 688136 | tf_op jit(solution)/shard_map/ppermute | solution.py:219
  68.2 7.3 %collective-permute-start.21 = (bf16[2,16,1792]{2,1,0:T(8,128)(2,1)S(1)}, bf16[2,16,1792]{2,1,0:T(8,128)(2,1)S(1)}, u32[]{:S(2)}, u32[]{:S(2)}) collective-permute-start(bf16[2,16,1792]{2,1,0:T(8,128)(2,1)S(1)} %collective-permute-done.19), channel_id=1, source_target_pairs={{0,4},{1,3},{2,6},{3,1},{4,0},{5,7},{6,2},{7,5},{8,12},{9,11},{10,... | collective-permute-start | bytes 344072 | tf_op jit(solution)/shard_map/ppermute | solution.py:219
  70.7 4.8 %collective-permute-start.18 = (bf16[2,16,1792]{2,1,0:T(8,128)(2,1)S(1)}, bf16[2,16,1792]{2,1,0:T(8,128)(2,1)S(1)}, u32[]{:S(2)}, u32[]{:S(2)}) collective-permute-start(bf16[2,16,1792]{2,1,0:T(8,128)(2,1)S(1)} %collective-permute-done.16), channel_id=1, source_target_pairs={{0,4},{1,3},{2,6},{3,1},{4,0},{5,7},{6,2},{7,5},{8,12},{9,11},{10,... | collective-permute-start | bytes 344072 | tf_op jit(solution)/shard_map/ppermute | solution.py:219
  72.0 4.8 %collective-permute-start.22 = (bf16[2,16,1792]{2,1,0:T(8,128)(2,1)S(1)}, bf16[2,16,1792]{2,1,0:T(8,128)(2,1)S(1)}, u32[]{:S(2)}, u32[]{:S(2)}) collective-permute-start(bf16[2,16,1792]{2,1,0:T(8,128)(2,1)S(1)} %collective-permute-done.20), channel_id=1, source_target_pairs={{0,4},{1,3},{2,6},{3,1},{4,0},{5,7},{6,2},{7,5},{8,12},{9,11},{10,... | collective-permute-start | bytes 344072 | tf_op jit(solution)/shard_map/ppermute | solution.py:219
  72.9 6.6 %collective-permute-start.24 = (bf16[128,1792]{1,0:T(8,128)(2,1)S(1)}, bf16[128,1792]{1,0:T(8,128)(2,1)S(1)}, u32[]{:S(2)}, u32[]{:S(2)}) collective-permute-start(bf16[128,1792]{1,0:T(8,128)(2,1)S(1)} %slice_bitcast_fusion.2), channel_id=1, source_target_pairs={{0,1},{1,0},{2,3},{3,2},{4,5},{5,4},{6,7},{7,6},{8,9},{9,8},{10,11... | collective-permute-start | bytes 1376264 | tf_op jit(solution)/shard_map/ppermute | solution.py:225
  76.8 2.8 %collective-permute-start.25 = (bf16[128,1792]{1,0:T(8,128)(2,1)S(1)}, bf16[128,1792]{1,0:T(8,128)(2,1)S(1)}, u32[]{:S(2)}, u32[]{:S(2)}) collective-permute-start(bf16[128,1792]{1,0:T(8,128)(2,1)S(1)} %slice_bitcast_fusion.1), channel_id=1, source_target_pairs={{0,1},{1,0},{2,3},{3,2},{4,5},{5,4},{6,7},{7,6},{8,9},{9,8},{10,11... | collective-permute-start | bytes 1376264 | tf_op jit(solution)/shard_map/ppermute | solution.py:225
  79.5 1.1 %copy-start.3 = (bf16[16,16,1184]{2,1,0:T(8,128)(2,1)S(1)}, bf16[16,16,1184]{2,1,0:T(8,128)(2,1)}, u32[]{:S(2)}) copy-start(bf16[16,16,1184]{2,1,0:T(8,128)(2,1)} %up.3) | copy-start | bytes 1818628

commit v4 on v3

--- a/solution.py
+++ b/solution.py
@@ -22,7 +22,7 @@
     width = hidden.shape[1]
     rows = hidden[...].astype(jnp.float32)
     scale = lax.rsqrt(jnp.mean(rows * rows, axis=1, keepdims=True) + norm_epsilon)
-    packet[:, :width] = (rows * scale * gain[...]).astype(jnp.bfloat16)
+    packet[:, :width] = (rows * scale * gain[...][None]).astype(jnp.bfloat16)
 
     def ones(shape, hit):
         at = [lax.broadcasted_iota(jnp.int32, shape, d) for d in range(2)]
@@ -36,9 +36,14 @@
     found = codes[...]
     high = (found // LBLOCK).astype(jnp.bfloat16)
     low = (found % LBLOCK).astype(jnp.bfloat16)
-    marks = sum(
-        times(values, ones((values.shape[1], LANES), lambda r, c, n=n: c == r + n * ACTIVE))
-        for n, values in enumerate((owners, high, low))
+    def spot(n):
+        return ones((ACTIVE, LANES), lambda r, c: c == r + n * ACTIVE)
+
+    marks = times(owners, spot(0)) + sum(
+        lax.dot_general(
+            values, spot(n + 1), (((0,), (0,)), ((), ())), preferred_element_type=jnp.float32
+        )
+        for n, values in enumerate((high, low))
     )
     packet[:, width:] = marks.astype(jnp.bfloat16)
 
@@ -106,14 +111,15 @@
 
 
 def resid_kernel(hidden, gain, ready, *refs):
-    parts, out = refs[:-1], refs[-1]
+    parts, out, again = refs[:-2], refs[-2], refs[-1]
     rows = hidden[...].astype(jnp.float32)
     scale = lax.rsqrt(jnp.mean(rows * rows, axis=1, keepdims=True) + norm_epsilon)
     normed = rows * scale
-    scaled = gain[...] * sum(part[...].astype(jnp.float32) for part in parts)
+    scaled = gain[...][None] * sum(part[...].astype(jnp.float32) for part in parts)
     out[...] = (
         scale * (scaled - normed * jnp.mean(normed * scaled, axis=1, keepdims=True))
     ).astype(jnp.bfloat16)
+    again[...] = out[...]
 
 
 def pieces(extent):
@@ -231,7 +237,7 @@
         in_specs=[vmem] * 4,
         out_specs=vmem,
         compiler_params=params(16),
-    )(final_hidden[0], norm_gain[None], active_blocks[0], positives[0])
+    )(final_hidden[0], norm_gain, active_blocks[0], positives[0].T)
 
     def along(piece):
         line = [piece]
@@ -313,15 +319,15 @@
         out_specs=[vmem] * depth,
         compiler_params=params(16),
     )(place, far, far_mate, total, embed, marks, *ready)
-    resid_bf = pl.pallas_call(
+    resid_bf, resid_again = pl.pallas_call(
         resid_kernel,
-        out_shape=jax.ShapeDtypeStruct((query_count, width), jnp.bfloat16),
+        out_shape=[jax.ShapeDtypeStruct((query_count, width), jnp.bfloat16)] * 2,
         in_specs=[vmem, vmem, anywhere] + [vmem] * depth,
-        out_specs=vmem,
+        out_specs=[vmem] * 2,
         compiler_params=params(16),
     )(
         final_hidden[0],
-        norm_gain[None],
+        norm_gain,
         weights[-1],
         parts[0],
         *[swap(parts[s], PLANE * s, PLANE * s) for s in range(1, depth)],
@@ -330,13 +336,13 @@
     slab = width // groups
     own = jnp.stack(
         [
-            lax.dynamic_slice_in_dim(resid_bf, ((core - n) % groups) * slab, slab, 1)
+            lax.dynamic_slice_in_dim(resid_again, ((core - n) % groups) * slab, slab, 1)
             for n in range(groups)
         ]
     )
     line = along(own)
     rows = []
-    for some in [line[: depth // 2]] + [[piece] for piece in line[depth // 2 :]]:
+    for some in [line[:1], line[1 : depth // 2 + 1]] + [[piece] for piece in line[depth // 2 + 1 :]]:
         some = jnp.concatenate(some, axis=1)
         first, second = swap(some, 1, 2), swap(some, 2, 1)
         found = (some, first, second, swap(first, 2, 1))

time: 86.1 us -> 84.4 us (0.980)
  local copies, waits for them, and re-layouts: 8.5 us -> 7.53 us
    unnamed x39 -> x45, local copies, waits for them, and re-layouts: 4.49 us -> 5.9 us
  transfers between devices with their start and end apart: 26 -> 26, of which waited for: 12 -> 9; matrix products, arithmetic and copies ran while one was open for 5% -> 3% of each run, Pallas kernels for 13% -> 13%
where the time goes in v4:
time: 84.4 us; the launch traced here: 84 us
  waiting for transfers between devices  31.3 us (37%)
  starting transfers between devices  26.2 us (31%)
  Pallas kernels  16.8 us (20%)
  local copies, waits for them, and re-layouts  7.53 us (9%)
  other arithmetic  1.13 us (1%)
  between operations  1.01 us (1%)
    ppermute x20, waiting for transfers between devices, swap(): return lax.ppermute(array, ('label', 'fsdp'), pairs)  31.3 us
    ppermute x20, starting transfers between devices, swap(): return lax.ppermute(array, ('label', 'fsdp'), pairs)  25 us
    unnamed x45, local copies, waits for them, and re-layouts  5.9 us
    pallas_call x1, Pallas kernels, shards(): pl.pallas_call(functools.partial(last_kernel, groups), out_shape=[jax.Sha...  5.07 us
    pallas_call x1, Pallas kernels, shards(): pl.pallas_call(near_kernel, out_shape=[jax.ShapeDtypeStruct((line_rows, w...  2.91 us
    pallas_call x1, Pallas kernels, shards(): pl.pallas_call(functools.partial(hidden_kernel, groups), out_shape=jax.Sh...  2.56 us
    pallas_call x1, Pallas kernels, shards(): pl.pallas_call(hold_kernel, out_shape=[jax.ShapeDtypeStruct(other.shape,...  2.37 us
    pallas_call x1, Pallas kernels, shards(): pl.pallas_call(functools.partial(far_kernel, depth), out_shape=[jax.Shape...  1.78 us
  transfers between devices with their start and end apart: 26, of which 9 were waited for; matrix products, arithmetic and copies ran while one was open for 3% of the time, Pallas kernels for 13%

profile of v4, /device:TPU:0, one launch (start us, length us, event | category | flops | bytes accessed | tf_op | source)
XLA Modules:
  0.0 84.0 jit_solution(8738707582767038911)
XLA Ops:
  0.7 0.5 collective-permute-start
  1.2 2.6 %collective-permute-start.1 = (bf16[128,3584]{1,0:T(8,128)(2,1)}, bf16[128,3584]{1,0:T(8,128)(2,1)S(1)}, u32[]{:S(2)}, u32[]{:S(2)}) collective-permute-start(bf16[128,3584]{1,0:T(8,128)(2,1)} %bitcast.27), channel_id=1, source_target_pairs={{0,2},{1,5},{2,0},{3,7},{4,6},{5,1},{6,4},{7,3},{8,10},{9,13},{10,... | collective-permute-start | bytes 2752520 | tf_op jit(solution)/shard_map/ppermute | solution.py:225
  3.7 0.9 %copy-done.6 = bf16[1,16,3584]{2,1,0:T(8,128)(2,1)S(1)} copy-done((bf16[1,16,3584]{2,1,0:T(8,128)(2,1)S(1)}, bf16[1,16,3584]{2,1,0:T(8,128)(2,1)}, u32[]{:S(2)}) %copy-start.6) | copy-done | bytes 114712
  4.6 0.7 copy-done.10
  5.4 0.7 copy-done.12
  6.0 0.7 copy-done.13
  6.7 0.2 shard_map.112.refs_0_
  7.0 2.6 %collective-permute-start.2 = (bf16[16,3712]{1,0:T(8,128)(2,1)S(1)}, bf16[16,3712]{1,0:T(8,128)(2,1)S(1)}, u32[]{:S(2)}, u32[]{:S(2)}) collective-permute-start(bf16[16,3712]{1,0:T(8,128)(2,1)S(1)} %shard_map.112.refs_0_), channel_id=1, source_target_pairs={{0,16},{1,17},{2,18},{3,19},{4,20},{5,21},{6,22},{7,23},{8,24},{9,... | collective-permute-start | bytes 356360 | tf_op jit(solution)/shard_map/ppermute | solution.py:225
  9.6 6.2 %collective-permute-done.2.refs_2_ = bf16[16,3712]{1,0:T(8,128)(2,1)S(1)} collective-permute-done((bf16[16,3712]{1,0:T(8,128)(2,1)S(1)}, bf16[16,3712]{1,0:T(8,128)(2,1)S(1)}, u32[]{:S(2)}, u32[]{:S(2)}) %collective-permute-start.2) | collective-permute-done | bytes 118816 | tf_op jit(solution)/shard_map/ppermute | solution.py:225
  15.8 0.6 copy-done.8
  16.4 0.0 collective-permute-done.1.near
  16.4 0.0 collective-permute-start.7
  16.4 0.8 slice_select_fusion
  17.2 1.0 %collective-permute-start.3 = (bf16[64,3584]{1,0:T(8,128)(2,1)}, bf16[64,3584]{1,0:T(8,128)(2,1)}, u32[]{:S(2)}, u32[]{:S(2)}) collective-permute-start(bf16[64,3584]{1,0:T(8,128)(2,1)} %slice_select_fusion), channel_id=1, source_target_pairs={{0,4},{1,3},{2,6},{3,1},{4,0},{5,7},{6,2},{7,5},{8,12},{9,11},{10,... | collective-permute-start | bytes 1376264 | tf_op jit(solution)/shard_map/ppermute | solution.py:225
  18.2 1.6 %collective-permute-start.4 = (bf16[16,3712]{1,0:T(8,128)(2,1)S(1)}, bf16[16,3712]{1,0:T(8,128)(2,1)}, u32[]{:S(2)}, u32[]{:S(2)}) collective-permute-start(bf16[16,3712]{1,0:T(8,128)(2,1)S(1)} %shard_map.112.refs_0_), channel_id=1, source_target_pairs={{0,8},{1,9},{2,10},{3,11},{4,12},{5,13},{6,14},{7,15},{8,0},{9,1},... | collective-permute-start | bytes 356360 | tf_op jit(solution)/shard_map/ppermute | solution.py:225
  19.8 0.1 pad_add_fusion.1
  19.8 0.5 collective-permute-start.5
  20.3 0.1 add_xor_fusion
  20.4 0.1 xor.10.order
  20.5 1.1 %copy-done.2 = bf16[16,16,1184]{2,1,0:T(8,128)(2,1)S(1)} copy-done((bf16[16,16,1184]{2,1,0:T(8,128)(2,1)S(1)}, bf16[16,16,1184]{2,1,0:T(8,128)(2,1)}, u32[]{:S(2)}) %copy-start.2) | copy-done | bytes 606232
  21.5 0.9 %shard_map.113.refs_0_ = bf16[1184,256]{1,0:T(8,128)(2,1)S(1)} custom-call(s32[16]{0:T(128)S(1)} %xor.10.order, bf16[16,16,1184]{2,1,0:T(8,128)(2,1)S(1)} %copy-done.1, bf16[16,16,1184]{2,1,0:T(8,128)(2,1)S(1)} %copy-done.2), custom_call_target="tpu_custom_call" | custom-call | flops 2424832 | bytes 2424832 | tf_op jit(solution)/shard_map/pallas_call | solution.py:278
  22.5 1.9 %collective-permute-done.4.refs_1_ = bf16[16,3712]{1,0:T(8,128)(2,1)} collective-permute-done((bf16[16,3712]{1,0:T(8,128)(2,1)S(1)}, bf16[16,3712]{1,0:T(8,128)(2,1)}, u32[]{:S(2)}, u32[]{:S(2)}) %collective-permute-start.4) | collective-permute-done | bytes 118816 | tf_op jit(solution)/shard_map/ppermute | solution.py:225
  24.4 0.7 slice.65.refs_2_
  25.0 1.1 %collective-permute-done.5.refs_3_ = bf16[16,3712]{1,0:T(8,128)(2,1)} collective-permute-done((bf16[16,3712]{1,0:T(8,128)(2,1)}, bf16[16,3712]{1,0:T(8,128)(2,1)}, u32[]{:S(2)}, u32[]{:S(2)}) %collective-permute-start.5) | collective-permute-done | bytes 118816 | tf_op jit(solution)/shard_map/ppermute | solution.py:225
  26.2 0.7 slice.66.refs_4_
  26.9 0.0 collective-permute-start.6
  26.9 0.1 pad_add_fusion.place
  27.0 2.9 %shard_map.114 = (f32[64,3584]{1,0:T(8,128)S(1)}, bf16[64,3584]{1,0:T(8,128)(2,1)S(1)}, s32[64,128]{1,0:T(8,128)S(1)}) custom-call(s32[2]{0:T(128)S(1)} %pad_add_fusion.place, bf16[128,3584]{1,0:T(8,128)(2,1)S(1)} %bitcast.28, bf16[128,3584]{1,0:T(8,128)(2,1)S(1)} %collective-permute-done.1.near, bf16[128,3584]{1,0:T(8,128)(2,1)S(1)} %collective-permute-done.7.across, ...), custom_call_target="tpu_custom_call" | custom-call | flops 352321536 | bytes 2752512 | tf_op jit(solution)/shard_map/pallas_call | solution.py:299
  29.9 1.8 %shard_map.115 = (bf16[16,3584]{1,0:T(8,128)(2,1)S(1)}, bf16[16,3584]{1,0:T(8,128)(2,1)S(1)}, bf16[16,3584]{1,0:T(8,128)(2,1)S(1)}, bf16[16,3584]{1,0:T(8,128)(2,1)S(1)}) custom-call(s32[2]{0:T(128)S(1)} %pad_add_fusion.place, bf16[64,3584]{1,0:T(8,128)(2,1)} %collective-permute-done.3.far, bf16[64,3584]{1,0:T(8,128)(2,1)S(1)} %collective-permute-done.6.across, ...), custom_call_target="tpu_custom_call" | custom-call | tf_op jit(solution)/shard_map/pallas_call | solution.py:315
  31.7 1.6 %collective-permute-start.8 = (bf16[16,3584]{1,0:T(8,128)(2,1)S(1)}, bf16[16,3584]{1,0:T(8,128)(2,1)S(1)}, u32[]{:S(2)}, u32[]{:S(2)}) collective-permute-start(bf16[16,3584]{1,0:T(8,128)(2,1)S(1)} %get-tuple-element.34), channel_id=1, source_target_pairs={{0,8},{1,9},{2,10},{3,11},{4,12},{5,13},{6,14},{7,15},{8,0},{9,1},... | collective-permute-start | bytes 344072 | tf_op jit(solution)/shard_map/ppermute | solution.py:225
  33.3 2.9 %collective-permute-start.9 = (bf16[16,3584]{1,0:T(8,128)(2,1)S(1)}, bf16[16,3584]{1,0:T(8,128)(2,1)S(1)}, u32[]{:S(2)}, u32[]{:S(2)}) collective-permute-start(bf16[16,3584]{1,0:T(8,128)(2,1)S(1)} %get-tuple-element.35), channel_id=1, source_target_pairs={{0,16},{1,17},{2,18},{3,19},{4,20},{5,21},{6,22},{7,23},{8,24},{9,... | collective-permute-start | bytes 344072 | tf_op jit(solution)/shard_map/ppermute | solution.py:225
  36.2 0.0 copy-start.11
  36.2 0.0 slice-start
  36.2 2.4 %shard_map.111.ready.refs_1_ = bf16[1184,1792]{1,0:T(8,128)(2,1)S(1)} custom-call(bf16[1184,1792]{1,0:T(8,128)(2,1)} %bitcast.1.refs_0_), custom_call_target="tpu_custom_call" | custom-call | bytes 16973824 | tf_op jit(solution)/shard_map/pallas_call | solution.py:266
  38.6 0.0 collective-permute-done.8.refs_1_
  38.6 6.5 %collective-permute-done.9.refs_2_ = bf16[16,3584]{1,0:T(8,128)(2,1)S(1)} collective-permute-done((bf16[16,3584]{1,0:T(8,128)(2,1)S(1)}, bf16[16,3584]{1,0:T(8,128)(2,1)S(1)}, u32[]{:S(2)}, u32[]{:S(2)}) %collective-permute-start.9) | collective-permute-done | bytes 114720 | tf_op jit(solution)/shard_map/ppermute | solution.py:225
  45.1 0.0 collective-permute-done.10.refs_3_
  45.1 0.0 slice-start.1
  45.1 0.9 %shard_map.116 = (bf16[16,3584]{1,0:T(8,128)(2,1)}, bf16[16,3584]{1,0:T(8,128)(2,1)S(1)}) custom-call(bf16[16,3584]{1,0:T(8,128)(2,1)S(1)} %bitcast.30, f32[3584]{0:T(1024)S(1)} %copy-done.11, bf16[1184,1792]{1,0:T(8,128)(2,1)S(1)} %shard_map.111.ready.refs_1_, bf16[16,3584]{1,0:T(8,128)(2,1)S(1)} %get-tuple-element.33.refs_0_, ...), custom_call_target="tpu_custom_call" | custom-call | tf_op jit(solution)/shard_map/pallas_call | solution.py:322
  46.1 0.7 collective-permute-start.11
  46.8 3.7 %collective-permute-start.15 = (bf16[2,16,1792]{2,1,0:T(8,128)(2,1)S(1)}, bf16[2,16,1792]{2,1,0:T(8,128)(2,1)S(1)}, u32[]{:S(2)}, u32[]{:S(2)}) collective-permute-start(bf16[2,16,1792]{2,1,0:T(8,128)(2,1)S(1)} %get-tuple-element.62), channel_id=1, source_target_pairs={{0,16},{1,17},{2,18},{3,19},{4,20},{5,21},{6,22},{7,23},{8,24},{9,... | collective-permute-start | bytes 344072 | tf_op jit(solution)/shard_map/ppermute | solution.py:225
  50.5 0.0 collective-permute-start.14
  50.5 1.1 %collective-permute-start.12 = (bf16[2,16,1792]{2,1,0:T(8,128)(2,1)S(1)}, bf16[2,16,1792]{2,1,0:T(8,128)(2,1)S(1)}, u32[]{:S(2)}, u32[]{:S(2)}) collective-permute-start(bf16[2,16,1792]{2,1,0:T(8,128)(2,1)S(1)} %get-tuple-element.62), channel_id=1, source_target_pairs={{0,4},{1,3},{2,6},{3,1},{4,0},{5,7},{6,2},{7,5},{8,12},{9,11},{10,... | collective-permute-start | bytes 344072 | tf_op jit(solution)/shard_map/ppermute | solution.py:225
  51.6 0.9 %collective-permute-start.13 = (bf16[2,16,1792]{2,1,0:T(8,128)(2,1)S(1)}, bf16[2,16,1792]{2,1,0:T(8,128)(2,1)S(1)}, u32[]{:S(2)}, u32[]{:S(2)}) collective-permute-start(bf16[2,16,1792]{2,1,0:T(8,128)(2,1)S(1)} %collective-permute-done.11), channel_id=1, source_target_pairs={{0,4},{1,3},{2,6},{3,1},{4,0},{5,7},{6,2},{7,5},{8,12},{9,11},{10,... | collective-permute-start | bytes 344072 | tf_op jit(solution)/shard_map/ppermute | solution.py:225
  52.5 3.7 %collective-permute-done.15 = bf16[2,16,1792]{2,1,0:T(8,128)(2,1)S(1)} collective-permute-done((bf16[2,16,1792]{2,1,0:T(8,128)(2,1)S(1)}, bf16[2,16,1792]{2,1,0:T(8,128)(2,1)S(1)}, u32[]{:S(2)}, u32[]{:S(2)}) %collective-permute-start.15) | collective-permute-done | bytes 114720 | tf_op jit(solution)/shard_map/ppermute | solution.py:225
  56.2 0.2 collective-permute-start.19
  56.4 0.1 collective-permute-done.13
  56.6 1.3 %collective-permute-start.16 = (bf16[2,32,1792]{2,1,0:T(8,128)(2,1)S(1)}, bf16[2,32,1792]{2,1,0:T(8,128)(2,1)S(1)}, u32[]{:S(2)}, u32[]{:S(2)}) collective-permute-start(bf16[2,32,1792]{2,1,0:T(8,128)(2,1)S(1)} %constant_dynamic-update-slice_fusion), channel_id=1, source_target_pairs={{0,2},{1,5},{2,0},{3,7},{4,6},{5,1},{6,4},{7,3},{8,10},{9,13},{10,... | collective-permute-start | bytes 688136 | tf_op jit(solution)/shard_map/ppermute | solution.py:225
  57.9 3.1 %collective-permute-done.19 = bf16[2,16,1792]{2,1,0:T(8,128)(2,1)S(1)} collective-permute-done((bf16[2,16,1792]{2,1,0:T(8,128)(2,1)S(1)}, bf16[2,16,1792]{2,1,0:T(8,128)(2,1)S(1)}, u32[]{:S(2)}, u32[]{:S(2)}) %collective-permute-start.19) | collective-permute-done | bytes 114720 | tf_op jit(solution)/shard_map/ppermute | solution.py:225
  61.0 0.4 collective-permute-start.20
  61.4 0.2 collective-permute-start.17
  61.6 1.8 %collective-permute-start.21 = (bf16[2,16,1792]{2,1,0:T(8,128)(2,1)S(1)}, bf16[2,16,1792]{2,1,0:T(8,128)(2,1)S(1)}, u32[]{:S(2)}, u32[]{:S(2)}) collective-permute-start(bf16[2,16,1792]{2,1,0:T(8,128)(2,1)S(1)} %collective-permute-done.19), channel_id=1, source_target_pairs={{0,4},{1,3},{2,6},{3,1},{4,0},{5,7},{6,2},{7,5},{8,12},{9,11},{10,... | collective-permute-start | bytes 344072 | tf_op jit(solution)/shard_map/ppermute | solution.py:225
  63.4 3.6 %collective-permute-done.20 = bf16[2,16,1792]{2,1,0:T(8,128)(2,1)S(1)} collective-permute-done((bf16[2,16,1792]{2,1,0:T(8,128)(2,1)S(1)}, bf16[2,16,1792]{2,1,0:T(8,128)(2,1)S(1)}, u32[]{:S(2)}, u32[]{:S(2)}) %collective-permute-start.20) | collective-permute-done | bytes 114720 | tf_op jit(solution)/shard_map/ppermute | solution.py:225
  67.0 0.5 collective-permute-start.22
  67.5 1.5 %collective-permute-start.18 = (bf16[2,32,1792]{2,1,0:T(8,128)(2,1)S(1)}, bf16[2,32,1792]{2,1,0:T(8,128)(2,1)S(1)}, u32[]{:S(2)}, u32[]{:S(2)}) collective-permute-start(bf16[2,32,1792]{2,1,0:T(8,128)(2,1)S(1)} %collective-permute-done.16), channel_id=1, source_target_pairs={{0,4},{1,3},{2,6},{3,1},{4,0},{5,7},{6,2},{7,5},{8,12},{9,11},{10,... | collective-permute-start | bytes 688136 | tf_op jit(solution)/shard_map/ppermute | solution.py:225
  69.1 5.2 %collective-permute-done.18 = bf16[2,32,1792]{2,1,0:T(8,128)(2,1)S(1)} collective-permute-done((bf16[2,32,1792]{2,1,0:T(8,128)(2,1)S(1)}, bf16[2,32,1792]{2,1,0:T(8,128)(2,1)S(1)}, u32[]{:S(2)}, u32[]{:S(2)}) %collective-permute-start.18) | collective-permute-done | bytes 229408 | tf_op jit(solution)/shard_map/ppermute | solution.py:225
  74.4 0.1 collective-permute-start.24
  74.7 0.6 collective-permute-start.25
  75.3 2.6 %shard_map.117.hidden_grad = f32[256,1184]{1,0:T(8,128)S(1)} custom-call(bf16[2,256,1792]{2,1,0:T(8,128)(2,1)S(1)} %get-tuple-element.64.grads, bf16[1184,1792]{1,0:T(8,128)(2,1)S(1)} %bitcast.26, bf16[1184,1792]{1,0:T(8,128)(2,1)S(1)} %shard_map.111.ready.refs_1_), custom_call_target="tpu_custom_call" | custom-call | flops 2172649472 | bytes 8486912 | tf_op jit(solution)/shard_map/pallas_call | solution.py:361
  77.8 0.0 copy-start.3
  77.8 0.1 slice_bitcast_fusion.refs_2_
  77.9 0.1 pad_maximum_fusion.refs_3_
  78.0 0.9 %copy-done.3 = bf16[16,16,1184]{2,1,0:T(8,128)(2,1)S(1)} copy-done((bf16[16,16,1184]{2,1,0:T(8,128)(2,1)S(1)}, bf16[16,16,1184]{2,1,0:T(8,128)(2,1)}, u32[]{:S(2)}) %copy-start.3) | copy-done | bytes 606232
  78.9 5.1 %shard_map.118 = (f32[1184,1792]{1,0:T(8,128)}, bf16[16,16,1184]{2,1,0:T(8,128)(2,1)}, bf16[16,16,1184]{2,1,0:T(8,128)(2,1)}) custom-call(s32[16]{0:T(128)S(1)} %xor.10.order, f32[256,1184]{1,0:T(8,128)S(1)} %shard_map.117.hidden_grad, bf16[16,16,1184]{2,1,0:T(8,128)(2,1)S(1)} %copy-done.1, bf16[16,16,1184]{2,1,0:T(8,128)(2,1)S(1)} %copy-done.3, ...), custom_call_target="tpu_custom_call" | custom-call | flops 2172649472 | bytes 10911744 | tf_op jit(solution)/shard_map/pallas_call | solution.py:373
  (60 shorter events, 0.5 us)
Async XLA Ops:
  0.6 26.3 %copy-start = (bf16[1,128,3584]{2,1,0:T(8,128)(2,1)S(1)}, bf16[1,128,3584]{2,1,0:T(8,128)(2,1)}, u32[]{:S(2)}) copy-start(bf16[1,128,3584]{2,1,0:T(8,128)(2,1)} %param.10) | copy-start | bytes 2752516
  0.6 19.8 %copy-start.1 = (bf16[16,16,1184]{2,1,0:T(8,128)(2,1)S(1)}, bf16[16,16,1184]{2,1,0:T(8,128)(2,1)}, u32[]{:S(2)}) copy-start(bf16[16,16,1184]{2,1,0:T(8,128)(2,1)} %gate.3) | copy-start | bytes 1818628
  0.7 35.5 %collective-permute-start = (bf16[1792,1184]{0,1:T(8,128)(2,1)}, bf16[1792,1184]{0,1:T(8,128)(2,1)}, u32[]{:S(2)}, u32[]{:S(2)}) collective-permute-start(bf16[1792,1184]{0,1:T(8,128)(2,1)} %param.15), channel_id=1, source_target_pairs={{0,1},{1,0},{2,3},{3,2},{4,5},{5,4},{6,7},{7,6},{8,9},{9,8},{10,11... | collective-permute-start | bytes 12730376 | tf_op jit(solution)/shard_map/ppermute | solution.py:231
  1.2 15.2 %collective-permute-start.1 = (bf16[128,3584]{1,0:T(8,128)(2,1)}, bf16[128,3584]{1,0:T(8,128)(2,1)S(1)}, u32[]{:S(2)}, u32[]{:S(2)}) collective-permute-start(bf16[128,3584]{1,0:T(8,128)(2,1)} %bitcast.27), channel_id=1, source_target_pairs={{0,2},{1,5},{2,0},{3,7},{4,6},{5,1},{6,4},{7,3},{8,10},{9,13},{10,... | collective-permute-start | bytes 2752520 | tf_op jit(solution)/shard_map/ppermute | solution.py:225
  3.7 0.9 %copy-start.6 = (bf16[1,16,3584]{2,1,0:T(8,128)(2,1)S(1)}, bf16[1,16,3584]{2,1,0:T(8,128)(2,1)}, u32[]{:S(2)}) copy-start(bf16[1,16,3584]{2,1,0:T(8,128)(2,1)} %param.8) | copy-start | bytes 344068
  4.6 0.7 copy-start.10
  5.4 0.7 copy-start.12
  6.0 0.7 copy-start.13
  7.0 8.8 %collective-permute-start.2 = (bf16[16,3712]{1,0:T(8,128)(2,1)S(1)}, bf16[16,3712]{1,0:T(8,128)(2,1)S(1)}, u32[]{:S(2)}, u32[]{:S(2)}) collective-permute-start(bf16[16,3712]{1,0:T(8,128)(2,1)S(1)} %shard_map.112.refs_0_), channel_id=1, source_target_pairs={{0,16},{1,17},{2,18},{3,19},{4,20},{5,21},{6,22},{7,23},{8,24},{9,... | collective-permute-start | bytes 356360 | tf_op jit(solution)/shard_map/ppermute | solution.py:225
  15.8 0.6 copy-start.8
  16.4 10.5 %collective-permute-start.7 = (bf16[128,3584]{1,0:T(8,128)(2,1)S(1)}, bf16[128,3584]{1,0:T(8,128)(2,1)S(1)}, u32[]{:S(2)}, u32[]{:S(2)}) collective-permute-start(bf16[128,3584]{1,0:T(8,128)(2,1)S(1)} %collective-permute-done.1.near), channel_id=1, source_target_pairs={{0,1},{1,0},{2,3},{3,2},{4,5},{5,4},{6,7},{7,6},{8,9},{9,8},{10,11... | collective-permute-start | bytes 2752520 | tf_op jit(solution)/shard_map/ppermute | solution.py:228
  17.2 9.6 %collective-permute-start.3 = (bf16[64,3584]{1,0:T(8,128)(2,1)}, bf16[64,3584]{1,0:T(8,128)(2,1)}, u32[]{:S(2)}, u32[]{:S(2)}) collective-permute-start(bf16[64,3584]{1,0:T(8,128)(2,1)} %slice_select_fusion), channel_id=1, source_target_pairs={{0,4},{1,3},{2,6},{3,1},{4,0},{5,7},{6,2},{7,5},{8,12},{9,11},{10,... | collective-permute-start | bytes 1376264 | tf_op jit(solution)/shard_map/ppermute | solution.py:225
  18.2 6.2 %collective-permute-start.4 = (bf16[16,3712]{1,0:T(8,128)(2,1)S(1)}, bf16[16,3712]{1,0:T(8,128)(2,1)}, u32[]{:S(2)}, u32[]{:S(2)}) collective-permute-start(bf16[16,3712]{1,0:T(8,128)(2,1)S(1)} %shard_map.112.refs_0_), channel_id=1, source_target_pairs={{0,8},{1,9},{2,10},{3,11},{4,12},{5,13},{6,14},{7,15},{8,0},{9,1},... | collective-permute-start | bytes 356360 | tf_op jit(solution)/shard_map/ppermute | solution.py:225
  19.8 6.3 %collective-permute-start.5 = (bf16[16,3712]{1,0:T(8,128)(2,1)}, bf16[16,3712]{1,0:T(8,128)(2,1)}, u32[]{:S(2)}, u32[]{:S(2)}) collective-permute-start(bf16[16,3712]{1,0:T(8,128)(2,1)} %copy-done.8), channel_id=1, source_target_pairs={{0,8},{1,9},{2,10},{3,11},{4,12},{5,13},{6,14},{7,15},{8,0},{9,1},... | collective-permute-start | bytes 356360 | tf_op jit(solution)/shard_map/ppermute | solution.py:225
  20.5 1.1 %copy-start.2 = (bf16[16,16,1184]{2,1,0:T(8,128)(2,1)S(1)}, bf16[16,16,1184]{2,1,0:T(8,128)(2,1)}, u32[]{:S(2)}) copy-start(bf16[16,16,1184]{2,1,0:T(8,128)(2,1)} %up.3) | copy-start | bytes 1818628
  21.5 5.4 %copy-start.9 = (bf16[16,3712]{1,0:T(8,128)(2,1)S(1)}, bf16[16,3712]{1,0:T(8,128)(2,1)}, u32[]{:S(2)}) copy-start(bf16[16,3712]{1,0:T(8,128)(2,1)} %copy-done.8) | copy-start | bytes 356356
  22.5 7.4 %copy-start.4 = (bf16[1184,256]{1,0:T(8,128)(2,1)}, bf16[1184,256]{1,0:T(8,128)(2,1)S(1)}, u32[]{:S(2)}) copy-start(bf16[1184,256]{1,0:T(8,128)(2,1)S(1)} %shard_map.113.refs_0_) | copy-start | bytes 1818628
  26.9 3.0 %collective-permute-start.6 = (bf16[64,3584]{1,0:T(8,128)(2,1)}, bf16[64,3584]{1,0:T(8,128)(2,1)S(1)}, u32[]{:S(2)}, u32[]{:S(2)}) collective-permute-start(bf16[64,3584]{1,0:T(8,128)(2,1)} %collective-permute-done.3.far), channel_id=1, source_target_pairs={{0,1},{1,0},{2,3},{3,2},{4,5},{5,4},{6,7},{7,6},{8,9},{9,8},{10,11... | collective-permute-start | bytes 1376264 | tf_op jit(solution)/shard_map/ppermute | solution.py:228
  31.7 6.9 %collective-permute-start.8 = (bf16[16,3584]{1,0:T(8,128)(2,1)S(1)}, bf16[16,3584]{1,0:T(8,128)(2,1)S(1)}, u32[]{:S(2)}, u32[]{:S(2)}) collective-permute-start(bf16[16,3584]{1,0:T(8,128)(2,1)S(1)} %get-tuple-element.34), channel_id=1, source_target_pairs={{0,8},{1,9},{2,10},{3,11},{4,12},{5,13},{6,14},{7,15},{8,0},{9,1},... | collective-permute-start | bytes 344072 | tf_op jit(solution)/shard_map/ppermute | solution.py:225
  33.3 11.8 %collective-permute-start.9 = (bf16[16,3584]{1,0:T(8,128)(2,1)S(1)}, bf16[16,3584]{1,0:T(8,128)(2,1)S(1)}, u32[]{:S(2)}, u32[]{:S(2)}) collective-permute-start(bf16[16,3584]{1,0:T(8,128)(2,1)S(1)} %get-tuple-element.35), channel_id=1, source_target_pairs={{0,16},{1,17},{2,18},{3,19},{4,20},{5,21},{6,22},{7,23},{8,24},{9,... | collective-permute-start | bytes 344072 | tf_op jit(solution)/shard_map/ppermute | solution.py:225
  36.2 8.9 %collective-permute-start.10 = (bf16[16,3584]{1,0:T(8,128)(2,1)S(1)}, bf16[16,3584]{1,0:T(8,128)(2,1)S(1)}, u32[]{:S(2)}, u32[]{:S(2)}) collective-permute-start(bf16[16,3584]{1,0:T(8,128)(2,1)S(1)} %get-tuple-element.36), channel_id=1, source_target_pairs={{0,24},{1,25},{2,26},{3,27},{4,28},{5,29},{6,30},{7,31},{8,16},{9,... | collective-permute-start | bytes 344072 | tf_op jit(solution)/shard_map/ppermute | solution.py:225
  36.2 8.9 %copy-start.7 = (bf16[1,16,3584]{2,1,0:T(8,128)(2,1)S(1)}, bf16[1,16,3584]{2,1,0:T(8,128)(2,1)}, u32[]{:S(2)}) copy-start(bf16[1,16,3584]{2,1,0:T(8,128)(2,1)} %param.8) | copy-start | bytes 344068
  36.2 8.9 %copy-start.11 = (f32[3584]{0:T(1024)S(1)}, f32[3584]{0:T(1024)}, u32[]{:S(2)}) copy-start(f32[3584]{0:T(1024)} %gain.3) | copy-start | bytes 43012
  36.2 39.0 %slice-start = ((s8[4243456]{0:T(1024)(128)(4,1)}), s8[4194304]{0:T(1024)(128)(4,1)S(1)}, s32[]{:S(2)}) async-start(s8[4243456]{0:T(1024)(128)(4,1)} %bitcast.24), calls=%async_computation | async-start | bytes 8388608
  45.1 30.1 %slice-start.1 = ((s8[4243456]{0:T(1024)(128)(4,1)}), s8[49152]{0:T(1024)(128)(4,1)S(1)}, s32[]{:S(2)}) async-start(s8[4243456]{0:T(1024)(128)(4,1)} %bitcast.24), calls=%async_computation.1 | async-start | bytes 98304
  46.0 15.3 %copy-start.5 = (bf16[1184,256]{1,0:T(8,128)(2,1)S(1)}, bf16[1184,256]{1,0:T(8,128)(2,1)}, u32[]{:S(2)}) copy-start(bf16[1184,256]{1,0:T(8,128)(2,1)} %copy-done.4) | copy-start | bytes 1818628
  46.1 5.5 %collective-permute-start.11 = (bf16[2,16,1792]{2,1,0:T(8,128)(2,1)S(1)}, bf16[2,16,1792]{2,1,0:T(8,128)(2,1)S(1)}, u32[]{:S(2)}, u32[]{:S(2)}) collective-permute-start(bf16[2,16,1792]{2,1,0:T(8,128)(2,1)S(1)} %get-tuple-element.62), channel_id=1, source_target_pairs={{0,2},{1,5},{2,0},{3,7},{4,6},{5,1},{6,4},{7,3},{8,10},{9,13},{10,... | collective-permute-start | bytes 344072 | tf_op jit(solution)/shard_map/ppermute | solution.py:225
  46.8 9.4 %collective-permute-start.15 = (bf16[2,16,1792]{2,1,0:T(8,128)(2,1)S(1)}, bf16[2,16,1792]{2,1,0:T(8,128)(2,1)S(1)}, u32[]{:S(2)}, u32[]{:S(2)}) collective-permute-start(bf16[2,16,1792]{2,1,0:T(8,128)(2,1)S(1)} %get-tuple-element.62), channel_id=1, source_target_pairs={{0,16},{1,17},{2,18},{3,19},{4,20},{5,21},{6,22},{7,23},{8,24},{9,... | collective-permute-start | bytes 344072 | tf_op jit(solution)/shard_map/ppermute | solution.py:225
  50.5 6.0 %collective-permute-start.14 = (bf16[2,16,1792]{2,1,0:T(8,128)(2,1)S(1)}, bf16[2,16,1792]{2,1,0:T(8,128)(2,1)S(1)}, u32[]{:S(2)}, u32[]{:S(2)}) collective-permute-start(bf16[2,16,1792]{2,1,0:T(8,128)(2,1)S(1)} %get-tuple-element.62), channel_id=1, source_target_pairs={{0,8},{1,9},{2,10},{3,11},{4,12},{5,13},{6,14},{7,15},{8,0},{9,1},... | collective-permute-start | bytes 344072 | tf_op jit(solution)/shard_map/ppermute | solution.py:225
  50.5 5.9 %collective-permute-start.12 = (bf16[2,16,1792]{2,1,0:T(8,128)(2,1)S(1)}, bf16[2,16,1792]{2,1,0:T(8,128)(2,1)S(1)}, u32[]{:S(2)}, u32[]{:S(2)}) collective-permute-start(bf16[2,16,1792]{2,1,0:T(8,128)(2,1)S(1)} %get-tuple-element.62), channel_id=1, source_target_pairs={{0,4},{1,3},{2,6},{3,1},{4,0},{5,7},{6,2},{7,5},{8,12},{9,11},{10,... | collective-permute-start | bytes 344072 | tf_op jit(solution)/shard_map/ppermute | solution.py:225
  51.6 4.9 %collective-permute-start.13 = (bf16[2,16,1792]{2,1,0:T(8,128)(2,1)S(1)}, bf16[2,16,1792]{2,1,0:T(8,128)(2,1)S(1)}, u32[]{:S(2)}, u32[]{:S(2)}) collective-permute-start(bf16[2,16,1792]{2,1,0:T(8,128)(2,1)S(1)} %collective-permute-done.11), channel_id=1, source_target_pairs={{0,4},{1,3},{2,6},{3,1},{4,0},{5,7},{6,2},{7,5},{8,12},{9,11},{10,... | collective-permute-start | bytes 344072 | tf_op jit(solution)/shard_map/ppermute | solution.py:225
  56.2 4.8 %collective-permute-start.19 = (bf16[2,16,1792]{2,1,0:T(8,128)(2,1)S(1)}, bf16[2,16,1792]{2,1,0:T(8,128)(2,1)S(1)}, u32[]{:S(2)}, u32[]{:S(2)}) collective-permute-start(bf16[2,16,1792]{2,1,0:T(8,128)(2,1)S(1)} %collective-permute-done.15), channel_id=1, source_target_pairs={{0,8},{1,9},{2,10},{3,11},{4,12},{5,13},{6,14},{7,15},{8,0},{9,1},... | collective-permute-start | bytes 344072 | tf_op jit(solution)/shard_map/ppermute | solution.py:225
  56.6 10.9 %collective-permute-start.16 = (bf16[2,32,1792]{2,1,0:T(8,128)(2,1)S(1)}, bf16[2,32,1792]{2,1,0:T(8,128)(2,1)S(1)}, u32[]{:S(2)}, u32[]{:S(2)}) collective-permute-start(bf16[2,32,1792]{2,1,0:T(8,128)(2,1)S(1)} %constant_dynamic-update-slice_fusion), channel_id=1, source_target_pairs={{0,2},{1,5},{2,0},{3,7},{4,6},{5,1},{6,4},{7,3},{8,10},{9,13},{10,... | collective-permute-start | bytes 688136 | tf_op jit(solution)/shard_map/ppermute | solution.py:225
  61.0 6.0 %collective-permute-start.20 = (bf16[2,16,1792]{2,1,0:T(8,128)(2,1)S(1)}, bf16[2,16,1792]{2,1,0:T(8,128)(2,1)S(1)}, u32[]{:S(2)}, u32[]{:S(2)}) collective-permute-start(bf16[2,16,1792]{2,1,0:T(8,128)(2,1)S(1)} %collective-permute-done.19), channel_id=1, source_target_pairs={{0,2},{1,5},{2,0},{3,7},{4,6},{5,1},{6,4},{7,3},{8,10},{9,13},{10,... | collective-permute-start | bytes 344072 | tf_op jit(solution)/shard_map/ppermute | solution.py:225
  61.4 16.6 %collective-permute-start.23 = (bf16[1184,256]{1,0:T(8,128)(2,1)S(1)}, bf16[1184,256]{1,0:T(8,128)(2,1)S(1)}, u32[]{:S(2)}, u32[]{:S(2)}) collective-permute-start(bf16[1184,256]{1,0:T(8,128)(2,1)S(1)} %copy-done.5), channel_id=1, source_target_pairs={{0,1},{1,0},{2,3},{3,2},{4,5},{5,4},{6,7},{7,6},{8,9},{9,8},{10,11... | collective-permute-start | bytes 1818632 | tf_op jit(solution)/shard_map/ppermute | solution.py:231
  61.4 7.7 %collective-permute-start.17 = (bf16[2,32,1792]{2,1,0:T(8,128)(2,1)S(1)}, bf16[2,32,1792]{2,1,0:T(8,128)(2,1)S(1)}, u32[]{:S(2)}, u32[]{:S(2)}) collective-permute-start(bf16[2,32,1792]{2,1,0:T(8,128)(2,1)S(1)} %constant_dynamic-update-slice_fusion), channel_id=1, source_target_pairs={{0,4},{1,3},{2,6},{3,1},{4,0},{5,7},{6,2},{7,5},{8,12},{9,11},{10,... | collective-permute-start | bytes 688136 | tf_op jit(solution)/shard_map/ppermute | solution.py:225
  61.6 13.0 %collective-permute-start.21 = (bf16[2,16,1792]{2,1,0:T(8,128)(2,1)S(1)}, bf16[2,16,1792]{2,1,0:T(8,128)(2,1)S(1)}, u32[]{:S(2)}, u32[]{:S(2)}) collective-permute-start(bf16[2,16,1792]{2,1,0:T(8,128)(2,1)S(1)} %collective-permute-done.19), channel_id=1, source_target_pairs={{0,4},{1,3},{2,6},{3,1},{4,0},{5,7},{6,2},{7,5},{8,12},{9,11},{10,... | collective-permute-start | bytes 344072 | tf_op jit(solution)/shard_map/ppermute | solution.py:225
  67.0 7.6 %collective-permute-start.22 = (bf16[2,16,1792]{2,1,0:T(8,128)(2,1)S(1)}, bf16[2,16,1792]{2,1,0:T(8,128)(2,1)S(1)}, u32[]{:S(2)}, u32[]{:S(2)}) collective-permute-start(bf16[2,16,1792]{2,1,0:T(8,128)(2,1)S(1)} %collective-permute-done.20), channel_id=1, source_target_pairs={{0,4},{1,3},{2,6},{3,1},{4,0},{5,7},{6,2},{7,5},{8,12},{9,11},{10,... | collective-permute-start | bytes 344072 | tf_op jit(solution)/shard_map/ppermute | solution.py:225
  67.5 6.8 %collective-permute-start.18 = (bf16[2,32,1792]{2,1,0:T(8,128)(2,1)S(1)}, bf16[2,32,1792]{2,1,0:T(8,128)(2,1)S(1)}, u32[]{:S(2)}, u32[]{:S(2)}) collective-permute-start(bf16[2,32,1792]{2,1,0:T(8,128)(2,1)S(1)} %collective-permute-done.16), channel_id=1, source_target_pairs={{0,4},{1,3},{2,6},{3,1},{4,0},{5,7},{6,2},{7,5},{8,12},{9,11},{10,... | collective-permute-start | bytes 688136 | tf_op jit(solution)/shard_map/ppermute | solution.py:225
  74.4 3.5 %collective-permute-start.24 = (bf16[128,1792]{1,0:T(8,128)(2,1)S(1)}, bf16[128,1792]{1,0:T(8,128)(2,1)S(1)}, u32[]{:S(2)}, u32[]{:S(2)}) collective-permute-start(bf16[128,1792]{1,0:T(8,128)(2,1)S(1)} %slice_bitcast_fusion.2), channel_id=1, source_target_pairs={{0,1},{1,0},{2,3},{3,2},{4,5},{5,4},{6,7},{7,6},{8,9},{9,8},{10,11... | collective-permute-start | bytes 1376264 | tf_op jit(solution)/shard_map/ppermute | solution.py:231
  74.7 3.2 %collective-permute-start.25 = (bf16[128,1792]{1,0:T(8,128)(2,1)S(1)}, bf16[128,1792]{1,0:T(8,128)(2,1)S(1)}, u32[]{:S(2)}, u32[]{:S(2)}) collective-permute-start(bf16[128,1792]{1,0:T(8,128)(2,1)S(1)} %slice_bitcast_fusion.1), channel_id=1, source_target_pairs={{0,1},{1,0},{2,3},{3,2},{4,5},{5,4},{6,7},{7,6},{8,9},{9,8},{10,11... | collective-permute-start | bytes 1376264 | tf_op jit(solution)/shard_map/ppermute | solution.py:231
  77.8 1.1 %copy-start.3 = (bf16[16,16,1184]{2,1,0:T(8,128)(2,1)S(1)}, bf16[16,16,1184]{2,1,0:T(8,128)(2,1)}, u32[]{:S(2)}) copy-start(bf16[16,16,1184]{2,1,0:T(8,128)(2,1)} %up.3) | copy-start | bytes 1818628

commit v5 on v4

--- a/solution.py
+++ b/solution.py
@@ -291,7 +291,7 @@
     acts = [act] + [between(act, n) for n in range(1, groups)]
 
     far, more = lax.optimization_barrier(
-        (far, [array[:8, :LANES] for array in [act, *packets[1:]]])
+        (far, [array[:8, :LANES] for array in [act, packets[1], packets[-1]]])
     )
     far_mate = mate(far)
     ready = ready + more

time: 84.4 us -> 84.4 us (level)
  no operation moved by 1% of the time
where the time goes in v5:
time: 84.4 us; the launch traced here: 84 us
  waiting for transfers between devices  31.3 us (37%)
  starting transfers between devices  26.2 us (31%)
  Pallas kernels  16.8 us (20%)
  local copies, waits for them, and re-layouts  7.53 us (9%)
  other arithmetic  1.13 us (1%)
  between operations  1.01 us (1%)
    ppermute x20, waiting for transfers between devices, swap(): return lax.ppermute(array, ('label', 'fsdp'), pairs)  31.3 us
    ppermute x20, starting transfers between devices, swap(): return lax.ppermute(array, ('label', 'fsdp'), pairs)  25 us
    unnamed x45, local copies, waits for them, and re-layouts  5.9 us
    pallas_call x1, Pallas kernels, shards(): pl.pallas_call(functools.partial(last_kernel, groups), out_shape=[jax.Sha...  5.07 us
    pallas_call x1, Pallas kernels, shards(): pl.pallas_call(near_kernel, out_shape=[jax.ShapeDtypeStruct((line_rows, w...  2.91 us
    pallas_call x1, Pallas kernels, shards(): pl.pallas_call(functools.partial(hidden_kernel, groups), out_shape=jax.Sh...  2.56 us
    pallas_call x1, Pallas kernels, shards(): pl.pallas_call(hold_kernel, out_shape=[jax.ShapeDtypeStruct(other.shape,...  2.37 us
    pallas_call x1, Pallas kernels, shards(): pl.pallas_call(functools.partial(far_kernel, depth), out_shape=[jax.Shape...  1.78 us
  transfers between devices with their start and end apart: 26, of which 9 were waited for; matrix products, arithmetic and copies ran while one was open for 3% of the time, Pallas kernels for 13%

profile of v5, /device:TPU:0, one launch (start us, length us, event | category | flops | bytes accessed | tf_op | source)
XLA Modules:
  0.0 84.0 jit_solution(17162992120580963348)
XLA Ops:
  0.7 0.5 collective-permute-start
  1.2 2.6 %collective-permute-start.1 = (bf16[128,3584]{1,0:T(8,128)(2,1)}, bf16[128,3584]{1,0:T(8,128)(2,1)S(1)}, u32[]{:S(2)}, u32[]{:S(2)}) collective-permute-start(bf16[128,3584]{1,0:T(8,128)(2,1)} %bitcast.27), channel_id=1, source_target_pairs={{0,2},{1,5},{2,0},{3,7},{4,6},{5,1},{6,4},{7,3},{8,10},{9,13},{10,... | collective-permute-start | bytes 2752520 | tf_op jit(solution)/shard_map/ppermute | solution.py:225
  3.7 0.9 %copy-done.6 = bf16[1,16,3584]{2,1,0:T(8,128)(2,1)S(1)} copy-done((bf16[1,16,3584]{2,1,0:T(8,128)(2,1)S(1)}, bf16[1,16,3584]{2,1,0:T(8,128)(2,1)}, u32[]{:S(2)}) %copy-start.6) | copy-done | bytes 114712
  4.6 0.7 copy-done.10
  5.4 0.7 copy-done.12
  6.0 0.7 copy-done.13
  6.7 0.2 shard_map.112.refs_0_
  7.0 2.6 %collective-permute-start.2 = (bf16[16,3712]{1,0:T(8,128)(2,1)S(1)}, bf16[16,3712]{1,0:T(8,128)(2,1)S(1)}, u32[]{:S(2)}, u32[]{:S(2)}) collective-permute-start(bf16[16,3712]{1,0:T(8,128)(2,1)S(1)} %shard_map.112.refs_0_), channel_id=1, source_target_pairs={{0,16},{1,17},{2,18},{3,19},{4,20},{5,21},{6,22},{7,23},{8,24},{9,... | collective-permute-start | bytes 356360 | tf_op jit(solution)/shard_map/ppermute | solution.py:225
  9.6 6.2 %collective-permute-done.2.refs_2_ = bf16[16,3712]{1,0:T(8,128)(2,1)S(1)} collective-permute-done((bf16[16,3712]{1,0:T(8,128)(2,1)S(1)}, bf16[16,3712]{1,0:T(8,128)(2,1)S(1)}, u32[]{:S(2)}, u32[]{:S(2)}) %collective-permute-start.2) | collective-permute-done | bytes 118816 | tf_op jit(solution)/shard_map/ppermute | solution.py:225
  15.8 0.6 copy-done.8
  16.4 0.0 collective-permute-done.1.near
  16.4 0.0 collective-permute-start.7
  16.4 0.8 slice_select_fusion
  17.2 1.0 %collective-permute-start.3 = (bf16[64,3584]{1,0:T(8,128)(2,1)}, bf16[64,3584]{1,0:T(8,128)(2,1)}, u32[]{:S(2)}, u32[]{:S(2)}) collective-permute-start(bf16[64,3584]{1,0:T(8,128)(2,1)} %slice_select_fusion), channel_id=1, source_target_pairs={{0,4},{1,3},{2,6},{3,1},{4,0},{5,7},{6,2},{7,5},{8,12},{9,11},{10,... | collective-permute-start | bytes 1376264 | tf_op jit(solution)/shard_map/ppermute | solution.py:225
  18.2 1.6 %collective-permute-start.4 = (bf16[16,3712]{1,0:T(8,128)(2,1)S(1)}, bf16[16,3712]{1,0:T(8,128)(2,1)}, u32[]{:S(2)}, u32[]{:S(2)}) collective-permute-start(bf16[16,3712]{1,0:T(8,128)(2,1)S(1)} %shard_map.112.refs_0_), channel_id=1, source_target_pairs={{0,8},{1,9},{2,10},{3,11},{4,12},{5,13},{6,14},{7,15},{8,0},{9,1},... | collective-permute-start | bytes 356360 | tf_op jit(solution)/shard_map/ppermute | solution.py:225
  19.8 0.1 pad_add_fusion.1
  19.8 0.5 collective-permute-start.5
  20.3 0.1 add_xor_fusion
  20.4 0.1 xor.10.order
  20.5 1.1 %copy-done.2 = bf16[16,16,1184]{2,1,0:T(8,128)(2,1)S(1)} copy-done((bf16[16,16,1184]{2,1,0:T(8,128)(2,1)S(1)}, bf16[16,16,1184]{2,1,0:T(8,128)(2,1)}, u32[]{:S(2)}) %copy-start.2) | copy-done | bytes 606232
  21.5 0.9 %shard_map.113.refs_0_ = bf16[1184,256]{1,0:T(8,128)(2,1)S(1)} custom-call(s32[16]{0:T(128)S(1)} %xor.10.order, bf16[16,16,1184]{2,1,0:T(8,128)(2,1)S(1)} %copy-done.1, bf16[16,16,1184]{2,1,0:T(8,128)(2,1)S(1)} %copy-done.2), custom_call_target="tpu_custom_call" | custom-call | flops 2424832 | bytes 2424832 | tf_op jit(solution)/shard_map/pallas_call | solution.py:278
  22.5 1.9 %collective-permute-done.4.refs_1_ = bf16[16,3712]{1,0:T(8,128)(2,1)} collective-permute-done((bf16[16,3712]{1,0:T(8,128)(2,1)S(1)}, bf16[16,3712]{1,0:T(8,128)(2,1)}, u32[]{:S(2)}, u32[]{:S(2)}) %collective-permute-start.4) | collective-permute-done | bytes 118816 | tf_op jit(solution)/shard_map/ppermute | solution.py:225
  24.4 0.7 slice.64.refs_2_
  25.0 1.1 %collective-permute-done.5.refs_3_ = bf16[16,3712]{1,0:T(8,128)(2,1)} collective-permute-done((bf16[16,3712]{1,0:T(8,128)(2,1)}, bf16[16,3712]{1,0:T(8,128)(2,1)}, u32[]{:S(2)}, u32[]{:S(2)}) %collective-permute-start.5) | collective-permute-done | bytes 118816 | tf_op jit(solution)/shard_map/ppermute | solution.py:225
  26.2 0.7 slice.65.refs_3_
  26.9 0.0 collective-permute-start.6
  26.9 0.1 pad_add_fusion.place
  27.0 2.9 %shard_map.114 = (f32[64,3584]{1,0:T(8,128)S(1)}, bf16[64,3584]{1,0:T(8,128)(2,1)S(1)}, s32[64,128]{1,0:T(8,128)S(1)}) custom-call(s32[2]{0:T(128)S(1)} %pad_add_fusion.place, bf16[128,3584]{1,0:T(8,128)(2,1)S(1)} %bitcast.28, bf16[128,3584]{1,0:T(8,128)(2,1)S(1)} %collective-permute-done.1.near, bf16[128,3584]{1,0:T(8,128)(2,1)S(1)} %collective-permute-done.7.across, ...), custom_call_target="tpu_custom_call" | custom-call | flops 352321536 | bytes 2752512 | tf_op jit(solution)/shard_map/pallas_call | solution.py:299
  29.9 1.8 %shard_map.115 = (bf16[16,3584]{1,0:T(8,128)(2,1)S(1)}, bf16[16,3584]{1,0:T(8,128)(2,1)S(1)}, bf16[16,3584]{1,0:T(8,128)(2,1)S(1)}, bf16[16,3584]{1,0:T(8,128)(2,1)S(1)}) custom-call(s32[2]{0:T(128)S(1)} %pad_add_fusion.place, bf16[64,3584]{1,0:T(8,128)(2,1)} %collective-permute-done.3.far, bf16[64,3584]{1,0:T(8,128)(2,1)S(1)} %collective-permute-done.6.across, ...), custom_call_target="tpu_custom_call" | custom-call | tf_op jit(solution)/shard_map/pallas_call | solution.py:315
  31.7 1.6 %collective-permute-start.8 = (bf16[16,3584]{1,0:T(8,128)(2,1)S(1)}, bf16[16,3584]{1,0:T(8,128)(2,1)S(1)}, u32[]{:S(2)}, u32[]{:S(2)}) collective-permute-start(bf16[16,3584]{1,0:T(8,128)(2,1)S(1)} %get-tuple-element.32), channel_id=1, source_target_pairs={{0,8},{1,9},{2,10},{3,11},{4,12},{5,13},{6,14},{7,15},{8,0},{9,1},... | collective-permute-start | bytes 344072 | tf_op jit(solution)/shard_map/ppermute | solution.py:225
  33.3 2.9 %collective-permute-start.9 = (bf16[16,3584]{1,0:T(8,128)(2,1)S(1)}, bf16[16,3584]{1,0:T(8,128)(2,1)S(1)}, u32[]{:S(2)}, u32[]{:S(2)}) collective-permute-start(bf16[16,3584]{1,0:T(8,128)(2,1)S(1)} %get-tuple-element.33), channel_id=1, source_target_pairs={{0,16},{1,17},{2,18},{3,19},{4,20},{5,21},{6,22},{7,23},{8,24},{9,... | collective-permute-start | bytes 344072 | tf_op jit(solution)/shard_map/ppermute | solution.py:225
  36.2 0.0 copy-start.11
  36.2 0.0 slice-start
  36.2 2.4 %shard_map.111.ready.refs_1_ = bf16[1184,1792]{1,0:T(8,128)(2,1)S(1)} custom-call(bf16[1184,1792]{1,0:T(8,128)(2,1)} %bitcast.1.refs_0_), custom_call_target="tpu_custom_call" | custom-call | bytes 16973824 | tf_op jit(solution)/shard_map/pallas_call | solution.py:266
  38.6 0.0 collective-permute-done.8.refs_1_
  38.6 6.5 %collective-permute-done.9.refs_2_ = bf16[16,3584]{1,0:T(8,128)(2,1)S(1)} collective-permute-done((bf16[16,3584]{1,0:T(8,128)(2,1)S(1)}, bf16[16,3584]{1,0:T(8,128)(2,1)S(1)}, u32[]{:S(2)}, u32[]{:S(2)}) %collective-permute-start.9) | collective-permute-done | bytes 114720 | tf_op jit(solution)/shard_map/ppermute | solution.py:225
  45.1 0.0 collective-permute-done.10.refs_3_
  45.1 0.0 slice-start.1
  45.1 0.9 %shard_map.116 = (bf16[16,3584]{1,0:T(8,128)(2,1)}, bf16[16,3584]{1,0:T(8,128)(2,1)S(1)}) custom-call(bf16[16,3584]{1,0:T(8,128)(2,1)S(1)} %bitcast.30, f32[3584]{0:T(1024)S(1)} %copy-done.11, bf16[1184,1792]{1,0:T(8,128)(2,1)S(1)} %shard_map.111.ready.refs_1_, bf16[16,3584]{1,0:T(8,128)(2,1)S(1)} %get-tuple-element.31.refs_0_, ...), custom_call_target="tpu_custom_call" | custom-call | tf_op jit(solution)/shard_map/pallas_call | solution.py:322
  46.1 0.7 collective-permute-start.11
  46.8 3.7 %collective-permute-start.15 = (bf16[2,16,1792]{2,1,0:T(8,128)(2,1)S(1)}, bf16[2,16,1792]{2,1,0:T(8,128)(2,1)S(1)}, u32[]{:S(2)}, u32[]{:S(2)}) collective-permute-start(bf16[2,16,1792]{2,1,0:T(8,128)(2,1)S(1)} %get-tuple-element.60), channel_id=1, source_target_pairs={{0,16},{1,17},{2,18},{3,19},{4,20},{5,21},{6,22},{7,23},{8,24},{9,... | collective-permute-start | bytes 344072 | tf_op jit(solution)/shard_map/ppermute | solution.py:225
  50.5 0.0 collective-permute-start.14
  50.5 1.1 %collective-permute-start.12 = (bf16[2,16,1792]{2,1,0:T(8,128)(2,1)S(1)}, bf16[2,16,1792]{2,1,0:T(8,128)(2,1)S(1)}, u32[]{:S(2)}, u32[]{:S(2)}) collective-permute-start(bf16[2,16,1792]{2,1,0:T(8,128)(2,1)S(1)} %get-tuple-element.60), channel_id=1, source_target_pairs={{0,4},{1,3},{2,6},{3,1},{4,0},{5,7},{6,2},{7,5},{8,12},{9,11},{10,... | collective-permute-start | bytes 344072 | tf_op jit(solution)/shard_map/ppermute | solution.py:225
  51.6 0.9 %collective-permute-start.13 = (bf16[2,16,1792]{2,1,0:T(8,128)(2,1)S(1)}, bf16[2,16,1792]{2,1,0:T(8,128)(2,1)S(1)}, u32[]{:S(2)}, u32[]{:S(2)}) collective-permute-start(bf16[2,16,1792]{2,1,0:T(8,128)(2,1)S(1)} %collective-permute-done.11), channel_id=1, source_target_pairs={{0,4},{1,3},{2,6},{3,1},{4,0},{5,7},{6,2},{7,5},{8,12},{9,11},{10,... | collective-permute-start | bytes 344072 | tf_op jit(solution)/shard_map/ppermute | solution.py:225
  52.5 3.7 %collective-permute-done.15 = bf16[2,16,1792]{2,1,0:T(8,128)(2,1)S(1)} collective-permute-done((bf16[2,16,1792]{2,1,0:T(8,128)(2,1)S(1)}, bf16[2,16,1792]{2,1,0:T(8,128)(2,1)S(1)}, u32[]{:S(2)}, u32[]{:S(2)}) %collective-permute-start.15) | collective-permute-done | bytes 114720 | tf_op jit(solution)/shard_map/ppermute | solution.py:225
  56.2 0.2 collective-permute-start.19
  56.4 0.1 collective-permute-done.13
  56.6 1.3 %collective-permute-start.16 = (bf16[2,32,1792]{2,1,0:T(8,128)(2,1)S(1)}, bf16[2,32,1792]{2,1,0:T(8,128)(2,1)S(1)}, u32[]{:S(2)}, u32[]{:S(2)}) collective-permute-start(bf16[2,32,1792]{2,1,0:T(8,128)(2,1)S(1)} %constant_dynamic-update-slice_fusion), channel_id=1, source_target_pairs={{0,2},{1,5},{2,0},{3,7},{4,6},{5,1},{6,4},{7,3},{8,10},{9,13},{10,... | collective-permute-start | bytes 688136 | tf_op jit(solution)/shard_map/ppermute | solution.py:225
  57.9 3.1 %collective-permute-done.19 = bf16[2,16,1792]{2,1,0:T(8,128)(2,1)S(1)} collective-permute-done((bf16[2,16,1792]{2,1,0:T(8,128)(2,1)S(1)}, bf16[2,16,1792]{2,1,0:T(8,128)(2,1)S(1)}, u32[]{:S(2)}, u32[]{:S(2)}) %collective-permute-start.19) | collective-permute-done | bytes 114720 | tf_op jit(solution)/shard_map/ppermute | solution.py:225
  61.0 0.4 collective-permute-start.20
  61.4 0.2 collective-permute-start.17
  61.6 1.8 %collective-permute-start.21 = (bf16[2,16,1792]{2,1,0:T(8,128)(2,1)S(1)}, bf16[2,16,1792]{2,1,0:T(8,128)(2,1)S(1)}, u32[]{:S(2)}, u32[]{:S(2)}) collective-permute-start(bf16[2,16,1792]{2,1,0:T(8,128)(2,1)S(1)} %collective-permute-done.19), channel_id=1, source_target_pairs={{0,4},{1,3},{2,6},{3,1},{4,0},{5,7},{6,2},{7,5},{8,12},{9,11},{10,... | collective-permute-start | bytes 344072 | tf_op jit(solution)/shard_map/ppermute | solution.py:225
  63.4 3.6 %collective-permute-done.20 = bf16[2,16,1792]{2,1,0:T(8,128)(2,1)S(1)} collective-permute-done((bf16[2,16,1792]{2,1,0:T(8,128)(2,1)S(1)}, bf16[2,16,1792]{2,1,0:T(8,128)(2,1)S(1)}, u32[]{:S(2)}, u32[]{:S(2)}) %collective-permute-start.20) | collective-permute-done | bytes 114720 | tf_op jit(solution)/shard_map/ppermute | solution.py:225
  67.0 0.5 collective-permute-start.22
  67.5 1.5 %collective-permute-start.18 = (bf16[2,32,1792]{2,1,0:T(8,128)(2,1)S(1)}, bf16[2,32,1792]{2,1,0:T(8,128)(2,1)S(1)}, u32[]{:S(2)}, u32[]{:S(2)}) collective-permute-start(bf16[2,32,1792]{2,1,0:T(8,128)(2,1)S(1)} %collective-permute-done.16), channel_id=1, source_target_pairs={{0,4},{1,3},{2,6},{3,1},{4,0},{5,7},{6,2},{7,5},{8,12},{9,11},{10,... | collective-permute-start | bytes 688136 | tf_op jit(solution)/shard_map/ppermute | solution.py:225
  69.1 5.2 %collective-permute-done.18 = bf16[2,32,1792]{2,1,0:T(8,128)(2,1)S(1)} collective-permute-done((bf16[2,32,1792]{2,1,0:T(8,128)(2,1)S(1)}, bf16[2,32,1792]{2,1,0:T(8,128)(2,1)S(1)}, u32[]{:S(2)}, u32[]{:S(2)}) %collective-permute-start.18) | collective-permute-done | bytes 229408 | tf_op jit(solution)/shard_map/ppermute | solution.py:225
  74.4 0.1 collective-permute-start.24
  74.7 0.6 collective-permute-start.25
  75.3 2.6 %shard_map.117.hidden_grad = f32[256,1184]{1,0:T(8,128)S(1)} custom-call(bf16[2,256,1792]{2,1,0:T(8,128)(2,1)S(1)} %get-tuple-element.62.grads, bf16[1184,1792]{1,0:T(8,128)(2,1)S(1)} %bitcast.26, bf16[1184,1792]{1,0:T(8,128)(2,1)S(1)} %shard_map.111.ready.refs_1_), custom_call_target="tpu_custom_call" | custom-call | flops 2172649472 | bytes 8486912 | tf_op jit(solution)/shard_map/pallas_call | solution.py:361
  77.8 0.0 copy-start.3
  77.8 0.1 slice_bitcast_fusion.refs_2_
  77.9 0.1 pad_maximum_fusion.refs_3_
  78.0 0.9 %copy-done.3 = bf16[16,16,1184]{2,1,0:T(8,128)(2,1)S(1)} copy-done((bf16[16,16,1184]{2,1,0:T(8,128)(2,1)S(1)}, bf16[16,16,1184]{2,1,0:T(8,128)(2,1)}, u32[]{:S(2)}) %copy-start.3) | copy-done | bytes 606232
  78.9 5.1 %shard_map.118 = (f32[1184,1792]{1,0:T(8,128)}, bf16[16,16,1184]{2,1,0:T(8,128)(2,1)}, bf16[16,16,1184]{2,1,0:T(8,128)(2,1)}) custom-call(s32[16]{0:T(128)S(1)} %xor.10.order, f32[256,1184]{1,0:T(8,128)S(1)} %shard_map.117.hidden_grad, bf16[16,16,1184]{2,1,0:T(8,128)(2,1)S(1)} %copy-done.1, bf16[16,16,1184]{2,1,0:T(8,128)(2,1)S(1)} %copy-done.3, ...), custom_call_target="tpu_custom_call" | custom-call | flops 2172649472 | bytes 10911744 | tf_op jit(solution)/shard_map/pallas_call | solution.py:373
  (60 shorter events, 0.5 us)
Async XLA Ops:
  0.6 26.3 %copy-start = (bf16[1,128,3584]{2,1,0:T(8,128)(2,1)S(1)}, bf16[1,128,3584]{2,1,0:T(8,128)(2,1)}, u32[]{:S(2)}) copy-start(bf16[1,128,3584]{2,1,0:T(8,128)(2,1)} %param.10) | copy-start | bytes 2752516
  0.6 19.8 %copy-start.1 = (bf16[16,16,1184]{2,1,0:T(8,128)(2,1)S(1)}, bf16[16,16,1184]{2,1,0:T(8,128)(2,1)}, u32[]{:S(2)}) copy-start(bf16[16,16,1184]{2,1,0:T(8,128)(2,1)} %gate.3) | copy-start | bytes 1818628
  0.7 35.5 %collective-permute-start = (bf16[1792,1184]{0,1:T(8,128)(2,1)}, bf16[1792,1184]{0,1:T(8,128)(2,1)}, u32[]{:S(2)}, u32[]{:S(2)}) collective-permute-start(bf16[1792,1184]{0,1:T(8,128)(2,1)} %param.15), channel_id=1, source_target_pairs={{0,1},{1,0},{2,3},{3,2},{4,5},{5,4},{6,7},{7,6},{8,9},{9,8},{10,11... | collective-permute-start | bytes 12730376 | tf_op jit(solution)/shard_map/ppermute | solution.py:231
  1.2 15.2 %collective-permute-start.1 = (bf16[128,3584]{1,0:T(8,128)(2,1)}, bf16[128,3584]{1,0:T(8,128)(2,1)S(1)}, u32[]{:S(2)}, u32[]{:S(2)}) collective-permute-start(bf16[128,3584]{1,0:T(8,128)(2,1)} %bitcast.27), channel_id=1, source_target_pairs={{0,2},{1,5},{2,0},{3,7},{4,6},{5,1},{6,4},{7,3},{8,10},{9,13},{10,... | collective-permute-start | bytes 2752520 | tf_op jit(solution)/shard_map/ppermute | solution.py:225
  3.7 0.9 %copy-start.6 = (bf16[1,16,3584]{2,1,0:T(8,128)(2,1)S(1)}, bf16[1,16,3584]{2,1,0:T(8,128)(2,1)}, u32[]{:S(2)}) copy-start(bf16[1,16,3584]{2,1,0:T(8,128)(2,1)} %param.8) | copy-start | bytes 344068
  4.6 0.7 copy-start.10
  5.4 0.7 copy-start.12
  6.0 0.7 copy-start.13
  7.0 8.8 %collective-permute-start.2 = (bf16[16,3712]{1,0:T(8,128)(2,1)S(1)}, bf16[16,3712]{1,0:T(8,128)(2,1)S(1)}, u32[]{:S(2)}, u32[]{:S(2)}) collective-permute-start(bf16[16,3712]{1,0:T(8,128)(2,1)S(1)} %shard_map.112.refs_0_), channel_id=1, source_target_pairs={{0,16},{1,17},{2,18},{3,19},{4,20},{5,21},{6,22},{7,23},{8,24},{9,... | collective-permute-start | bytes 356360 | tf_op jit(solution)/shard_map/ppermute | solution.py:225
  15.8 0.6 copy-start.8
  16.4 10.5 %collective-permute-start.7 = (bf16[128,3584]{1,0:T(8,128)(2,1)S(1)}, bf16[128,3584]{1,0:T(8,128)(2,1)S(1)}, u32[]{:S(2)}, u32[]{:S(2)}) collective-permute-start(bf16[128,3584]{1,0:T(8,128)(2,1)S(1)} %collective-permute-done.1.near), channel_id=1, source_target_pairs={{0,1},{1,0},{2,3},{3,2},{4,5},{5,4},{6,7},{7,6},{8,9},{9,8},{10,11... | collective-permute-start | bytes 2752520 | tf_op jit(solution)/shard_map/ppermute | solution.py:228
  17.2 9.6 %collective-permute-start.3 = (bf16[64,3584]{1,0:T(8,128)(2,1)}, bf16[64,3584]{1,0:T(8,128)(2,1)}, u32[]{:S(2)}, u32[]{:S(2)}) collective-permute-start(bf16[64,3584]{1,0:T(8,128)(2,1)} %slice_select_fusion), channel_id=1, source_target_pairs={{0,4},{1,3},{2,6},{3,1},{4,0},{5,7},{6,2},{7,5},{8,12},{9,11},{10,... | collective-permute-start | bytes 1376264 | tf_op jit(solution)/shard_map/ppermute | solution.py:225
  18.2 6.2 %collective-permute-start.4 = (bf16[16,3712]{1,0:T(8,128)(2,1)S(1)}, bf16[16,3712]{1,0:T(8,128)(2,1)}, u32[]{:S(2)}, u32[]{:S(2)}) collective-permute-start(bf16[16,3712]{1,0:T(8,128)(2,1)S(1)} %shard_map.112.refs_0_), channel_id=1, source_target_pairs={{0,8},{1,9},{2,10},{3,11},{4,12},{5,13},{6,14},{7,15},{8,0},{9,1},... | collective-permute-start | bytes 356360 | tf_op jit(solution)/shard_map/ppermute | solution.py:225
  19.8 6.3 %collective-permute-start.5 = (bf16[16,3712]{1,0:T(8,128)(2,1)}, bf16[16,3712]{1,0:T(8,128)(2,1)}, u32[]{:S(2)}, u32[]{:S(2)}) collective-permute-start(bf16[16,3712]{1,0:T(8,128)(2,1)} %copy-done.8), channel_id=1, source_target_pairs={{0,8},{1,9},{2,10},{3,11},{4,12},{5,13},{6,14},{7,15},{8,0},{9,1},... | collective-permute-start | bytes 356360 | tf_op jit(solution)/shard_map/ppermute | solution.py:225
  20.5 1.1 %copy-start.2 = (bf16[16,16,1184]{2,1,0:T(8,128)(2,1)S(1)}, bf16[16,16,1184]{2,1,0:T(8,128)(2,1)}, u32[]{:S(2)}) copy-start(bf16[16,16,1184]{2,1,0:T(8,128)(2,1)} %up.3) | copy-start | bytes 1818628
  21.5 5.4 %copy-start.9 = (bf16[16,3712]{1,0:T(8,128)(2,1)S(1)}, bf16[16,3712]{1,0:T(8,128)(2,1)}, u32[]{:S(2)}) copy-start(bf16[16,3712]{1,0:T(8,128)(2,1)} %copy-done.8) | copy-start | bytes 356356
  22.5 7.4 %copy-start.4 = (bf16[1184,256]{1,0:T(8,128)(2,1)}, bf16[1184,256]{1,0:T(8,128)(2,1)S(1)}, u32[]{:S(2)}) copy-start(bf16[1184,256]{1,0:T(8,128)(2,1)S(1)} %shard_map.113.refs_0_) | copy-start | bytes 1818628
  26.9 3.0 %collective-permute-start.6 = (bf16[64,3584]{1,0:T(8,128)(2,1)}, bf16[64,3584]{1,0:T(8,128)(2,1)S(1)}, u32[]{:S(2)}, u32[]{:S(2)}) collective-permute-start(bf16[64,3584]{1,0:T(8,128)(2,1)} %collective-permute-done.3.far), channel_id=1, source_target_pairs={{0,1},{1,0},{2,3},{3,2},{4,5},{5,4},{6,7},{7,6},{8,9},{9,8},{10,11... | collective-permute-start | bytes 1376264 | tf_op jit(solution)/shard_map/ppermute | solution.py:228
  31.7 6.9 %collective-permute-start.8 = (bf16[16,3584]{1,0:T(8,128)(2,1)S(1)}, bf16[16,3584]{1,0:T(8,128)(2,1)S(1)}, u32[]{:S(2)}, u32[]{:S(2)}) collective-permute-start(bf16[16,3584]{1,0:T(8,128)(2,1)S(1)} %get-tuple-element.32), channel_id=1, source_target_pairs={{0,8},{1,9},{2,10},{3,11},{4,12},{5,13},{6,14},{7,15},{8,0},{9,1},... | collective-permute-start | bytes 344072 | tf_op jit(solution)/shard_map/ppermute | solution.py:225
  33.3 11.8 %collective-permute-start.9 = (bf16[16,3584]{1,0:T(8,128)(2,1)S(1)}, bf16[16,3584]{1,0:T(8,128)(2,1)S(1)}, u32[]{:S(2)}, u32[]{:S(2)}) collective-permute-start(bf16[16,3584]{1,0:T(8,128)(2,1)S(1)} %get-tuple-element.33), channel_id=1, source_target_pairs={{0,16},{1,17},{2,18},{3,19},{4,20},{5,21},{6,22},{7,23},{8,24},{9,... | collective-permute-start | bytes 344072 | tf_op jit(solution)/shard_map/ppermute | solution.py:225
  36.2 8.9 %collective-permute-start.10 = (bf16[16,3584]{1,0:T(8,128)(2,1)S(1)}, bf16[16,3584]{1,0:T(8,128)(2,1)S(1)}, u32[]{:S(2)}, u32[]{:S(2)}) collective-permute-start(bf16[16,3584]{1,0:T(8,128)(2,1)S(1)} %get-tuple-element.34), channel_id=1, source_target_pairs={{0,24},{1,25},{2,26},{3,27},{4,28},{5,29},{6,30},{7,31},{8,16},{9,... | collective-permute-start | bytes 344072 | tf_op jit(solution)/shard_map/ppermute | solution.py:225
  36.2 8.9 %copy-start.7 = (bf16[1,16,3584]{2,1,0:T(8,128)(2,1)S(1)}, bf16[1,16,3584]{2,1,0:T(8,128)(2,1)}, u32[]{:S(2)}) copy-start(bf16[1,16,3584]{2,1,0:T(8,128)(2,1)} %param.8) | copy-start | bytes 344068
  36.2 8.9 %copy-start.11 = (f32[3584]{0:T(1024)S(1)}, f32[3584]{0:T(1024)}, u32[]{:S(2)}) copy-start(f32[3584]{0:T(1024)} %gain.3) | copy-start | bytes 43012
  36.2 39.0 %slice-start = ((s8[4243456]{0:T(1024)(128)(4,1)}), s8[4194304]{0:T(1024)(128)(4,1)S(1)}, s32[]{:S(2)}) async-start(s8[4243456]{0:T(1024)(128)(4,1)} %bitcast.24), calls=%async_computation | async-start | bytes 8388608
  45.1 30.1 %slice-start.1 = ((s8[4243456]{0:T(1024)(128)(4,1)}), s8[49152]{0:T(1024)(128)(4,1)S(1)}, s32[]{:S(2)}) async-start(s8[4243456]{0:T(1024)(128)(4,1)} %bitcast.24), calls=%async_computation.1 | async-start | bytes 98304
  46.0 15.3 %copy-start.5 = (bf16[1184,256]{1,0:T(8,128)(2,1)S(1)}, bf16[1184,256]{1,0:T(8,128)(2,1)}, u32[]{:S(2)}) copy-start(bf16[1184,256]{1,0:T(8,128)(2,1)} %copy-done.4) | copy-start | bytes 1818628
  46.1 5.5 %collective-permute-start.11 = (bf16[2,16,1792]{2,1,0:T(8,128)(2,1)S(1)}, bf16[2,16,1792]{2,1,0:T(8,128)(2,1)S(1)}, u32[]{:S(2)}, u32[]{:S(2)}) collective-permute-start(bf16[2,16,1792]{2,1,0:T(8,128)(2,1)S(1)} %get-tuple-element.60), channel_id=1, source_target_pairs={{0,2},{1,5},{2,0},{3,7},{4,6},{5,1},{6,4},{7,3},{8,10},{9,13},{10,... | collective-permute-start | bytes 344072 | tf_op jit(solution)/shard_map/ppermute | solution.py:225
  46.8 9.4 %collective-permute-start.15 = (bf16[2,16,1792]{2,1,0:T(8,128)(2,1)S(1)}, bf16[2,16,1792]{2,1,0:T(8,128)(2,1)S(1)}, u32[]{:S(2)}, u32[]{:S(2)}) collective-permute-start(bf16[2,16,1792]{2,1,0:T(8,128)(2,1)S(1)} %get-tuple-element.60), channel_id=1, source_target_pairs={{0,16},{1,17},{2,18},{3,19},{4,20},{5,21},{6,22},{7,23},{8,24},{9,... | collective-permute-start | bytes 344072 | tf_op jit(solution)/shard_map/ppermute | solution.py:225
  50.5 6.0 %collective-permute-start.14 = (bf16[2,16,1792]{2,1,0:T(8,128)(2,1)S(1)}, bf16[2,16,1792]{2,1,0:T(8,128)(2,1)S(1)}, u32[]{:S(2)}, u32[]{:S(2)}) collective-permute-start(bf16[2,16,1792]{2,1,0:T(8,128)(2,1)S(1)} %get-tuple-element.60), channel_id=1, source_target_pairs={{0,8},{1,9},{2,10},{3,11},{4,12},{5,13},{6,14},{7,15},{8,0},{9,1},... | collective-permute-start | bytes 344072 | tf_op jit(solution)/shard_map/ppermute | solution.py:225
  50.5 5.9 %collective-permute-start.12 = (bf16[2,16,1792]{2,1,0:T(8,128)(2,1)S(1)}, bf16[2,16,1792]{2,1,0:T(8,128)(2,1)S(1)}, u32[]{:S(2)}, u32[]{:S(2)}) collective-permute-start(bf16[2,16,1792]{2,1,0:T(8,128)(2,1)S(1)} %get-tuple-element.60), channel_id=1, source_target_pairs={{0,4},{1,3},{2,6},{3,1},{4,0},{5,7},{6,2},{7,5},{8,12},{9,11},{10,... | collective-permute-start | bytes 344072 | tf_op jit(solution)/shard_map/ppermute | solution.py:225
  51.6 4.9 %collective-permute-start.13 = (bf16[2,16,1792]{2,1,0:T(8,128)(2,1)S(1)}, bf16[2,16,1792]{2,1,0:T(8,128)(2,1)S(1)}, u32[]{:S(2)}, u32[]{:S(2)}) collective-permute-start(bf16[2,16,1792]{2,1,0:T(8,128)(2,1)S(1)} %collective-permute-done.11), channel_id=1, source_target_pairs={{0,4},{1,3},{2,6},{3,1},{4,0},{5,7},{6,2},{7,5},{8,12},{9,11},{10,... | collective-permute-start | bytes 344072 | tf_op jit(solution)/shard_map/ppermute | solution.py:225
  56.2 4.8 %collective-permute-start.19 = (bf16[2,16,1792]{2,1,0:T(8,128)(2,1)S(1)}, bf16[2,16,1792]{2,1,0:T(8,128)(2,1)S(1)}, u32[]{:S(2)}, u32[]{:S(2)}) collective-permute-start(bf16[2,16,1792]{2,1,0:T(8,128)(2,1)S(1)} %collective-permute-done.15), channel_id=1, source_target_pairs={{0,8},{1,9},{2,10},{3,11},{4,12},{5,13},{6,14},{7,15},{8,0},{9,1},... | collective-permute-start | bytes 344072 | tf_op jit(solution)/shard_map/ppermute | solution.py:225
  56.6 10.9 %collective-permute-start.16 = (bf16[2,32,1792]{2,1,0:T(8,128)(2,1)S(1)}, bf16[2,32,1792]{2,1,0:T(8,128)(2,1)S(1)}, u32[]{:S(2)}, u32[]{:S(2)}) collective-permute-start(bf16[2,32,1792]{2,1,0:T(8,128)(2,1)S(1)} %constant_dynamic-update-slice_fusion), channel_id=1, source_target_pairs={{0,2},{1,5},{2,0},{3,7},{4,6},{5,1},{6,4},{7,3},{8,10},{9,13},{10,... | collective-permute-start | bytes 688136 | tf_op jit(solution)/shard_map/ppermute | solution.py:225
  61.0 6.0 %collective-permute-start.20 = (bf16[2,16,1792]{2,1,0:T(8,128)(2,1)S(1)}, bf16[2,16,1792]{2,1,0:T(8,128)(2,1)S(1)}, u32[]{:S(2)}, u32[]{:S(2)}) collective-permute-start(bf16[2,16,1792]{2,1,0:T(8,128)(2,1)S(1)} %collective-permute-done.19), channel_id=1, source_target_pairs={{0,2},{1,5},{2,0},{3,7},{4,6},{5,1},{6,4},{7,3},{8,10},{9,13},{10,... | collective-permute-start | bytes 344072 | tf_op jit(solution)/shard_map/ppermute | solution.py:225
  61.4 16.6 %collective-permute-start.23 = (bf16[1184,256]{1,0:T(8,128)(2,1)S(1)}, bf16[1184,256]{1,0:T(8,128)(2,1)S(1)}, u32[]{:S(2)}, u32[]{:S(2)}) collective-permute-start(bf16[1184,256]{1,0:T(8,128)(2,1)S(1)} %copy-done.5), channel_id=1, source_target_pairs={{0,1},{1,0},{2,3},{3,2},{4,5},{5,4},{6,7},{7,6},{8,9},{9,8},{10,11... | collective-permute-start | bytes 1818632 | tf_op jit(solution)/shard_map/ppermute | solution.py:231
  61.4 7.7 %collective-permute-start.17 = (bf16[2,32,1792]{2,1,0:T(8,128)(2,1)S(1)}, bf16[2,32,1792]{2,1,0:T(8,128)(2,1)S(1)}, u32[]{:S(2)}, u32[]{:S(2)}) collective-permute-start(bf16[2,32,1792]{2,1,0:T(8,128)(2,1)S(1)} %constant_dynamic-update-slice_fusion), channel_id=1, source_target_pairs={{0,4},{1,3},{2,6},{3,1},{4,0},{5,7},{6,2},{7,5},{8,12},{9,11},{10,... | collective-permute-start | bytes 688136 | tf_op jit(solution)/shard_map/ppermute | solution.py:225
  61.6 13.0 %collective-permute-start.21 = (bf16[2,16,1792]{2,1,0:T(8,128)(2,1)S(1)}, bf16[2,16,1792]{2,1,0:T(8,128)(2,1)S(1)}, u32[]{:S(2)}, u32[]{:S(2)}) collective-permute-start(bf16[2,16,1792]{2,1,0:T(8,128)(2,1)S(1)} %collective-permute-done.19), channel_id=1, source_target_pairs={{0,4},{1,3},{2,6},{3,1},{4,0},{5,7},{6,2},{7,5},{8,12},{9,11},{10,... | collective-permute-start | bytes 344072 | tf_op jit(solution)/shard_map/ppermute | solution.py:225
  67.0 7.6 %collective-permute-start.22 = (bf16[2,16,1792]{2,1,0:T(8,128)(2,1)S(1)}, bf16[2,16,1792]{2,1,0:T(8,128)(2,1)S(1)}, u32[]{:S(2)}, u32[]{:S(2)}) collective-permute-start(bf16[2,16,1792]{2,1,0:T(8,128)(2,1)S(1)} %collective-permute-done.20), channel_id=1, source_target_pairs={{0,4},{1,3},{2,6},{3,1},{4,0},{5,7},{6,2},{7,5},{8,12},{9,11},{10,... | collective-permute-start | bytes 344072 | tf_op jit(solution)/shard_map/ppermute | solution.py:225
  67.5 6.8 %collective-permute-start.18 = (bf16[2,32,1792]{2,1,0:T(8,128)(2,1)S(1)}, bf16[2,32,1792]{2,1,0:T(8,128)(2,1)S(1)}, u32[]{:S(2)}, u32[]{:S(2)}) collective-permute-start(bf16[2,32,1792]{2,1,0:T(8,128)(2,1)S(1)} %collective-permute-done.16), channel_id=1, source_target_pairs={{0,4},{1,3},{2,6},{3,1},{4,0},{5,7},{6,2},{7,5},{8,12},{9,11},{10,... | collective-permute-start | bytes 688136 | tf_op jit(solution)/shard_map/ppermute | solution.py:225
  74.4 3.5 %collective-permute-start.24 = (bf16[128,1792]{1,0:T(8,128)(2,1)S(1)}, bf16[128,1792]{1,0:T(8,128)(2,1)S(1)}, u32[]{:S(2)}, u32[]{:S(2)}) collective-permute-start(bf16[128,1792]{1,0:T(8,128)(2,1)S(1)} %slice_bitcast_fusion.2), channel_id=1, source_target_pairs={{0,1},{1,0},{2,3},{3,2},{4,5},{5,4},{6,7},{7,6},{8,9},{9,8},{10,11... | collective-permute-start | bytes 1376264 | tf_op jit(solution)/shard_map/ppermute | solution.py:231
  74.7 3.2 %collective-permute-start.25 = (bf16[128,1792]{1,0:T(8,128)(2,1)S(1)}, bf16[128,1792]{1,0:T(8,128)(2,1)S(1)}, u32[]{:S(2)}, u32[]{:S(2)}) collective-permute-start(bf16[128,1792]{1,0:T(8,128)(2,1)S(1)} %slice_bitcast_fusion.1), channel_id=1, source_target_pairs={{0,1},{1,0},{2,3},{3,2},{4,5},{5,4},{6,7},{7,6},{8,9},{9,8},{10,11... | collective-permute-start | bytes 1376264 | tf_op jit(solution)/shard_map/ppermute | solution.py:231
  77.8 1.1 %copy-start.3 = (bf16[16,16,1184]{2,1,0:T(8,128)(2,1)S(1)}, bf16[16,16,1184]{2,1,0:T(8,128)(2,1)}, u32[]{:S(2)}) copy-start(bf16[16,16,1184]{2,1,0:T(8,128)(2,1)} %up.3) | copy-start | bytes 1818628
